TPU v7x, 32 devices: a whole 2x2x4 slice. The times are simulated.
32 devices in a mesh: leaf: 8 (over y, x, core), blk: 4 (over z).
Axes of the slice: x: 2, y: 2, z: 4, core: 2. Of those that a mesh axis runs over, the one named last changes fastest.
Arguments:
- interface: bfloat16 [32768, 512], P(('leaf', 'blk')), may hold values from -6 to 6
- owners: int32 [32768, 1], P(('leaf', 'blk')), may hold values from 0 to 7; in each aligned block of 1024 rows (0 to 1023, 1024 to 2047, ...) at most 256 rows name the same one
- keep_proj: bfloat16 [3, 512, 512], replicated, may hold values from -0.25 to 0.25
- sibling_proj: bfloat16 [3, 512, 512], replicated, may hold values from -0.25 to 0.25
- coupling: bfloat16 [8, 512, 512], P('leaf'), may hold values from -0.25 to 0.25
- pattern: int32 [8, 8, 8], P('leaf'), may hold values 0 or 1
Outputs:
- coupled: bfloat16 [32768, 512], P(('leaf', 'blk'))
Inputs may be any that keep to these rules, and one draw needn't show every extreme that they name: `owners`: among the 1024 rows of one device no owner is named by more than 256 rows, a bound that some block reaches.
All inputs are finite; a program needn't handle non-finite values. No bound on the sum of `pattern` on one device may be relied on, other than what follows from the above.
Results may differ from a plain program's by a relative error of at most 0.0075.
Values may be sent and summed in bfloat16 or wider, within the bound.
No kernel may reach another device: no remote copies, remote signals or barrier semaphores. Data moves between devices by JAX's collectives and lax.ppermute only.
A program may use at most 64 MiB of HBM per device.

v0:
```python
import jax
import jax.numpy as jnp
from jax import lax
from jax.sharding import PartitionSpec as P

BS = 64
LEVELS = 3


epsilon = 1e-06


def swapped(value, axis, bit):
    mask = 2**bit
    pairs = [(source, source ^ mask) for source in range(lax.axis_size(axis))]
    return lax.ppermute(value, axis, pairs)


def local(interface, owners, keep_proj, sibling_proj, coupling, pattern):
    row_count, features = interface.shape
    current = interface
    for tree_level in range(LEVELS):
        sibling = swapped(current, "leaf", tree_level)
        combined = jnp.dot(current, keep_proj[tree_level], preferred_element_type=jnp.float32)
        combined = combined + jnp.dot(
            sibling, sibling_proj[tree_level], preferred_element_type=jnp.float32
        )
        scale_rows = lax.rsqrt(jnp.mean(combined * combined, axis=1, keepdims=True) + epsilon)
        current = (combined * scale_rows).astype(jnp.bfloat16)
    leaves = lax.axis_size("leaf")
    capacity = 2 * row_count // leaves
    target = owners[:, 0]
    onehot = (target[:, None] == jnp.arange(leaves, dtype=jnp.int32)[None, :]).astype(jnp.int32)
    slot_index = jnp.sum(jnp.cumsum(onehot, axis=0) * onehot, axis=1) - 1
    position = target * capacity + slot_index
    outgoing = jnp.zeros((leaves * capacity, features), jnp.bfloat16).at[position].set(current)
    expanded = jnp.repeat(jnp.repeat(pattern[0], BS, axis=0), BS, axis=1)
    masked = coupling[0] * expanded.astype(jnp.bfloat16)
    sectioned = outgoing.reshape(leaves, capacity, features)
    product = jnp.einsum(
        "...m,mn->...n",
        lax.all_to_all(sectioned, "leaf", split_axis=0, concat_axis=0, tiled=True),
        masked,
        preferred_element_type=jnp.float32,
    )
    result = product.astype(jnp.bfloat16)
    returned = lax.all_to_all(result, "leaf", split_axis=0, concat_axis=0, tiled=True)
    returned = returned.reshape(leaves * capacity, features)
    return returned[position]


def solution(mesh):
    in_specs = (
        P(("leaf", "blk"), None),
        P(("leaf", "blk"), None),
        P(),
        P(),
        P("leaf", None, None),
        P("leaf", None, None),
    )
    out_specs = P(("leaf", "blk"), None)
    return jax.shard_map(local, mesh=mesh, in_specs=in_specs, out_specs=out_specs, check_vma=False)
```

profile of v0, /device:TPU:0, one launch (start us, length us, event | category | flops | bytes accessed | tf_op | source)
XLA Modules:
  0.0 135.3 jit_solution(388243998630380705)
XLA Ops:
  0.0 0.5 collective-permute-start
  0.5 2.1 %fusion.10 = f32[1024,512]{0,1:T(8,128)S(1)} fusion(bf16[1024,512]{1,0:T(8,128)(2,1)} %param.6, bf16[3,512,512]{2,1,0:T(8,128)(2,1)} %param.8), kind=kOutput, calls=%fused_computation.23 | convolution fusion | flops 536870912 | bytes 3670016 | tf_op jit(solution)/shard_map/dot_general | solution.py:24
  2.6 0.4 collective-permute-done
  3.0 1.8 %multiply_reduce_fusion.2 = (f32[1024]{0:T(1024)S(1)}, f32[1024,512]{0,1:T(8,128)S(1)}) fusion(f32[1024,512]{0,1:T(8,128)S(1)} %fusion.10, bf16[1024,512]{1,0:T(8,128)(2,1)S(1)} %collective-permute-done, bf16[3,512,512]{2,1,0:T(8,128)(2,1)} %param.9), kind=kOutput, calls=%fused_computation.7 | convolution fusion | flops 538442752 | bytes 5771264 | tf_op jit(solution)/shard_map/dot_general | solution.py:25
  4.8 0.3 multiply_convert_fusion.2
  5.1 2.9 %collective-permute-start.1 = (bf16[1024,512]{0,1:T(8,128)(2,1)S(1)}, bf16[1024,512]{0,1:T(8,128)(2,1)}, u32[]{:S(2)}, u32[]{:S(2)}) collective-permute-start(bf16[1024,512]{0,1:T(8,128)(2,1)S(1)} %multiply_convert_fusion.2), channel_id=1, source_target_pairs={{0,8},{4,12},{8,0},{12,4},{16,24},{20,28},{24,16},{28,20},{1,9},{5... | collective-permute-start | bytes 3145736 | tf_op jit(solution)/shard_map/ppermute | solution.py:16
  8.0 2.3 %reduce-window.6 = s32[8,8,128]{2,1,0:T(8,128)S(1)} reduce-window(s32[8,8,128]{2,1,0:T(8,128)S(1)} %fusion.20, s32[]{:T(128)} %constant.7.clone.1), window={size=1x1x128 pad=0_0x0_0x127_0}, to_apply=%region_0.0 | reduce-window | flops 1040384 | bytes 65540 | tf_op jit(solution)/shard_map/reduce-window
  10.3 0.3 slice_reduce_fusion
  10.7 0.8 fusion.7
  11.5 20.1 %collective-permute-done.1 = bf16[1024,512]{0,1:T(8,128)(2,1)} collective-permute-done((bf16[1024,512]{0,1:T(8,128)(2,1)S(1)}, bf16[1024,512]{0,1:T(8,128)(2,1)}, u32[]{:S(2)}, u32[]{:S(2)}) %collective-permute-start.1) | collective-permute-done | bytes 1048608 | tf_op jit(solution)/shard_map/ppermute | solution.py:16
  31.6 2.0 %multiply_reduce_fusion.1 = (f32[1024]{0:T(1024)S(1)}, f32[1024,512]{0,1:T(8,128)S(1)}) fusion(f32[1024,512]{0,1:T(8,128)S(1)} %fusion.7, bf16[1024,512]{0,1:T(8,128)(2,1)} %collective-permute-done.1, bf16[3,512,512]{2,1,0:T(8,128)(2,1)S(1)} %copy-done.1), kind=kOutput, calls=%fused_computation.5 | convolution fusion | flops 538442752 | bytes 5771264 | tf_op jit(solution)/shard_map/dot_general | solution.py:25
  33.6 0.3 multiply_convert_fusion.1
  33.9 1.8 %collective-permute-start.2 = (bf16[1024,512]{0,1:T(8,128)(2,1)S(1)}, bf16[1024,512]{0,1:T(8,128)(2,1)S(1)}, u32[]{:S(2)}, u32[]{:S(2)}) collective-permute-start(bf16[1024,512]{0,1:T(8,128)(2,1)S(1)} %multiply_convert_fusion.1), channel_id=1, source_target_pairs={{0,16},{4,20},{8,24},{12,28},{16,0},{20,4},{24,8},{28,12},{1,17},{... | collective-permute-start | bytes 3145736 | tf_op jit(solution)/shard_map/ppermute | solution.py:16
  35.8 0.8 fusion.4
  36.6 22.0 %collective-permute-done.2 = bf16[1024,512]{0,1:T(8,128)(2,1)S(1)} collective-permute-done((bf16[1024,512]{0,1:T(8,128)(2,1)S(1)}, bf16[1024,512]{0,1:T(8,128)(2,1)S(1)}, u32[]{:S(2)}, u32[]{:S(2)}) %collective-permute-start.2) | collective-permute-done | bytes 1048608 | tf_op jit(solution)/shard_map/ppermute | solution.py:16
  58.6 0.8 multiply_reduce_fusion
  59.7 0.5 copy.7
  60.3 6.7 %scatter_custom_fusion = bf16[2048,512]{1,0:T(8,128)(2,1)} fusion(s32[1024]{0:T(1024)S(1)} %bitcast.66, bf16[1024,512]{1,0:T(8,128)(2,1)S(1)} %copy.7, bf16[]{:T(256)} %constant.8.clone.1), kind=kCustom, calls=%fused_computation.12 | custom fusion | bytes 2097154 | tf_op jit(solution)/shard_map/scatter | solution.py:36
  67.0 3.8 %all-to-all-start = ((bf16[8,256,512]{2,1,0:T(8,128)(2,1)}), bf16[8,256,512]{2,1,0:T(8,128)(2,1)S(1)}, u32[]{:S(2)}, u32[]{:S(2)}) async-start(bf16[8,256,512]{2,1,0:T(8,128)(2,1)} %bitcast.11), calls=%async_computation | async-start | bytes 4194304 | tf_op jit(solution)/shard_map/all_to_all | solution.py:42
  71.3 26.1 %all-to-all-done = bf16[8,256,512]{2,1,0:T(8,128)(2,1)S(1)} async-done(((bf16[8,256,512]{2,1,0:T(8,128)(2,1)}), bf16[8,256,512]{2,1,0:T(8,128)(2,1)S(1)}, u32[]{:S(2)}, u32[]{:S(2)}) %all-to-all-start) | async-done | bytes 2097184 | tf_op jit(solution)/shard_map/all_to_all | solution.py:42
  97.4 2.6 %convolution_convert_fusion = bf16[8,256,512]{2,1,0:T(8,128)(2,1)} fusion(bf16[8,256,512]{2,1,0:T(8,128)(2,1)S(1)} %all-to-all-done, bf16[512,512]{0,1:T(8,128)(2,1)S(1)} %bitcast_multiply_fusion), kind=kOutput, calls=%fused_computation.8 | convolution fusion | flops 1074790400 | bytes 4718592 | tf_op jit(solution)/shard_map/...m,mn->...n/dot_general | solution.py:40
  100.0 3.6 %all-to-all-start.1 = ((bf16[8,256,512]{2,1,0:T(8,128)(2,1)}), bf16[8,256,512]{2,1,0:T(8,128)(2,1)S(1)}, u32[]{:S(2)}, u32[]{:S(2)}) async-start(bf16[8,256,512]{2,1,0:T(8,128)(2,1)} %convolution_convert_fusion), calls=%async_computation.1 | async-start | bytes 4194304 | tf_op jit(solution)/shard_map/all_to_all | solution.py:47
  103.7 26.6 %all-to-all-done.1 = bf16[8,256,512]{2,1,0:T(8,128)(2,1)S(1)} async-done(((bf16[8,256,512]{2,1,0:T(8,128)(2,1)}), bf16[8,256,512]{2,1,0:T(8,128)(2,1)S(1)}, u32[]{:S(2)}, u32[]{:S(2)}) %all-to-all-start.1) | async-done | bytes 2097184 | tf_op jit(solution)/shard_map/all_to_all | solution.py:47
  130.2 5.1 %gather_fusion = bf16[1024,512]{1,0:T(8,128)(2,1)} fusion(bf16[2048,512]{1,0:T(8,128)(2,1)S(1)} %bitcast.63, s32[1024]{0:T(1024)S(1)} %broadcast_clamp_fusion), kind=kCustom, calls=%fused_computation | custom fusion | bytes 2101248 | tf_op jit(solution)/shard_map/gather | solution.py:49
  (27 shorter events, 1.1 us)
Async XLA Ops:
  0.0 3.0 %collective-permute-start = (bf16[1024,512]{1,0:T(8,128)(2,1)}, bf16[1024,512]{1,0:T(8,128)(2,1)S(1)}, u32[]{:S(2)}, u32[]{:S(2)}) collective-permute-start(bf16[1024,512]{1,0:T(8,128)(2,1)} %param.6), channel_id=1, source_target_pairs={{0,4},{4,0},{8,12},{12,8},{16,20},{20,16},{24,28},{28,24},{1,5},{5... | collective-permute-start | bytes 3145736 | tf_op jit(solution)/shard_map/ppermute | solution.py:16
  4.8 3.2 %copy-start.3 = (s32[1024,1]{0,1:T(1,128)S(1)}, s32[1024,1]{0,1:T(1,128)}, u32[]{:S(2)}) copy-start(s32[1024,1]{0,1:T(1,128)} %param.7) | copy-start | bytes 12292
  4.8 5.9 %copy-start = (bf16[3,512,512]{2,1,0:T(8,128)(2,1)S(1)}, bf16[3,512,512]{2,1,0:T(8,128)(2,1)}, u32[]{:S(2)}) copy-start(bf16[3,512,512]{2,1,0:T(8,128)(2,1)} %param.8) | copy-start | bytes 4718596
  5.1 26.5 %collective-permute-start.1 = (bf16[1024,512]{0,1:T(8,128)(2,1)S(1)}, bf16[1024,512]{0,1:T(8,128)(2,1)}, u32[]{:S(2)}, u32[]{:S(2)}) collective-permute-start(bf16[1024,512]{0,1:T(8,128)(2,1)S(1)} %multiply_convert_fusion.2), channel_id=1, source_target_pairs={{0,8},{4,12},{8,0},{12,4},{16,24},{20,28},{24,16},{28,20},{1,9},{5... | collective-permute-start | bytes 3145736 | tf_op jit(solution)/shard_map/ppermute | solution.py:16
  10.7 20.8 %copy-start.1 = (bf16[3,512,512]{2,1,0:T(8,128)(2,1)S(1)}, bf16[3,512,512]{2,1,0:T(8,128)(2,1)}, u32[]{:S(2)}) copy-start(bf16[3,512,512]{2,1,0:T(8,128)(2,1)} %param.9) | copy-start | bytes 4718596
  33.9 24.8 %collective-permute-start.2 = (bf16[1024,512]{0,1:T(8,128)(2,1)S(1)}, bf16[1024,512]{0,1:T(8,128)(2,1)S(1)}, u32[]{:S(2)}, u32[]{:S(2)}) collective-permute-start(bf16[1024,512]{0,1:T(8,128)(2,1)S(1)} %multiply_convert_fusion.1), channel_id=1, source_target_pairs={{0,16},{4,20},{8,24},{12,28},{16,0},{20,4},{24,8},{28,12},{1,17},{... | collective-permute-start | bytes 3145736 | tf_op jit(solution)/shard_map/ppermute | solution.py:16
  67.0 3.8 %copy-start.2 = (bf16[1,512,512]{2,1,0:T(8,128)(2,1)S(1)}, bf16[1,512,512]{2,1,0:T(8,128)(2,1)}, u32[]{:S(2)}) copy-start(bf16[1,512,512]{2,1,0:T(8,128)(2,1)} %param.10) | copy-start | bytes 1572868
  67.0 4.0 %copy-start.4 = (s32[1,8,8]{2,1,0:T(8,128)S(1)}, s32[1,8,8]{2,1,0:T(8,128)}, u32[]{:S(2)}) copy-start(s32[1,8,8]{2,1,0:T(8,128)} %param.11) | copy-start | bytes 772
  67.0 30.4 %all-to-all-start = ((bf16[8,256,512]{2,1,0:T(8,128)(2,1)}), bf16[8,256,512]{2,1,0:T(8,128)(2,1)S(1)}, u32[]{:S(2)}, u32[]{:S(2)}) async-start(bf16[8,256,512]{2,1,0:T(8,128)(2,1)} %bitcast.11), calls=%async_computation | async-start | bytes 4194304 | tf_op jit(solution)/shard_map/all_to_all | solution.py:42
  100.0 30.2 %all-to-all-start.1 = ((bf16[8,256,512]{2,1,0:T(8,128)(2,1)}), bf16[8,256,512]{2,1,0:T(8,128)(2,1)S(1)}, u32[]{:S(2)}, u32[]{:S(2)}) async-start(bf16[8,256,512]{2,1,0:T(8,128)(2,1)} %convolution_convert_fusion), calls=%async_computation.1 | async-start | bytes 4194304 | tf_op jit(solution)/shard_map/all_to_all | solution.py:47
where the time goes:
time: 136 us; the launch traced here: 135 us
  waiting for transfers between devices  95.1 us (70%)
  local copies, waits for them, and re-layouts  13.1 us (10%)
  starting transfers between devices  12.6 us (9%)
  matrix products  10.9 us (8%)
  other arithmetic  3.37 us (2%)
    ppermute x3, waiting for transfers between devices, swapped(): return lax.ppermute(value, axis, pairs)  42.5 us
    all_to_all x1, waiting for transfers between devices, local(): lax.all_to_all(result, 'leaf', split_axis=0, concat_axis=0, tiled=True)  26.6 us
    all_to_all x1, waiting for transfers between devices, local(): lax.all_to_all(sectioned, 'leaf', split_axis=0, concat_axis=0, tiled=True)  26.1 us
    scatter x1, local copies, waits for them, and re-layouts, local(): jnp.zeros((leaves * capacity, features), jnp.bfloat16).at[position]  6.7 us
    ppermute x3, starting transfers between devices, swapped(): return lax.ppermute(value, axis, pairs)  5.21 us
    gather x1, local copies, waits for them, and re-layouts, local(): return returned[position]  5.07 us
    dot_general x3, matrix products, local(): jnp.dot(sibling, sibling_proj[tree_level], preferred_element_type=jnp.flo...  4.63 us
    all_to_all x1, starting transfers between devices, local(): lax.all_to_all(sectioned, 'leaf', split_axis=0, concat_axis=0, tiled=True)  3.78 us
  transfers between devices with their start and end apart: 5, of which 5 were waited for; matrix products, arithmetic and copies ran while one was open for 5% of the time, Pallas kernels for 0%

commit v1 on v0

v1 whole, which is shorter than its diff:
```python
import functools
import jax
import jax.numpy as jnp
from jax import lax
from jax.experimental import pallas as pl
from jax.experimental.pallas import tpu as pltpu
from jax.sharding import PartitionSpec as P

BS = 64
LEVELS = 3
EPSILON = 1e-06
VMEM = pl.BlockSpec(memory_space=pltpu.VMEM)
SMEM = pl.BlockSpec(memory_space=pltpu.SMEM)


def swapped(value, mask):
    pairs = [(source, source ^ mask) for source in range(lax.axis_size("leaf"))]
    return lax.ppermute(value, "leaf", pairs)


def mixed(own, sibling, keep, cross):
    combined = jnp.dot(own, keep, preferred_element_type=jnp.float32)
    combined = combined + jnp.dot(sibling, cross, preferred_element_type=jnp.float32)
    scale_rows = lax.rsqrt(jnp.mean(combined * combined, axis=1, keepdims=True) + EPSILON)
    return (combined * scale_rows).astype(jnp.bfloat16)


def call(body, outs, cost, n_smem, *args):
    return pl.pallas_call(
        body,
        out_shape=outs,
        in_specs=[SMEM] * n_smem + [VMEM] * (len(args) - n_smem),
        out_specs=jax.tree.map(lambda _: VMEM, outs),
        cost_estimate=pl.CostEstimate(flops=cost, bytes_accessed=4 << 20, transcendentals=0),
        compiler_params=pltpu.CompilerParams(vmem_limit_bytes=40 << 20),
    )(*args)


def first_level(chip, own, sibling, keep, cross, *outs):
    size = outs[0].shape[0]
    for m, out in enumerate(outs):
        rows = pl.ds(pl.multiple_of((chip[0] ^ m) * size, size), size)
        out[...] = mixed(own[rows, :], sibling[rows, :], keep[...], cross[...])


def later_levels(x0, x1, x2, x3, keep, cross, *outs):
    current = [x0[...], x1[...], x2[...], x3[...]]
    current = [mixed(current[m], current[m ^ 1], keep[1], cross[1]) for m in range(4)]
    for m in range(4):
        outs[m][...] = mixed(current[m], current[m ^ 2], keep[2], cross[2])


def masked_coupling(coupling, pattern, out):
    for i in range(pattern.shape[1]):
        row = jnp.concatenate(
            [jnp.full((BS, BS), pattern[0, i, j], jnp.int32) for j in range(pattern.shape[2])], axis=1
        )
        block = coupling[0, i * BS : (i + 1) * BS, :]
        out[i * BS : (i + 1) * BS, :] = jnp.where(row != 0, block, jnp.zeros_like(block))


def couple(n_owner, me, owners, x0, x1, x2, x3, *rest):
    dense, out = rest[:n_owner], rest[n_owner]
    size = x0.shape[0]
    for m, x in enumerate((x0, x1, x2, x3)):
        rows = pl.ds(pl.multiple_of(((me[0] >> 1) ^ m) * size, size), size)
        relative = owners[rows, :] ^ me[0]
        total = jnp.zeros(x.shape, jnp.float32)
        value = x[...]
        for o in range(n_owner):
            chosen = jnp.where(relative == o, value, jnp.zeros_like(value))
            total += jnp.dot(chosen, dense[o][...], preferred_element_type=jnp.float32)
        out[rows, :] = total.astype(jnp.bfloat16)


def gathered_coupling(dense):
    across = [dense] + [swapped(dense, 2 * m) for m in range(1, 4)]
    return [each for mine in across for each in (mine, swapped(mine, 1))]


def routed(current, owners, dense):
    row_count, features = current.shape
    leaves = lax.axis_size("leaf")
    capacity = 2 * row_count // leaves
    target = owners[:, 0]
    onehot = (target[:, None] == jnp.arange(leaves, dtype=jnp.int32)[None, :]).astype(jnp.int32)
    slot_index = jnp.sum(jnp.cumsum(onehot, axis=0) * onehot, axis=1) - 1
    position = target * capacity + slot_index
    outgoing = jnp.zeros((leaves * capacity, features), jnp.bfloat16).at[position].set(current)
    sectioned = outgoing.reshape(leaves, capacity, features)
    arrived = lax.all_to_all(sectioned, "leaf", split_axis=0, concat_axis=0, tiled=True)
    product = jnp.einsum("...m,mn->...n", arrived, dense, preferred_element_type=jnp.float32)
    result = product.astype(jnp.bfloat16)
    returned = lax.all_to_all(result, "leaf", split_axis=0, concat_axis=0, tiled=True)
    return returned.reshape(leaves * capacity, features)[position]


def local(interface, owners, keep_proj, sibling_proj, coupling, pattern):
    rows, features = interface.shape
    leaves = lax.axis_size("leaf")
    me = lax.axis_index("leaf").astype(jnp.int32)
    quarter = rows // 4
    work = 4 * rows * features * features
    part = jax.ShapeDtypeStruct((quarter, features), jnp.bfloat16)
    chip = (me // 2 % 4).reshape(1)

    sibling = swapped(interface, 1)
    dense = call(
        masked_coupling, jax.ShapeDtypeStruct(coupling.shape[1:], jnp.bfloat16), 0, 0, coupling, pattern
    )
    few = leaves == 8
    if few:
        matrices = gathered_coupling(dense)
    sent = call(first_level, [part] * 4, work, 1, chip, interface, sibling, keep_proj[0], sibling_proj[0])
    mixed_rows = [sent[0]] + [swapped(sent[m], 2 * m) for m in range(1, 4)]
    done = call(later_levels, [part] * 4, 2 * work, 0, *mixed_rows, keep_proj, sibling_proj)
    back = [done[0]] + [swapped(done[m], 2 * m) for m in range(1, 4)]
    if few:
        return call(
            functools.partial(couple, leaves),
            jax.ShapeDtypeStruct((rows, features), jnp.bfloat16),
            2 * work,
            1,
            me.reshape(1),
            owners,
            *back,
            *matrices,
        )
    current = jnp.zeros((rows, features), jnp.bfloat16)
    for m in range(4):
        current = lax.dynamic_update_slice_in_dim(current, back[m], (chip[0] ^ m) * quarter, 0)
    return routed(current, owners, dense)


def solution(mesh):
    in_specs = (
        P(("leaf", "blk"), None),
        P(("leaf", "blk"), None),
        P(),
        P(),
        P("leaf", None, None),
        P("leaf", None, None),
    )
    out_specs = P(("leaf", "blk"), None)
    return jax.shard_map(local, mesh=mesh, in_specs=in_specs, out_specs=out_specs, check_vma=False)
```

time: 136 us -> 70.7 us (0.52)
  waiting for transfers between devices: 95.1 us -> 39 us
  Pallas kernels: 0 us -> 11.8 us
  matrix products: 10.9 us -> 0 us
  local copies, waits for them, and re-layouts: 13.1 us -> 4.9 us
  other arithmetic: 3.37 us -> 0 us
  starting transfers between devices: 12.6 us -> 14.7 us
    all_to_all x2 -> x0, waiting for transfers between devices: 52.7 us -> none  [the longest x1 26.6 us: local(): lax.all_to_all(result, 'leaf', split_axis=0, concat_axis=0, tiled=True)]
    pallas_call x0 -> x4, Pallas kernels: none -> 11.8 us  [call(): pl.pallas_call(body, out_shape=outs, in_specs=[SMEM] * n_smem + [VMEM] *...]
    dot_general x7 -> x0, matrix products: 10.9 us -> none  [the longest x3 4.63 us: local(): jnp.dot(sibling, sibling_proj[tree_level], preferred_element_type=jnp.flo...]
    ppermute x3 -> x14, starting transfers between devices: 5.21 us -> 14.7 us  [swapped(): return lax.ppermute(value, 'leaf', pairs)]
    all_to_all x2 -> x0, starting transfers between devices: 7.39 us -> none  [the longest x1 3.78 us: local(): lax.all_to_all(sectioned, 'leaf', split_axis=0, concat_axis=0, tiled=True)]
    scatter x1 -> x0, local copies, waits for them, and re-layouts: 6.7 us -> none  [local(): jnp.zeros((leaves * capacity, features), jnp.bfloat16).at[position]]
    gather x1 -> x0, local copies, waits for them, and re-layouts: 5.07 us -> none  [local(): return returned[position]]
    ppermute x3 -> x14, waiting for transfers between devices: 42.5 us -> 39 us  [swapped(): return lax.ppermute(value, 'leaf', pairs)]
  transfers between devices with their start and end apart: 5 -> 14, of which waited for: 5 -> 5; matrix products, arithmetic and copies ran while one was open for 5% -> 2% of each run, Pallas kernels for 0% -> 7%
where the time goes in v1:
time: 70.7 us; the launch traced here: 70.5 us
  waiting for transfers between devices  39 us (55%)
  starting transfers between devices  14.7 us (21%)
  Pallas kernels  11.8 us (17%)
  local copies, waits for them, and re-layouts  4.9 us (7%)
    ppermute x14, waiting for transfers between devices, swapped(): return lax.ppermute(value, 'leaf', pairs)  39 us
    ppermute x14, starting transfers between devices, swapped(): return lax.ppermute(value, 'leaf', pairs)  14.7 us
    pallas_call x4, Pallas kernels, call(): pl.pallas_call(body, out_shape=outs, in_specs=[SMEM] * n_smem + [VMEM] *...  11.8 us
    unnamed x17, local copies, waits for them, and re-layouts  3.63 us
  transfers between devices with their start and end apart: 14, of which 5 were waited for; matrix products, arithmetic and copies ran while one was open for 2% of the time, Pallas kernels for 7%

profile of v1, /device:TPU:0, one launch (start us, length us, event | category | flops | bytes accessed | tf_op | source)
XLA Modules:
  0.0 70.5 jit_solution(3500745387703274168)
XLA Ops:
  0.0 0.5 collective-permute-start
  0.5 1.0 %copy-done = bf16[1,512,512]{2,1,0:T(8,128)(2,1)S(1)} copy-done((bf16[1,512,512]{2,1,0:T(8,128)(2,1)S(1)}, bf16[1,512,512]{2,1,0:T(8,128)(2,1)}, u32[]{:S(2)}) %copy-start) | copy-done | bytes 524312
  1.5 0.7 copy-done.3
  2.2 0.2 shard_map.66.rest_0_
  2.4 2.6 %collective-permute-start.10 = (bf16[512,512]{1,0:T(8,128)(2,1)S(1)}, bf16[512,512]{1,0:T(8,128)(2,1)S(1)}, u32[]{:S(2)}, u32[]{:S(2)}) collective-permute-start(bf16[512,512]{1,0:T(8,128)(2,1)S(1)} %shard_map.66.rest_0_), channel_id=1, source_target_pairs={{0,16},{4,20},{8,24},{12,28},{16,0},{20,4},{24,8},{28,12},{1,17},{... | collective-permute-start | bytes 1572872 | tf_op jit(solution)/shard_map/ppermute | solution.py:18
  5.0 1.4 %collective-permute-start.12 = (bf16[512,512]{1,0:T(8,128)(2,1)S(1)}, bf16[512,512]{1,0:T(8,128)(2,1)}, u32[]{:S(2)}, u32[]{:S(2)}) collective-permute-start(bf16[512,512]{1,0:T(8,128)(2,1)S(1)} %shard_map.66.rest_0_), channel_id=1, source_target_pairs={{0,24},{4,28},{8,16},{12,20},{16,8},{20,12},{24,0},{28,4},{1,25},{... | collective-permute-start | bytes 1572872 | tf_op jit(solution)/shard_map/ppermute | solution.py:18
  6.5 1.3 %slice_bitcast_fusion = (bf16[512,512]{1,0:T(8,128)(2,1)S(1)}, bf16[512,512]{1,0:T(8,128)(2,1)S(1)}) fusion(bf16[3,512,512]{2,1,0:T(8,128)(2,1)} %cross.1, bf16[3,512,512]{2,1,0:T(8,128)(2,1)} %keep.1), kind=kLoop, calls=%fused_computation | loop fusion | bytes 2097152 | tf_op jit(solution)/shard_map/squeeze | solution.py:114
  7.8 1.4 %shard_map.64 = (bf16[256,512]{1,0:T(8,128)(2,1)S(1)}, bf16[256,512]{1,0:T(8,128)(2,1)S(1)}, bf16[256,512]{1,0:T(8,128)(2,1)S(1)}, bf16[256,512]{1,0:T(8,128)(2,1)S(1)}) custom-call(s32[1]{0:T(128)} %bitcast.1.chip, bf16[1024,512]{1,0:T(8,128)(2,1)S(1)} %copy-done.4, bf16[1024,512]{1,0:T(8,128)(2,1)S(1)} %collective-permute-done.sibling, ...), custom_call_target="tpu_custom_call" | custom-call | flops 1073741824 | bytes 4194304 | tf_op jit(solution)/shard_map/pallas_call | solution.py:29
  9.2 2.0 %collective-permute-start.1 = (bf16[256,512]{1,0:T(8,128)(2,1)S(1)}, bf16[256,512]{1,0:T(8,128)(2,1)S(1)}, u32[]{:S(2)}, u32[]{:S(2)}) collective-permute-start(bf16[256,512]{1,0:T(8,128)(2,1)S(1)} %get-tuple-element.14), channel_id=1, source_target_pairs={{0,8},{4,12},{8,0},{12,4},{16,24},{20,28},{24,16},{28,20},{1,9},{5... | collective-permute-start | bytes 786440 | tf_op jit(solution)/shard_map/ppermute | solution.py:18
  11.2 17.6 %collective-permute-done.10.rest_4_ = bf16[512,512]{1,0:T(8,128)(2,1)S(1)} collective-permute-done((bf16[512,512]{1,0:T(8,128)(2,1)S(1)}, bf16[512,512]{1,0:T(8,128)(2,1)S(1)}, u32[]{:S(2)}, u32[]{:S(2)}) %collective-permute-start.10) | collective-permute-done | bytes 524320 | tf_op jit(solution)/shard_map/ppermute | solution.py:18
  28.8 1.7 %collective-permute-start.2 = (bf16[256,512]{1,0:T(8,128)(2,1)S(1)}, bf16[256,512]{1,0:T(8,128)(2,1)S(1)}, u32[]{:S(2)}, u32[]{:S(2)}) collective-permute-start(bf16[256,512]{1,0:T(8,128)(2,1)S(1)} %get-tuple-element.15), channel_id=1, source_target_pairs={{0,16},{4,20},{8,24},{12,28},{16,0},{20,4},{24,8},{28,12},{1,17},{... | collective-permute-start | bytes 786440 | tf_op jit(solution)/shard_map/ppermute | solution.py:18
  30.6 2.9 %collective-permute-start.3 = (bf16[256,512]{1,0:T(8,128)(2,1)S(1)}, bf16[256,512]{1,0:T(8,128)(2,1)S(1)}, u32[]{:S(2)}, u32[]{:S(2)}) collective-permute-start(bf16[256,512]{1,0:T(8,128)(2,1)S(1)} %get-tuple-element.16), channel_id=1, source_target_pairs={{0,24},{4,28},{8,16},{12,20},{16,8},{20,12},{24,0},{28,4},{1,25},{... | collective-permute-start | bytes 786440 | tf_op jit(solution)/shard_map/ppermute | solution.py:18
  33.5 2.6 %collective-permute-done.1.x1 = bf16[256,512]{1,0:T(8,128)(2,1)S(1)} collective-permute-done((bf16[256,512]{1,0:T(8,128)(2,1)S(1)}, bf16[256,512]{1,0:T(8,128)(2,1)S(1)}, u32[]{:S(2)}, u32[]{:S(2)}) %collective-permute-start.1) | collective-permute-done | bytes 262176 | tf_op jit(solution)/shard_map/ppermute | solution.py:18
  36.1 6.6 %collective-permute-done.2.x2 = bf16[256,512]{1,0:T(8,128)(2,1)S(1)} collective-permute-done((bf16[256,512]{1,0:T(8,128)(2,1)S(1)}, bf16[256,512]{1,0:T(8,128)(2,1)S(1)}, u32[]{:S(2)}, u32[]{:S(2)}) %collective-permute-start.2) | collective-permute-done | bytes 262176 | tf_op jit(solution)/shard_map/ppermute | solution.py:18
  42.7 3.1 %shard_map.65 = (bf16[256,512]{1,0:T(8,128)(2,1)S(1)}, bf16[256,512]{1,0:T(8,128)(2,1)}, bf16[256,512]{1,0:T(8,128)(2,1)}, bf16[256,512]{1,0:T(8,128)(2,1)}) custom-call(bf16[256,512]{1,0:T(8,128)(2,1)S(1)} %get-tuple-element.13.x0, bf16[256,512]{1,0:T(8,128)(2,1)S(1)} %collective-permute-done.1.x1, bf16[256,512]{1,0:T(8,128)(2,1)S(1)} %collective-permute-done.2.x2, ...), custom_call_target="tpu_custom_call" | custom-call | flops 2147483648 | bytes 4194304 | tf_op jit(solution)/shard_map/pallas_call | solution.py:29
  45.8 0.7 %copy-done.5 = bf16[256,512]{1,0:T(8,128)(2,1)} copy-done((bf16[256,512]{1,0:T(8,128)(2,1)}, bf16[256,512]{1,0:T(8,128)(2,1)S(1)}, u32[]{:S(2)}) %copy-start.5) | copy-done | bytes 262168
  46.5 1.5 %collective-permute-start.4 = (bf16[256,512]{1,0:T(8,128)(2,1)}, bf16[256,512]{1,0:T(8,128)(2,1)S(1)}, u32[]{:S(2)}, u32[]{:S(2)}) collective-permute-start(bf16[256,512]{1,0:T(8,128)(2,1)} %get-tuple-element.18), channel_id=1, source_target_pairs={{0,8},{4,12},{8,0},{12,4},{16,24},{20,28},{24,16},{28,20},{1,9},{5... | collective-permute-start | bytes 786440 | tf_op jit(solution)/shard_map/ppermute | solution.py:18
  48.1 1.5 %collective-permute-start.5 = (bf16[256,512]{1,0:T(8,128)(2,1)}, bf16[256,512]{1,0:T(8,128)(2,1)}, u32[]{:S(2)}, u32[]{:S(2)}) collective-permute-start(bf16[256,512]{1,0:T(8,128)(2,1)} %get-tuple-element.19), channel_id=1, source_target_pairs={{0,16},{4,20},{8,24},{12,28},{16,0},{20,4},{24,8},{28,12},{1,17},{... | collective-permute-start | bytes 786440 | tf_op jit(solution)/shard_map/ppermute | solution.py:18
  49.6 0.5 collective-permute-start.6
  50.0 0.2 copy.7.owners
  50.3 5.6 %collective-permute-done.4.x1 = bf16[256,512]{1,0:T(8,128)(2,1)S(1)} collective-permute-done((bf16[256,512]{1,0:T(8,128)(2,1)}, bf16[256,512]{1,0:T(8,128)(2,1)S(1)}, u32[]{:S(2)}, u32[]{:S(2)}) %collective-permute-start.4) | collective-permute-done | bytes 262176 | tf_op jit(solution)/shard_map/ppermute | solution.py:18
  55.9 6.6 %collective-permute-done.5.x2 = bf16[256,512]{1,0:T(8,128)(2,1)} collective-permute-done((bf16[256,512]{1,0:T(8,128)(2,1)}, bf16[256,512]{1,0:T(8,128)(2,1)}, u32[]{:S(2)}, u32[]{:S(2)}) %collective-permute-start.5) | collective-permute-done | bytes 262176 | tf_op jit(solution)/shard_map/ppermute | solution.py:18
  62.4 0.9 %copy-done.6 = bf16[256,512]{1,0:T(8,128)(2,1)S(1)} copy-done((bf16[256,512]{1,0:T(8,128)(2,1)S(1)}, bf16[256,512]{1,0:T(8,128)(2,1)}, u32[]{:S(2)}) %copy-start.6) | copy-done | bytes 262168
  63.4 7.1 %shard_map.67 = bf16[1024,512]{1,0:T(8,128)(2,1)} custom-call(s32[1]{0:T(128)} %bitcast.me, s32[1024,1]{1,0:T(8,128)S(1)} %copy.7.owners, bf16[256,512]{1,0:T(8,128)(2,1)S(1)} %copy-done.6, bf16[256,512]{1,0:T(8,128)(2,1)S(1)} %collective-permute-done.4.x1, bf16[256,512]{1,0:T(8,128)(2,1)} %collective-permute-done.5.x2, ...), custom_call_target="tpu_custom_call" | custom-call | flops 2147483648 | bytes 4194304 | tf_op jit(solution)/shard_map/pallas_call | solution.py:29
  (26 shorter events, 0.2 us)
Async XLA Ops:
  0.0 7.8 %collective-permute-start = (bf16[1024,512]{1,0:T(8,128)(2,1)}, bf16[1024,512]{1,0:T(8,128)(2,1)S(1)}, u32[]{:S(2)}, u32[]{:S(2)}) collective-permute-start(bf16[1024,512]{1,0:T(8,128)(2,1)} %own.1), channel_id=1, source_target_pairs={{0,4},{4,0},{8,12},{12,8},{16,20},{20,16},{24,28},{28,24},{1,5},{5... | collective-permute-start | bytes 3145736 | tf_op jit(solution)/shard_map/ppermute | solution.py:18
  0.5 1.0 %copy-start = (bf16[1,512,512]{2,1,0:T(8,128)(2,1)S(1)}, bf16[1,512,512]{2,1,0:T(8,128)(2,1)}, u32[]{:S(2)}) copy-start(bf16[1,512,512]{2,1,0:T(8,128)(2,1)} %coupling.1) | copy-start | bytes 1572868
  1.5 0.7 copy-start.3
  2.2 5.6 %copy-start.4 = (bf16[1024,512]{1,0:T(8,128)(2,1)S(1)}, bf16[1024,512]{1,0:T(8,128)(2,1)}, u32[]{:S(2)}) copy-start(bf16[1024,512]{1,0:T(8,128)(2,1)} %own.1) | copy-start | bytes 3145732
  2.4 26.4 %collective-permute-start.10 = (bf16[512,512]{1,0:T(8,128)(2,1)S(1)}, bf16[512,512]{1,0:T(8,128)(2,1)S(1)}, u32[]{:S(2)}, u32[]{:S(2)}) collective-permute-start(bf16[512,512]{1,0:T(8,128)(2,1)S(1)} %shard_map.66.rest_0_), channel_id=1, source_target_pairs={{0,16},{4,20},{8,24},{12,28},{16,0},{20,4},{24,8},{28,12},{1,17},{... | collective-permute-start | bytes 1572872 | tf_op jit(solution)/shard_map/ppermute | solution.py:18
  5.0 25.6 %collective-permute-start.12 = (bf16[512,512]{1,0:T(8,128)(2,1)S(1)}, bf16[512,512]{1,0:T(8,128)(2,1)}, u32[]{:S(2)}, u32[]{:S(2)}) collective-permute-start(bf16[512,512]{1,0:T(8,128)(2,1)S(1)} %shard_map.66.rest_0_), channel_id=1, source_target_pairs={{0,24},{4,28},{8,16},{12,20},{16,8},{20,12},{24,0},{28,4},{1,25},{... | collective-permute-start | bytes 1572872 | tf_op jit(solution)/shard_map/ppermute | solution.py:18
  6.4 24.2 %collective-permute-start.8 = (bf16[512,512]{1,0:T(8,128)(2,1)S(1)}, bf16[512,512]{1,0:T(8,128)(2,1)}, u32[]{:S(2)}, u32[]{:S(2)}) collective-permute-start(bf16[512,512]{1,0:T(8,128)(2,1)S(1)} %shard_map.66.rest_0_), channel_id=1, source_target_pairs={{0,8},{4,12},{8,0},{12,4},{16,24},{20,28},{24,16},{28,20},{1,9},{5... | collective-permute-start | bytes 1572872 | tf_op jit(solution)/shard_map/ppermute | solution.py:18
  6.5 41.6 %collective-permute-start.7 = (bf16[512,512]{1,0:T(8,128)(2,1)S(1)}, bf16[512,512]{1,0:T(8,128)(2,1)}, u32[]{:S(2)}, u32[]{:S(2)}) collective-permute-start(bf16[512,512]{1,0:T(8,128)(2,1)S(1)} %shard_map.66.rest_0_), channel_id=1, source_target_pairs={{0,4},{4,0},{8,12},{12,8},{16,20},{20,16},{24,28},{28,24},{1,5},{5... | collective-permute-start | bytes 1572872 | tf_op jit(solution)/shard_map/ppermute | solution.py:18
  7.8 34.9 %copy-start.1 = (bf16[3,512,512]{2,1,0:T(8,128)(2,1)S(1)}, bf16[3,512,512]{2,1,0:T(8,128)(2,1)}, u32[]{:S(2)}) copy-start(bf16[3,512,512]{2,1,0:T(8,128)(2,1)} %cross.1) | copy-start | bytes 4718596
  7.8 34.9 %copy-start.2 = (bf16[3,512,512]{2,1,0:T(8,128)(2,1)S(1)}, bf16[3,512,512]{2,1,0:T(8,128)(2,1)}, u32[]{:S(2)}) copy-start(bf16[3,512,512]{2,1,0:T(8,128)(2,1)} %keep.1) | copy-start | bytes 4718596
  9.2 26.9 %collective-permute-start.1 = (bf16[256,512]{1,0:T(8,128)(2,1)S(1)}, bf16[256,512]{1,0:T(8,128)(2,1)S(1)}, u32[]{:S(2)}, u32[]{:S(2)}) collective-permute-start(bf16[256,512]{1,0:T(8,128)(2,1)S(1)} %get-tuple-element.14), channel_id=1, source_target_pairs={{0,8},{4,12},{8,0},{12,4},{16,24},{20,28},{24,16},{28,20},{1,9},{5... | collective-permute-start | bytes 786440 | tf_op jit(solution)/shard_map/ppermute | solution.py:18
  28.8 13.9 %collective-permute-start.2 = (bf16[256,512]{1,0:T(8,128)(2,1)S(1)}, bf16[256,512]{1,0:T(8,128)(2,1)S(1)}, u32[]{:S(2)}, u32[]{:S(2)}) collective-permute-start(bf16[256,512]{1,0:T(8,128)(2,1)S(1)} %get-tuple-element.15), channel_id=1, source_target_pairs={{0,16},{4,20},{8,24},{12,28},{16,0},{20,4},{24,8},{28,12},{1,17},{... | collective-permute-start | bytes 786440 | tf_op jit(solution)/shard_map/ppermute | solution.py:18
  30.5 19.0 %collective-permute-start.11 = (bf16[512,512]{1,0:T(8,128)(2,1)S(1)}, bf16[512,512]{1,0:T(8,128)(2,1)S(1)}, u32[]{:S(2)}, u32[]{:S(2)}) collective-permute-start(bf16[512,512]{1,0:T(8,128)(2,1)S(1)} %collective-permute-done.10.rest_4_), channel_id=1, source_target_pairs={{0,4},{4,0},{8,12},{12,8},{16,20},{20,16},{24,28},{28,24},{1,5},{5... | collective-permute-start | bytes 1572872 | tf_op jit(solution)/shard_map/ppermute | solution.py:18
  30.6 12.1 %collective-permute-start.3 = (bf16[256,512]{1,0:T(8,128)(2,1)S(1)}, bf16[256,512]{1,0:T(8,128)(2,1)S(1)}, u32[]{:S(2)}, u32[]{:S(2)}) collective-permute-start(bf16[256,512]{1,0:T(8,128)(2,1)S(1)} %get-tuple-element.16), channel_id=1, source_target_pairs={{0,24},{4,28},{8,16},{12,20},{16,8},{20,12},{24,0},{28,4},{1,25},{... | collective-permute-start | bytes 786440 | tf_op jit(solution)/shard_map/ppermute | solution.py:18
  36.1 14.2 %collective-permute-start.13 = (bf16[512,512]{1,0:T(8,128)(2,1)}, bf16[512,512]{1,0:T(8,128)(2,1)S(1)}, u32[]{:S(2)}, u32[]{:S(2)}) collective-permute-start(bf16[512,512]{1,0:T(8,128)(2,1)} %collective-permute-done.12.rest_6_), channel_id=1, source_target_pairs={{0,4},{4,0},{8,12},{12,8},{16,20},{20,16},{24,28},{28,24},{1,5},{5... | collective-permute-start | bytes 1572872 | tf_op jit(solution)/shard_map/ppermute | solution.py:18
  42.7 7.6 %collective-permute-start.9 = (bf16[512,512]{1,0:T(8,128)(2,1)}, bf16[512,512]{1,0:T(8,128)(2,1)S(1)}, u32[]{:S(2)}, u32[]{:S(2)}) collective-permute-start(bf16[512,512]{1,0:T(8,128)(2,1)} %collective-permute-done.8.rest_2_), channel_id=1, source_target_pairs={{0,4},{4,0},{8,12},{12,8},{16,20},{20,16},{24,28},{28,24},{1,5},{5... | collective-permute-start | bytes 1572872 | tf_op jit(solution)/shard_map/ppermute | solution.py:18
  42.7 7.4 %copy-start.7 = (s32[1024,1]{0,1:T(1,128)S(1)}, s32[1024,1]{0,1:T(1,128)}, u32[]{:S(2)}) copy-start(s32[1024,1]{0,1:T(1,128)} %param.7) | copy-start | bytes 12292
  45.8 0.7 %copy-start.5 = (bf16[256,512]{1,0:T(8,128)(2,1)}, bf16[256,512]{1,0:T(8,128)(2,1)S(1)}, u32[]{:S(2)}) copy-start(bf16[256,512]{1,0:T(8,128)(2,1)S(1)} %get-tuple-element.17.x0) | copy-start | bytes 786436
  46.5 9.3 %collective-permute-start.4 = (bf16[256,512]{1,0:T(8,128)(2,1)}, bf16[256,512]{1,0:T(8,128)(2,1)S(1)}, u32[]{:S(2)}, u32[]{:S(2)}) collective-permute-start(bf16[256,512]{1,0:T(8,128)(2,1)} %get-tuple-element.18), channel_id=1, source_target_pairs={{0,8},{4,12},{8,0},{12,4},{16,24},{20,28},{24,16},{28,20},{1,9},{5... | collective-permute-start | bytes 786440 | tf_op jit(solution)/shard_map/ppermute | solution.py:18
  48.1 14.4 %collective-permute-start.5 = (bf16[256,512]{1,0:T(8,128)(2,1)}, bf16[256,512]{1,0:T(8,128)(2,1)}, u32[]{:S(2)}, u32[]{:S(2)}) collective-permute-start(bf16[256,512]{1,0:T(8,128)(2,1)} %get-tuple-element.19), channel_id=1, source_target_pairs={{0,16},{4,20},{8,24},{12,28},{16,0},{20,4},{24,8},{28,12},{1,17},{... | collective-permute-start | bytes 786440 | tf_op jit(solution)/shard_map/ppermute | solution.py:18
  49.6 12.8 %collective-permute-start.6 = (bf16[256,512]{1,0:T(8,128)(2,1)}, bf16[256,512]{1,0:T(8,128)(2,1)}, u32[]{:S(2)}, u32[]{:S(2)}) collective-permute-start(bf16[256,512]{1,0:T(8,128)(2,1)} %get-tuple-element.20), channel_id=1, source_target_pairs={{0,24},{4,28},{8,16},{12,20},{16,8},{20,12},{24,0},{28,4},{1,25},{... | collective-permute-start | bytes 786440 | tf_op jit(solution)/shard_map/ppermute | solution.py:18
  62.4 1.0 %copy-start.6 = (bf16[256,512]{1,0:T(8,128)(2,1)S(1)}, bf16[256,512]{1,0:T(8,128)(2,1)}, u32[]{:S(2)}) copy-start(bf16[256,512]{1,0:T(8,128)(2,1)} %copy-done.5) | copy-start | bytes 786436

commit v2 on v0

v2 whole, which is shorter than its diff:
```python
import functools
import jax
import jax.numpy as jnp
from jax import lax
from jax.experimental import pallas as pl
from jax.experimental.pallas import tpu as pltpu
from jax.sharding import PartitionSpec as P

BS = 64
EPSILON = 1e-06
VMEM = pl.BlockSpec(memory_space=pltpu.VMEM)
SMEM = pl.BlockSpec(memory_space=pltpu.SMEM)
HBM = pl.BlockSpec(memory_space=pltpu.HBM)


def swapped(value, mask, axis="leaf"):
    pairs = [(source, source ^ mask) for source in range(lax.axis_size(axis))]
    return lax.ppermute(value, axis, pairs)


def in_hbm(value):
    return pltpu.with_memory_space_constraint(value, pltpu.HBM)


def together(*values):
    return lax.optimization_barrier(values)


def after(value, *others):
    return lax.optimization_barrier((value, *others))[0]


def mixed(own, sibling, keep, cross):
    combined = jnp.dot(own, keep, preferred_element_type=jnp.float32)
    combined = combined + jnp.dot(sibling, cross, preferred_element_type=jnp.float32)
    scale_rows = lax.rsqrt(jnp.mean(combined * combined, axis=1, keepdims=True) + EPSILON)
    return (combined * scale_rows).astype(jnp.bfloat16)


def call(body, outs, flops, specs, *args, scratch=(), aliases=None):
    return pl.pallas_call(
        body,
        out_shape=[shape for shape, _ in outs],
        in_specs=specs,
        out_specs=[spec for _, spec in outs],
        scratch_shapes=list(scratch),
        input_output_aliases=aliases or {},
        cost_estimate=pl.CostEstimate(flops=flops, bytes_accessed=flops // 512, transcendentals=0),
        compiler_params=pltpu.CompilerParams(vmem_limit_bytes=24 << 20),
    )(*args)


def block_rows(me, m, size):
    return pl.ds(pl.multiple_of((((me[0] >> 1) & 3) ^ m) * size, size), size)


def first_level(me, sibling, interface, keep, cross, *rest):
    outs, (own, keep_here, cross_here, sems) = rest[:4], rest[4:]
    size = outs[0].shape[0]
    loads = [
        pltpu.make_async_copy(keep.at[0], keep_here, sems.at[4]),
        pltpu.make_async_copy(cross.at[0], cross_here, sems.at[5]),
    ]
    order = (1, 2, 3, 0)
    for m in order:
        rows = block_rows(me, m, size)
        loads.append(pltpu.make_async_copy(interface.at[rows], own.at[rows], sems.at[m]))
    for load in loads:
        load.start()
    loads[0].wait()
    loads[1].wait()
    for m, load in zip(order, loads[2:]):
        load.wait()
        rows = block_rows(me, m, size)
        outs[m][...] = mixed(own[rows, :], sibling[rows, :], keep_here[...], cross_here[...])


def second_level(x0, x1, keep, cross, out0, out1):
    out0[...] = mixed(x0[...], x1[...], keep[0], cross[0])
    out1[...] = mixed(x1[...], x0[...], keep[0], cross[0])


def third_level(x2, x3, y0, y1, keep, cross, *outs):
    y2 = mixed(x2[...], x3[...], keep[0], cross[0])
    y3 = mixed(x3[...], x2[...], keep[0], cross[0])
    outs[1][...] = mixed(y1[...], y3, keep[1], cross[1])
    outs[2][...] = mixed(y2, y0[...], keep[1], cross[1])
    outs[3][...] = mixed(y3, y1[...], keep[1], cross[1])
    outs[0][...] = mixed(y0[...], y2, keep[1], cross[1])


def masked_coupling(z, coupling, pattern, out, part, held, shown, sems):
    loads = [pltpu.make_async_copy(pattern, shown, sems.at[0]), pltpu.make_async_copy(coupling, held, sems.at[1])]
    for load in loads:
        load.start()
    for load in loads:
        load.wait()
    for i in range(shown.shape[1]):
        row = jnp.concatenate(
            [jnp.full((BS, BS), shown[0, i, j], jnp.int32) for j in range(shown.shape[2])], axis=1
        )
        block = held[0, i * BS : (i + 1) * BS, :]
        out[i * BS : (i + 1) * BS, :] = jnp.where(row != 0, block, jnp.zeros_like(block))
    part[...] = out[half_rows(z, 0, part.shape[0]), :]


def half_rows(z, other, depth):
    return pl.ds(pl.multiple_of(((z[0] & 1) ^ other) * depth, depth), depth)


def packed(*refs):
    *parts, out = refs
    at = 0
    for part in parts:
        out[at : at + part.shape[0], :] = part[...]
        at += part.shape[0]


def couple(m, me, z, owners, x, own, beside, *rest):
    packs, (out, held, sems) = rest[:2], rest[-3:]
    size, features = x.shape
    depth = features // 2
    rows = block_rows(me, m, size)
    lanes = owners.shape[1]
    groups = size // lanes
    diagonal = lax.broadcasted_iota(jnp.int32, (lanes, lanes), 0) == lax.broadcasted_iota(jnp.int32, (lanes, lanes), 1)
    named = owners[pl.ds((((me[0] >> 1) & 3) ^ m) * groups, groups), :] ^ me[0]
    relative = jnp.concatenate(
        [jnp.sum(jnp.where(diagonal, named[i : i + 1, :], 0), axis=1, keepdims=True) for i in range(groups)], axis=0
    )
    parts = [half_rows(z, other, depth) for other in range(2)]
    values = [x[:, part] for part in parts]
    chosen = [[jnp.where(relative == r, value, jnp.zeros_like(value)) for value in values] for r in range(8)]
    copies = []
    for n in range(2):
        columns = slice(n * depth, (n + 1) * depth)
        total = jnp.zeros((size, depth), jnp.float32)
        for r in range(8):
            for h in range(2):
                if r < 2:
                    piece = (own, beside)[r][parts[h], columns]
                else:
                    at = (r // 2 - 1 + 3 * h) * depth
                    piece = packs[r % 2][at : at + depth, columns]
                total += jnp.dot(chosen[r][h], piece, preferred_element_type=jnp.float32)
        held[:, columns] = total.astype(jnp.bfloat16)
        copies.append(pltpu.make_async_copy(held.at[:, columns], out.at[rows, columns], sems.at[n]))
        copies[-1].start()
    for copy in copies:
        copy.wait()


def fetched(keep, cross, keep_here, cross_here, sems):
    loads = [
        pltpu.make_async_copy(keep.at[1:], keep_here, sems.at[0]),
        pltpu.make_async_copy(cross.at[1:], cross_here, sems.at[1]),
    ]
    for load in loads:
        load.start()
    for load in loads:
        load.wait()


def routed(current, owners, dense):
    row_count, features = current.shape
    leaves = lax.axis_size("leaf")
    capacity = 2 * row_count // leaves
    target = owners[:, 0]
    onehot = (target[:, None] == jnp.arange(leaves, dtype=jnp.int32)[None, :]).astype(jnp.int32)
    slot_index = jnp.sum(jnp.cumsum(onehot, axis=0) * onehot, axis=1) - 1
    position = target * capacity + slot_index
    outgoing = jnp.zeros((leaves * capacity, features), jnp.bfloat16).at[position].set(current)
    sectioned = outgoing.reshape(leaves, capacity, features)
    arrived = lax.all_to_all(sectioned, "leaf", split_axis=0, concat_axis=0, tiled=True)
    product = jnp.einsum("...m,mn->...n", arrived, dense, preferred_element_type=jnp.float32)
    result = product.astype(jnp.bfloat16)
    returned = lax.all_to_all(result, "leaf", split_axis=0, concat_axis=0, tiled=True)
    return returned.reshape(leaves * capacity, features)[position]


def local(interface, owners, keep_proj, sibling_proj, coupling, pattern):
    rows, features = interface.shape
    leaves = lax.axis_size("leaf")
    me = lax.axis_index("leaf").astype(jnp.int32).reshape(1)
    z = lax.axis_index("blk").astype(jnp.int32).reshape(1)
    few = leaves == 8 and lax.axis_size("blk") % 2 == 0
    quarter = rows // 4
    depth = features // 2
    block_flops = 2 * quarter * features * features

    def array(*shape, space=VMEM):
        return jax.ShapeDtypeStruct(shape, jnp.bfloat16), space

    part = array(quarter, features)
    whole = array(rows, features, space=HBM)
    matrix = array(features, features)
    weights = in_hbm(keep_proj), in_hbm(sibling_proj)

    sibling = swapped(interface, 1)
    dense, mine = call(
        masked_coupling,
        [matrix, array(depth, features)],
        1,
        [SMEM] + [HBM] * 2,
        z,
        in_hbm(coupling),
        in_hbm(pattern),
        scratch=[
            pltpu.VMEM(coupling.shape, coupling.dtype),
            pltpu.VMEM(pattern.shape, pattern.dtype),
            pltpu.SemaphoreType.DMA((2,)),
        ],
    )
    if few:
        near = swapped(mine, 2), swapped(mine, 4)
        beside = swapped(dense, 1)
        sibling = after(sibling, beside)
    sent = call(
        first_level,
        [part] * 4,
        4 * block_flops,
        [SMEM, VMEM] + [HBM] * 3,
        me,
        sibling,
        in_hbm(interface),
        *weights,
        scratch=[pltpu.VMEM((rows, features), jnp.bfloat16)]
        + [pltpu.VMEM((features, features), jnp.bfloat16)] * 2
        + [pltpu.SemaphoreType.DMA((6,))],
    )
    x = [sent[0]] + [swapped(sent[m], 2 * m) for m in (1, 2, 3)]
    weights = call(
        fetched,
        [array(2, features, features)] * 2,
        1,
        [HBM] * 2,
        *(in_hbm(w) for w in together(keep_proj, sibling_proj, sent[0])[:2]),
        scratch=[pltpu.SemaphoreType.DMA((2,))],
    )
    if few:
        x_mine, y_mine, _ = together(*near, sent[0])
        x_other, y_other = swapped(x_mine, 1, "blk"), swapped(y_mine, 1, "blk")
        d_mine, d_other = swapped(y_mine, 2), swapped(x_other, 4)
        x = together(*x)
    y0, y1 = call(second_level, [part] * 2, (1 << 34), [VMEM] * 4, x[0], x[1], *weights)
    done = call(third_level, [part] * 4, (1 << 34), [VMEM] * 6, x[2], x[3], y0, y1, *weights)
    back = [done[0]] + [swapped(done[m], 2 * m) for m in (1, 2, 3)]
    if not few:
        current = jnp.zeros((rows, features), jnp.bfloat16)
        for m in range(4):
            current = lax.dynamic_update_slice_in_dim(current, back[m], ((me[0] // 2 % 4) ^ m) * quarter, 0)
        return routed(current, owners, dense)
    pieces = [x_mine, y_mine, d_mine, x_other, y_other, d_other]
    (pack,) = call(packed, [array(6 * depth, features)], 1, [VMEM] * 6, *together(*pieces, done[0])[:6])
    matrices = [dense, beside, pack, swapped(pack, 1)]
    out = None
    for m in range(4):
        extra = [] if out is None else [out]
        (out,) = call(
            functools.partial(couple, m),
            [whole],
            8 * block_flops,
            [SMEM] * 2 + [VMEM] * (2 + len(matrices)) + [HBM] * len(extra),
            me,
            z,
            owners.reshape(-1, 128),
            back[m],
            *matrices,
            *extra,
            scratch=[pltpu.VMEM((quarter, features), jnp.bfloat16), pltpu.SemaphoreType.DMA((2,))],
            aliases={4 + len(matrices): 0} if extra else None,
        )
    return out


def solution(mesh):
    in_specs = (
        P(("leaf", "blk"), None),
        P(("leaf", "blk"), None),
        P(),
        P(),
        P("leaf", None, None),
        P("leaf", None, None),
    )
    out_specs = P(("leaf", "blk"), None)
    return jax.shard_map(local, mesh=mesh, in_specs=in_specs, out_specs=out_specs, check_vma=False)
```

time: 136 us -> 53.3 us (0.39)
  waiting for transfers between devices: 95.1 us -> 16.1 us
  Pallas kernels: 0 us -> 18.4 us
  local copies, waits for them, and re-layouts: 13.1 us -> 0.01 us
  matrix products: 10.9 us -> 0 us
  starting transfers between devices: 12.6 us -> 18.5 us
  other arithmetic: 3.37 us -> 0 us
    all_to_all x2 -> x0, waiting for transfers between devices: 52.7 us -> none  [the longest x1 26.6 us: local(): lax.all_to_all(result, 'leaf', split_axis=0, concat_axis=0, tiled=True)]
    ppermute x3 -> x15, waiting for transfers between devices: 42.5 us -> 16.1 us  [swapped(): return lax.ppermute(value, axis, pairs)]
    pallas_call x0 -> x10, Pallas kernels: none -> 18.4 us  [call(): pl.pallas_call(body, out_shape=[shape for shape, _ in outs], in_specs=spe...]
    ppermute x3 -> x15, starting transfers between devices: 5.21 us -> 18.5 us  [swapped(): return lax.ppermute(value, axis, pairs)]
    dot_general x7 -> x0, matrix products: 10.9 us -> none  [the longest x3 4.63 us: local(): jnp.dot(sibling, sibling_proj[tree_level], preferred_element_type=jnp.flo...]
    all_to_all x2 -> x0, starting transfers between devices: 7.39 us -> none  [the longest x1 3.78 us: local(): lax.all_to_all(sectioned, 'leaf', split_axis=0, concat_axis=0, tiled=True)]
    scatter x1 -> x0, local copies, waits for them, and re-layouts: 6.7 us -> none  [local(): jnp.zeros((leaves * capacity, features), jnp.bfloat16).at[position]]
    gather x1 -> x0, local copies, waits for them, and re-layouts: 5.07 us -> none  [local(): return returned[position]]
  transfers between devices with their start and end apart: 5 -> 15, of which waited for: 5 -> 8; matrix products, arithmetic and copies ran while one was open for 5% -> 0% of each run, Pallas kernels for 0% -> 30%
where the time goes in v2:
time: 53.3 us; the launch traced here: 53.1 us
  starting transfers between devices  18.5 us (35%)
  Pallas kernels  18.4 us (35%)
  waiting for transfers between devices  16.1 us (30%)
    ppermute x15, starting transfers between devices, swapped(): return lax.ppermute(value, axis, pairs)  18.5 us
    pallas_call x10, Pallas kernels, call(): pl.pallas_call(body, out_shape=[shape for shape, _ in outs], in_specs=spe...  18.4 us
    ppermute x15, waiting for transfers between devices, swapped(): return lax.ppermute(value, axis, pairs)  16.1 us
  transfers between devices with their start and end apart: 15, of which 8 were waited for; matrix products, arithmetic and copies ran while one was open for 0% of the time, Pallas kernels for 30%

profile of v2, /device:TPU:0, one launch (start us, length us, event | category | flops | bytes accessed | tf_op | source)
XLA Modules:
  0.0 53.1 jit_solution(4896486818657355724)
XLA Ops:
  0.5 1.3 %shard_map.64 = (bf16[512,512]{1,0:T(8,128)(2,1)S(1)}, bf16[256,512]{1,0:T(8,128)(2,1)S(1)}) custom-call(s32[1]{0:T(128)} %bitcast.1.z, bf16[1,512,512]{2,1,0:T(8,128)(2,1)} %coupling.1, s32[1,8,8]{2,1,0:T(8,128)} %pattern.1), custom_call_target="tpu_custom_call" | custom-call | flops 1 | tf_op jit(solution)/shard_map/pallas_call | solution.py:41
  1.9 3.0 %collective-permute-start.7 = (bf16[256,512]{1,0:T(8,128)(2,1)S(1)}, bf16[256,512]{1,0:T(8,128)(2,1)S(1)}, u32[]{:S(2)}, u32[]{:S(2)}) collective-permute-start(bf16[256,512]{1,0:T(8,128)(2,1)S(1)} %get-tuple-element.51), channel_id=1, source_target_pairs={{0,16},{4,20},{8,24},{12,28},{16,0},{20,4},{24,8},{28,12},{1,17},{... | collective-permute-start | bytes 786440 | tf_op jit(solution)/shard_map/ppermute | solution.py:18
  4.8 1.5 %collective-permute-start.6 = (bf16[256,512]{1,0:T(8,128)(2,1)S(1)}, bf16[256,512]{1,0:T(8,128)(2,1)S(1)}, u32[]{:S(2)}, u32[]{:S(2)}) collective-permute-start(bf16[256,512]{1,0:T(8,128)(2,1)S(1)} %get-tuple-element.51), channel_id=1, source_target_pairs={{0,8},{4,12},{8,0},{12,4},{16,24},{20,28},{24,16},{28,20},{1,9},{5... | collective-permute-start | bytes 786440 | tf_op jit(solution)/shard_map/ppermute | solution.py:18
  6.3 3.4 %shard_map.65 = (bf16[256,512]{1,0:T(8,128)(2,1)S(1)}, bf16[256,512]{1,0:T(8,128)(2,1)S(1)}, bf16[256,512]{1,0:T(8,128)(2,1)S(1)}, bf16[256,512]{1,0:T(8,128)(2,1)S(1)}) custom-call(s32[1]{0:T(128)} %bitcast.me, bf16[1024,512]{1,0:T(8,128)(2,1)S(1)} %collective-permute-done.sibling, bf16[1024,512]{1,0:T(8,128)(2,1)} %interface.1, bf16[3,512,512]{2,1,0:T(8,128)(2,1)} %keep.2, ...), custom_call_target="tpu_custom_call" | custom-call | flops 536870912 | bytes 1048576 | tf_op jit(solution)/shard_map/pallas_call | solution.py:41
  10.4 1.0 %collective-permute-start.3 = (bf16[256,512]{1,0:T(8,128)(2,1)S(1)}, bf16[256,512]{1,0:T(8,128)(2,1)S(1)}, u32[]{:S(2)}, u32[]{:S(2)}) collective-permute-start(bf16[256,512]{1,0:T(8,128)(2,1)S(1)} %get-tuple-element.38), channel_id=1, source_target_pairs={{0,16},{4,20},{8,24},{12,28},{16,0},{20,4},{24,8},{28,12},{1,17},{... | collective-permute-start | bytes 786440 | tf_op jit(solution)/shard_map/ppermute | solution.py:18
  11.4 1.9 %collective-permute-start.4 = (bf16[256,512]{1,0:T(8,128)(2,1)S(1)}, bf16[256,512]{1,0:T(8,128)(2,1)S(1)}, u32[]{:S(2)}, u32[]{:S(2)}) collective-permute-start(bf16[256,512]{1,0:T(8,128)(2,1)S(1)} %get-tuple-element.39), channel_id=1, source_target_pairs={{0,24},{4,28},{8,16},{12,20},{16,8},{20,12},{24,0},{28,4},{1,25},{... | collective-permute-start | bytes 786440 | tf_op jit(solution)/shard_map/ppermute | solution.py:18
  13.7 1.6 %collective-permute-start.10 = (bf16[256,512]{1,0:T(8,128)(2,1)S(1)}, bf16[256,512]{1,0:T(8,128)(2,1)S(1)}, u32[]{:S(2)}, u32[]{:S(2)}) collective-permute-start(bf16[256,512]{1,0:T(8,128)(2,1)S(1)} %collective-permute-done.7.refs_1_), channel_id=1, source_target_pairs={{0,1},{1,0},{2,3},{3,2},{4,5},{5,4},{6,7},{7,6},{8,9},{9,8},{10,11... | collective-permute-start | bytes 786440 | tf_op jit(solution)/shard_map/ppermute | solution.py:18
  15.3 1.8 %collective-permute-start.8 = (bf16[256,512]{1,0:T(8,128)(2,1)S(1)}, bf16[256,512]{1,0:T(8,128)(2,1)S(1)}, u32[]{:S(2)}, u32[]{:S(2)}) collective-permute-start(bf16[256,512]{1,0:T(8,128)(2,1)S(1)} %collective-permute-done.7.refs_1_), channel_id=1, source_target_pairs={{0,8},{4,12},{8,0},{12,4},{16,24},{20,28},{24,16},{28,20},{1,9},{5... | collective-permute-start | bytes 786440 | tf_op jit(solution)/shard_map/ppermute | solution.py:18
  17.1 1.6 %shard_map.66 = (bf16[2,512,512]{2,1,0:T(8,128)(2,1)S(1)}, bf16[2,512,512]{2,1,0:T(8,128)(2,1)S(1)}) custom-call(bf16[3,512,512]{2,1,0:T(8,128)(2,1)} %keep.2, bf16[3,512,512]{2,1,0:T(8,128)(2,1)} %cross.2), custom_call_target="tpu_custom_call" | custom-call | flops 1 | tf_op jit(solution)/shard_map/pallas_call | solution.py:41
  18.7 0.6 %collective-permute-done.2.x1 = bf16[256,512]{1,0:T(8,128)(2,1)S(1)} collective-permute-done((bf16[256,512]{1,0:T(8,128)(2,1)S(1)}, bf16[256,512]{1,0:T(8,128)(2,1)S(1)}, u32[]{:S(2)}, u32[]{:S(2)}) %collective-permute-start.2) | collective-permute-done | bytes 262176 | tf_op jit(solution)/shard_map/ppermute | solution.py:18
  19.3 1.6 %collective-permute-start.9 = (bf16[256,512]{1,0:T(8,128)(2,1)S(1)}, bf16[256,512]{1,0:T(8,128)(2,1)S(1)}, u32[]{:S(2)}, u32[]{:S(2)}) collective-permute-start(bf16[256,512]{1,0:T(8,128)(2,1)S(1)} %collective-permute-done.6.refs_0_), channel_id=1, source_target_pairs={{0,1},{1,0},{2,3},{3,2},{4,5},{5,4},{6,7},{7,6},{8,9},{9,8},{10,11... | collective-permute-start | bytes 786440 | tf_op jit(solution)/shard_map/ppermute | solution.py:18
  20.9 3.7 %collective-permute-done.4.x3 = bf16[256,512]{1,0:T(8,128)(2,1)S(1)} collective-permute-done((bf16[256,512]{1,0:T(8,128)(2,1)S(1)}, bf16[256,512]{1,0:T(8,128)(2,1)S(1)}, u32[]{:S(2)}, u32[]{:S(2)}) %collective-permute-start.4) | collective-permute-done | bytes 262176 | tf_op jit(solution)/shard_map/ppermute | solution.py:18
  24.6 0.8 %shard_map.67 = (bf16[256,512]{1,0:T(8,128)(2,1)S(1)}, bf16[256,512]{1,0:T(8,128)(2,1)S(1)}) custom-call(bf16[256,512]{1,0:T(8,128)(2,1)S(1)} %get-tuple-element.42.x0, bf16[256,512]{1,0:T(8,128)(2,1)S(1)} %collective-permute-done.2.x1, bf16[2,512,512]{2,1,0:T(8,128)(2,1)S(1)} %get-tuple-element.46.keep, bf16[2,512,512]{2,1,0:T(8,128)(2,1)S(1)} %get-tuple-element.47.cross), custom_call_target="tpu_custom_call" | custom-call | flops 17179869184 | bytes 33554432 | tf_op jit(solution)/shard_map/pallas_call | solution.py:41
  25.9 1.3 %collective-permute-start.11 = (bf16[256,512]{1,0:T(8,128)(2,1)S(1)}, bf16[256,512]{1,0:T(8,128)(2,1)S(1)}, u32[]{:S(2)}, u32[]{:S(2)}) collective-permute-start(bf16[256,512]{1,0:T(8,128)(2,1)S(1)} %collective-permute-done.9.refs_3_), channel_id=1, source_target_pairs={{0,16},{4,20},{8,24},{12,28},{16,0},{20,4},{24,8},{28,12},{1,17},{... | collective-permute-start | bytes 786440 | tf_op jit(solution)/shard_map/ppermute | solution.py:18
  27.3 2.1 %shard_map.68 = (bf16[256,512]{1,0:T(8,128)(2,1)S(1)}, bf16[256,512]{1,0:T(8,128)(2,1)S(1)}, bf16[256,512]{1,0:T(8,128)(2,1)S(1)}, bf16[256,512]{1,0:T(8,128)(2,1)S(1)}) custom-call(bf16[256,512]{1,0:T(8,128)(2,1)S(1)} %collective-permute-done.3.x2, bf16[256,512]{1,0:T(8,128)(2,1)S(1)} %collective-permute-done.4.x3, ...), custom_call_target="tpu_custom_call" | custom-call | flops 17179869184 | bytes 33554432 | tf_op jit(solution)/shard_map/pallas_call | solution.py:41
  29.7 2.7 %collective-permute-done.11.refs_5_ = bf16[256,512]{1,0:T(8,128)(2,1)S(1)} collective-permute-done((bf16[256,512]{1,0:T(8,128)(2,1)S(1)}, bf16[256,512]{1,0:T(8,128)(2,1)S(1)}, u32[]{:S(2)}, u32[]{:S(2)}) %collective-permute-start.11) | collective-permute-done | bytes 262176 | tf_op jit(solution)/shard_map/ppermute | solution.py:18
  32.6 2.0 %collective-permute-start.14 = (bf16[256,512]{1,0:T(8,128)(2,1)S(1)}, bf16[256,512]{1,0:T(8,128)(2,1)S(1)}, u32[]{:S(2)}, u32[]{:S(2)}) collective-permute-start(bf16[256,512]{1,0:T(8,128)(2,1)S(1)} %get-tuple-element.62), channel_id=1, source_target_pairs={{0,8},{4,12},{8,0},{12,4},{16,24},{20,28},{24,16},{28,20},{1,9},{5... | collective-permute-start | bytes 786440 | tf_op jit(solution)/shard_map/ppermute | solution.py:18
  34.5 1.2 %collective-permute-start.13 = (bf16[256,512]{1,0:T(8,128)(2,1)S(1)}, bf16[256,512]{1,0:T(8,128)(2,1)S(1)}, u32[]{:S(2)}, u32[]{:S(2)}) collective-permute-start(bf16[256,512]{1,0:T(8,128)(2,1)S(1)} %get-tuple-element.61), channel_id=1, source_target_pairs={{0,16},{4,20},{8,24},{12,28},{16,0},{20,4},{24,8},{28,12},{1,17},{... | collective-permute-start | bytes 786440 | tf_op jit(solution)/shard_map/ppermute | solution.py:18
  36.1 2.3 %shard_map.70.rest_2_ = bf16[1024,512]{1,0:T(8,128)(2,1)} custom-call(s32[1]{0:T(128)} %bitcast.me, s32[1]{0:T(128)} %bitcast.1.z, s32[8,128]{1,0:T(8,128)S(1)} %bitcast.3, bf16[256,512]{1,0:T(8,128)(2,1)S(1)} %get-tuple-element.54.x, bf16[512,512]{1,0:T(8,128)(2,1)S(1)} %get-tuple-element.34.own, bf16[512,512]{1,0:T(8,128)(2,1)S(1)} %collective-permute-done.1.beside, ...), custom_call_target="tpu_custom_call" | custom-call | flops 1073741824 | bytes 2097152 | tf_op jit(solution)/shard_map/pallas_call | solution.py:41
  38.4 3.3 %collective-permute-done.14.x = bf16[256,512]{1,0:T(8,128)(2,1)S(1)} collective-permute-done((bf16[256,512]{1,0:T(8,128)(2,1)S(1)}, bf16[256,512]{1,0:T(8,128)(2,1)S(1)}, u32[]{:S(2)}, u32[]{:S(2)}) %collective-permute-start.14) | collective-permute-done | bytes 262176 | tf_op jit(solution)/shard_map/ppermute | solution.py:18
  41.7 2.3 %shard_map.71.rest_2_ = bf16[1024,512]{1,0:T(8,128)(2,1)} custom-call(s32[1]{0:T(128)} %bitcast.me, s32[1]{0:T(128)} %bitcast.1.z, s32[8,128]{1,0:T(8,128)S(1)} %bitcast.4, bf16[256,512]{1,0:T(8,128)(2,1)S(1)} %collective-permute-done.14.x, bf16[512,512]{1,0:T(8,128)(2,1)S(1)} %get-tuple-element.34.own, ...), custom_call_target="tpu_custom_call", output_to_operand_aliasing={{}: (8, {})} | custom-call | flops 1073741824 | bytes 2097152 | tf_op jit(solution)/shard_map/pallas_call | solution.py:41
  44.0 4.5 %collective-permute-done.13.x = bf16[256,512]{1,0:T(8,128)(2,1)S(1)} collective-permute-done((bf16[256,512]{1,0:T(8,128)(2,1)S(1)}, bf16[256,512]{1,0:T(8,128)(2,1)S(1)}, u32[]{:S(2)}, u32[]{:S(2)}) %collective-permute-start.13) | collective-permute-done | bytes 262176 | tf_op jit(solution)/shard_map/ppermute | solution.py:18
  48.5 2.3 %shard_map.72.rest_2_ = bf16[1024,512]{1,0:T(8,128)(2,1)} custom-call(s32[1]{0:T(128)} %bitcast.me, s32[1]{0:T(128)} %bitcast.1.z, s32[8,128]{1,0:T(8,128)S(1)} %bitcast.5, bf16[256,512]{1,0:T(8,128)(2,1)S(1)} %collective-permute-done.13.x, bf16[512,512]{1,0:T(8,128)(2,1)S(1)} %get-tuple-element.34.own, ...), custom_call_target="tpu_custom_call", output_to_operand_aliasing={{}: (8, {})} | custom-call | flops 1073741824 | bytes 2097152 | tf_op jit(solution)/shard_map/pallas_call | solution.py:41
  50.8 2.3 %shard_map.73 = bf16[1024,512]{1,0:T(8,128)(2,1)} custom-call(s32[1]{0:T(128)} %bitcast.me, s32[1]{0:T(128)} %bitcast.1.z, s32[8,128]{1,0:T(8,128)S(1)} %bitcast.6, bf16[256,512]{1,0:T(8,128)(2,1)S(1)} %collective-permute-done.5.x, bf16[512,512]{1,0:T(8,128)(2,1)S(1)} %get-tuple-element.34.own, ...), custom_call_target="tpu_custom_call", output_to_operand_aliasing={{}: (8, {})} | custom-call | flops 1073741824 | bytes 2097152 | tf_op jit(solution)/shard_map/pallas_call | solution.py:41
  (18 shorter events, 3.1 us)
Async XLA Ops:
  0.0 6.3 %collective-permute-start = (bf16[1024,512]{1,0:T(8,128)(2,1)}, bf16[1024,512]{1,0:T(8,128)(2,1)S(1)}, u32[]{:S(2)}, u32[]{:S(2)}) collective-permute-start(bf16[1024,512]{1,0:T(8,128)(2,1)} %interface.1), channel_id=1, source_target_pairs={{0,4},{4,0},{8,12},{12,8},{16,20},{20,16},{24,28},{28,24},{1,5},{5... | collective-permute-start | bytes 3145736 | tf_op jit(solution)/shard_map/ppermute | solution.py:18
  1.7 4.6 %collective-permute-start.1 = (bf16[512,512]{1,0:T(8,128)(2,1)S(1)}, bf16[512,512]{1,0:T(8,128)(2,1)S(1)}, u32[]{:S(2)}, u32[]{:S(2)}) collective-permute-start(bf16[512,512]{1,0:T(8,128)(2,1)S(1)} %get-tuple-element.34.own), channel_id=1, source_target_pairs={{0,4},{4,0},{8,12},{12,8},{16,20},{20,16},{24,28},{28,24},{1,5},{5... | collective-permute-start | bytes 1572872 | tf_op jit(solution)/shard_map/ppermute | solution.py:18
  1.9 11.5 %collective-permute-start.7 = (bf16[256,512]{1,0:T(8,128)(2,1)S(1)}, bf16[256,512]{1,0:T(8,128)(2,1)S(1)}, u32[]{:S(2)}, u32[]{:S(2)}) collective-permute-start(bf16[256,512]{1,0:T(8,128)(2,1)S(1)} %get-tuple-element.51), channel_id=1, source_target_pairs={{0,16},{4,20},{8,24},{12,28},{16,0},{20,4},{24,8},{28,12},{1,17},{... | collective-permute-start | bytes 786440 | tf_op jit(solution)/shard_map/ppermute | solution.py:18
  4.8 8.8 %collective-permute-start.6 = (bf16[256,512]{1,0:T(8,128)(2,1)S(1)}, bf16[256,512]{1,0:T(8,128)(2,1)S(1)}, u32[]{:S(2)}, u32[]{:S(2)}) collective-permute-start(bf16[256,512]{1,0:T(8,128)(2,1)S(1)} %get-tuple-element.51), channel_id=1, source_target_pairs={{0,8},{4,12},{8,0},{12,4},{16,24},{20,28},{24,16},{28,20},{1,9},{5... | collective-permute-start | bytes 786440 | tf_op jit(solution)/shard_map/ppermute | solution.py:18
  9.8 9.5 %collective-permute-start.2 = (bf16[256,512]{1,0:T(8,128)(2,1)S(1)}, bf16[256,512]{1,0:T(8,128)(2,1)S(1)}, u32[]{:S(2)}, u32[]{:S(2)}) collective-permute-start(bf16[256,512]{1,0:T(8,128)(2,1)S(1)} %get-tuple-element.37), channel_id=1, source_target_pairs={{0,8},{4,12},{8,0},{12,4},{16,24},{20,28},{24,16},{28,20},{1,9},{5... | collective-permute-start | bytes 786440 | tf_op jit(solution)/shard_map/ppermute | solution.py:18
  10.4 10.5 %collective-permute-start.3 = (bf16[256,512]{1,0:T(8,128)(2,1)S(1)}, bf16[256,512]{1,0:T(8,128)(2,1)S(1)}, u32[]{:S(2)}, u32[]{:S(2)}) collective-permute-start(bf16[256,512]{1,0:T(8,128)(2,1)S(1)} %get-tuple-element.38), channel_id=1, source_target_pairs={{0,16},{4,20},{8,24},{12,28},{16,0},{20,4},{24,8},{28,12},{1,17},{... | collective-permute-start | bytes 786440 | tf_op jit(solution)/shard_map/ppermute | solution.py:18
  11.4 13.2 %collective-permute-start.4 = (bf16[256,512]{1,0:T(8,128)(2,1)S(1)}, bf16[256,512]{1,0:T(8,128)(2,1)S(1)}, u32[]{:S(2)}, u32[]{:S(2)}) collective-permute-start(bf16[256,512]{1,0:T(8,128)(2,1)S(1)} %get-tuple-element.39), channel_id=1, source_target_pairs={{0,24},{4,28},{8,16},{12,20},{16,8},{20,12},{24,0},{28,4},{1,25},{... | collective-permute-start | bytes 786440 | tf_op jit(solution)/shard_map/ppermute | solution.py:18
  13.7 15.6 %collective-permute-start.10 = (bf16[256,512]{1,0:T(8,128)(2,1)S(1)}, bf16[256,512]{1,0:T(8,128)(2,1)S(1)}, u32[]{:S(2)}, u32[]{:S(2)}) collective-permute-start(bf16[256,512]{1,0:T(8,128)(2,1)S(1)} %collective-permute-done.7.refs_1_), channel_id=1, source_target_pairs={{0,1},{1,0},{2,3},{3,2},{4,5},{5,4},{6,7},{7,6},{8,9},{9,8},{10,11... | collective-permute-start | bytes 786440 | tf_op jit(solution)/shard_map/ppermute | solution.py:18
  15.3 14.4 %collective-permute-start.8 = (bf16[256,512]{1,0:T(8,128)(2,1)S(1)}, bf16[256,512]{1,0:T(8,128)(2,1)S(1)}, u32[]{:S(2)}, u32[]{:S(2)}) collective-permute-start(bf16[256,512]{1,0:T(8,128)(2,1)S(1)} %collective-permute-done.7.refs_1_), channel_id=1, source_target_pairs={{0,8},{4,12},{8,0},{12,4},{16,24},{20,28},{24,16},{28,20},{1,9},{5... | collective-permute-start | bytes 786440 | tf_op jit(solution)/shard_map/ppermute | solution.py:18
  19.3 6.7 %collective-permute-start.9 = (bf16[256,512]{1,0:T(8,128)(2,1)S(1)}, bf16[256,512]{1,0:T(8,128)(2,1)S(1)}, u32[]{:S(2)}, u32[]{:S(2)}) collective-permute-start(bf16[256,512]{1,0:T(8,128)(2,1)S(1)} %collective-permute-done.6.refs_0_), channel_id=1, source_target_pairs={{0,1},{1,0},{2,3},{3,2},{4,5},{5,4},{6,7},{7,6},{8,9},{9,8},{10,11... | collective-permute-start | bytes 786440 | tf_op jit(solution)/shard_map/ppermute | solution.py:18
  25.9 6.4 %collective-permute-start.11 = (bf16[256,512]{1,0:T(8,128)(2,1)S(1)}, bf16[256,512]{1,0:T(8,128)(2,1)S(1)}, u32[]{:S(2)}, u32[]{:S(2)}) collective-permute-start(bf16[256,512]{1,0:T(8,128)(2,1)S(1)} %collective-permute-done.9.refs_3_), channel_id=1, source_target_pairs={{0,16},{4,20},{8,24},{12,28},{16,0},{20,4},{24,8},{28,12},{1,17},{... | collective-permute-start | bytes 786440 | tf_op jit(solution)/shard_map/ppermute | solution.py:18
  32.4 3.7 %copy-start = (s32[1024,1]{0,1:T(1,128)S(1)}, s32[1024,1]{0,1:T(1,128)}, u32[]{:S(2)}) copy-start(s32[1024,1]{0,1:T(1,128)} %param.7) | copy-start | bytes 12292
  32.5 3.6 %collective-permute-start.12 = (bf16[1536,512]{1,0:T(8,128)(2,1)S(1)}, bf16[1536,512]{1,0:T(8,128)(2,1)S(1)}, u32[]{:S(2)}, u32[]{:S(2)}) collective-permute-start(bf16[1536,512]{1,0:T(8,128)(2,1)S(1)} %shard_map.69.rest_0_), channel_id=1, source_target_pairs={{0,4},{4,0},{8,12},{12,8},{16,20},{20,16},{24,28},{28,24},{1,5},{5... | collective-permute-start | bytes 4718600 | tf_op jit(solution)/shard_map/ppermute | solution.py:18
  32.6 9.2 %collective-permute-start.14 = (bf16[256,512]{1,0:T(8,128)(2,1)S(1)}, bf16[256,512]{1,0:T(8,128)(2,1)S(1)}, u32[]{:S(2)}, u32[]{:S(2)}) collective-permute-start(bf16[256,512]{1,0:T(8,128)(2,1)S(1)} %get-tuple-element.62), channel_id=1, source_target_pairs={{0,8},{4,12},{8,0},{12,4},{16,24},{20,28},{24,16},{28,20},{1,9},{5... | collective-permute-start | bytes 786440 | tf_op jit(solution)/shard_map/ppermute | solution.py:18
  34.5 14.0 %collective-permute-start.13 = (bf16[256,512]{1,0:T(8,128)(2,1)S(1)}, bf16[256,512]{1,0:T(8,128)(2,1)S(1)}, u32[]{:S(2)}, u32[]{:S(2)}) collective-permute-start(bf16[256,512]{1,0:T(8,128)(2,1)S(1)} %get-tuple-element.61), channel_id=1, source_target_pairs={{0,16},{4,20},{8,24},{12,28},{16,0},{20,4},{24,8},{28,12},{1,17},{... | collective-permute-start | bytes 786440 | tf_op jit(solution)/shard_map/ppermute | solution.py:18
  35.7 15.1 %collective-permute-start.5 = (bf16[256,512]{1,0:T(8,128)(2,1)S(1)}, bf16[256,512]{1,0:T(8,128)(2,1)S(1)}, u32[]{:S(2)}, u32[]{:S(2)}) collective-permute-start(bf16[256,512]{1,0:T(8,128)(2,1)S(1)} %get-tuple-element.50), channel_id=1, source_target_pairs={{0,24},{4,28},{8,16},{12,20},{16,8},{20,12},{24,0},{28,4},{1,25},{... | collective-permute-start | bytes 786440 | tf_op jit(solution)/shard_map/ppermute | solution.py:18

commit v3 on v2

--- a/solution.py
+++ b/solution.py
@@ -8,6 +8,7 @@
 
 BS = 64
 EPSILON = 1e-06
+PLACES = (0, 1), (2, 4), (5, 3), (6, 7)
 VMEM = pl.BlockSpec(memory_space=pltpu.VMEM)
 SMEM = pl.BlockSpec(memory_space=pltpu.SMEM)
 HBM = pl.BlockSpec(memory_space=pltpu.HBM)
@@ -89,7 +90,7 @@
     outs[0][...] = mixed(y0[...], y2, keep[1], cross[1])
 
 
-def masked_coupling(z, coupling, pattern, out, part, held, shown, sems):
+def masked_coupling(z, coupling, pattern, part, rest, held, shown, sems):
     loads = [pltpu.make_async_copy(pattern, shown, sems.at[0]), pltpu.make_async_copy(coupling, held, sems.at[1])]
     for load in loads:
         load.start()
@@ -100,8 +101,9 @@
             [jnp.full((BS, BS), shown[0, i, j], jnp.int32) for j in range(shown.shape[2])], axis=1
         )
         block = held[0, i * BS : (i + 1) * BS, :]
-        out[i * BS : (i + 1) * BS, :] = jnp.where(row != 0, block, jnp.zeros_like(block))
-    part[...] = out[half_rows(z, 0, part.shape[0]), :]
+        held[0, i * BS : (i + 1) * BS, :] = jnp.where(row != 0, block, jnp.zeros_like(block))
+    part[...] = held[0, half_rows(z, 0, part.shape[0]), :]
+    rest[...] = held[0, half_rows(z, 1, part.shape[0]), :]
 
 
 def half_rows(z, other, depth):
@@ -116,36 +118,36 @@
         at += part.shape[0]
 
 
-def couple(m, me, z, owners, x, own, beside, *rest):
-    packs, (out, held, sems) = rest[:2], rest[-3:]
-    size, features = x.shape
+def couple(blocks, me, z, owners, *rest):
+    n_block = len(blocks)
+    xs, packs, (out, held, sems) = rest[:n_block], rest[n_block : n_block + 2], rest[-3:]
+    size, features = xs[0].shape
     depth = features // 2
-    rows = block_rows(me, m, size)
     lanes = owners.shape[1]
     groups = size // lanes
     diagonal = lax.broadcasted_iota(jnp.int32, (lanes, lanes), 0) == lax.broadcasted_iota(jnp.int32, (lanes, lanes), 1)
-    named = owners[pl.ds((((me[0] >> 1) & 3) ^ m) * groups, groups), :] ^ me[0]
-    relative = jnp.concatenate(
-        [jnp.sum(jnp.where(diagonal, named[i : i + 1, :], 0), axis=1, keepdims=True) for i in range(groups)], axis=0
-    )
+    columns_of = []
+    for m in blocks:
+        named = owners[pl.ds((((me[0] >> 1) & 3) ^ m) * groups, groups), :] ^ me[0]
+        columns_of += [jnp.sum(jnp.where(diagonal, named[i : i + 1, :], 0), axis=1, keepdims=True) for i in range(groups)]
+    relative = jnp.concatenate(columns_of, axis=0)
     parts = [half_rows(z, other, depth) for other in range(2)]
-    values = [x[:, part] for part in parts]
+    values = [jnp.concatenate([x[:, part] for x in xs], axis=0) for part in parts]
     chosen = [[jnp.where(relative == r, value, jnp.zeros_like(value)) for value in values] for r in range(8)]
     copies = []
     for n in range(2):
         columns = slice(n * depth, (n + 1) * depth)
-        total = jnp.zeros((size, depth), jnp.float32)
+        total = jnp.zeros((n_block * size, depth), jnp.float32)
         for r in range(8):
             for h in range(2):
-                if r < 2:
-                    piece = (own, beside)[r][parts[h], columns]
-                else:
-                    at = (r // 2 - 1 + 3 * h) * depth
-                    piece = packs[r % 2][at : at + depth, columns]
+                at = PLACES[r // 2][h] * depth
+                piece = packs[r % 2][at : at + depth, columns]
                 total += jnp.dot(chosen[r][h], piece, preferred_element_type=jnp.float32)
         held[:, columns] = total.astype(jnp.bfloat16)
-        copies.append(pltpu.make_async_copy(held.at[:, columns], out.at[rows, columns], sems.at[n]))
-        copies[-1].start()
+        for i, m in enumerate(blocks):
+            to = out.at[block_rows(me, m, size), columns]
+            copies.append(pltpu.make_async_copy(held.at[i * size : (i + 1) * size, columns], to, sems.at[n, i]))
+            copies[-1].start()
     for copy in copies:
         copy.wait()
 
@@ -197,9 +199,9 @@
     weights = in_hbm(keep_proj), in_hbm(sibling_proj)
 
     sibling = swapped(interface, 1)
-    dense, mine = call(
+    mine, other = call(
         masked_coupling,
-        [matrix, array(depth, features)],
+        [array(depth, features)] * 2,
         1,
         [SMEM] + [HBM] * 2,
         z,
@@ -212,9 +214,7 @@
         ],
     )
     if few:
-        near = swapped(mine, 2), swapped(mine, 4)
-        beside = swapped(dense, 1)
-        sibling = after(sibling, beside)
+        near = swapped(mine, 2), swapped(other, 4)
     sent = call(
         first_level,
         [part] * 4,
@@ -238,9 +238,10 @@
         scratch=[pltpu.SemaphoreType.DMA((2,))],
     )
     if few:
-        x_mine, y_mine, _ = together(*near, sent[0])
-        x_other, y_other = swapped(x_mine, 1, "blk"), swapped(y_mine, 1, "blk")
-        d_mine, d_other = swapped(y_mine, 2), swapped(x_other, 4)
+        x_mine, y_other, _ = together(*near, sent[0])
+        (pack_near,) = call(packed, [array(2 * depth, features)], 1, [VMEM] * 2, x_mine, y_other)
+        pack_far = swapped(pack_near, 1, "blk")
+        d_mine, d_other = swapped(after(x_mine, x[1]), 4), swapped(after(y_other, x[1]), 2)
         x = together(*x)
     y0, y1 = call(second_level, [part] * 2, (1 << 34), [VMEM] * 4, x[0], x[1], *weights)
     done = call(third_level, [part] * 4, (1 << 34), [VMEM] * 6, x[2], x[3], y0, y1, *weights)
@@ -249,26 +250,27 @@
         current = jnp.zeros((rows, features), jnp.bfloat16)
         for m in range(4):
             current = lax.dynamic_update_slice_in_dim(current, back[m], ((me[0] // 2 % 4) ^ m) * quarter, 0)
-        return routed(current, owners, dense)
-    pieces = [x_mine, y_mine, d_mine, x_other, y_other, d_other]
-    (pack,) = call(packed, [array(6 * depth, features)], 1, [VMEM] * 6, *together(*pieces, done[0])[:6])
-    matrices = [dense, beside, pack, swapped(pack, 1)]
+        return routed(current, owners, jnp.where(z[0] % 2 == 0, jnp.concatenate([mine, other]), jnp.concatenate([other, mine])))
+    pieces = [mine, other, pack_near, pack_far, d_mine, d_other]
+    (pack,) = call(packed, [array(8 * depth, features)], 1, [VMEM] * 6, *together(*pieces, done[0])[:6])
+    matrices = [pack, swapped(pack, 1)]
     out = None
-    for m in range(4):
+    for blocks in ((0, 1), (2, 3)):
         extra = [] if out is None else [out]
+        n_block = len(blocks)
         (out,) = call(
-            functools.partial(couple, m),
+            functools.partial(couple, blocks),
             [whole],
-            8 * block_flops,
-            [SMEM] * 2 + [VMEM] * (2 + len(matrices)) + [HBM] * len(extra),
+            8 * n_block * block_flops,
+            [SMEM] * 2 + [VMEM] * (1 + n_block + len(matrices)) + [HBM] * len(extra),
             me,
             z,
             owners.reshape(-1, 128),
-            back[m],
+            *(back[m] for m in blocks),
             *matrices,
             *extra,
-            scratch=[pltpu.VMEM((quarter, features), jnp.bfloat16), pltpu.SemaphoreType.DMA((2,))],
-            aliases={4 + len(matrices): 0} if extra else None,
+            scratch=[pltpu.VMEM((n_block * quarter, features), jnp.bfloat16), pltpu.SemaphoreType.DMA((2, n_block))],
+            aliases={3 + n_block + len(matrices): 0} if extra else None,
         )
     return out
 

time: 53.3 us -> 48.8 us (0.916)
  starting transfers between devices: 18.5 us -> 15.4 us
  Pallas kernels: 18.4 us -> 16.3 us
  waiting for transfers between devices: 16.1 us -> 16.8 us
    ppermute x15 -> x13, starting transfers between devices: 18.5 us -> 15.4 us  [swapped(): return lax.ppermute(value, axis, pairs)]
    pallas_call x10 -> x9, Pallas kernels: 18.4 us -> 16.3 us  [call(): pl.pallas_call(body, out_shape=[shape for shape, _ in outs], in_specs=spe...]
    ppermute x15 -> x13, waiting for transfers between devices: 16.1 us -> 16.8 us  [swapped(): return lax.ppermute(value, axis, pairs)]
  transfers between devices with their start and end apart: 15 -> 13, of which waited for: 8 -> 8; matrix products, arithmetic and copies ran while one was open for 0% -> 0% of each run, Pallas kernels for 30% -> 26%
where the time goes in v3:
time: 48.8 us; the launch traced here: 48.6 us
  waiting for transfers between devices  16.8 us (34%)
  Pallas kernels  16.3 us (33%)
  starting transfers between devices  15.4 us (32%)
    ppermute x13, waiting for transfers between devices, swapped(): return lax.ppermute(value, axis, pairs)  16.8 us
    pallas_call x9, Pallas kernels, call(): pl.pallas_call(body, out_shape=[shape for shape, _ in outs], in_specs=spe...  16.3 us
    ppermute x13, starting transfers between devices, swapped(): return lax.ppermute(value, axis, pairs)  15.4 us
  transfers between devices with their start and end apart: 13, of which 8 were waited for; matrix products, arithmetic and copies ran while one was open for 0% of the time, Pallas kernels for 26%

profile of v3, /device:TPU:0, one launch (start us, length us, event | category | flops | bytes accessed | tf_op | source)
XLA Modules:
  0.0 48.6 jit_solution(2680876054698202794)
XLA Ops:
  0.5 1.3 %shard_map.68 = (bf16[256,512]{1,0:T(8,128)(2,1)S(1)}, bf16[256,512]{1,0:T(8,128)(2,1)S(1)}) custom-call(s32[1]{0:T(128)} %bitcast.1.z, bf16[1,512,512]{2,1,0:T(8,128)(2,1)} %coupling.1, s32[1,8,8]{2,1,0:T(8,128)} %pattern.1), custom_call_target="tpu_custom_call" | custom-call | flops 1 | tf_op jit(solution)/shard_map/pallas_call | solution.py:42
  1.8 2.6 %collective-permute-start.6 = (bf16[256,512]{1,0:T(8,128)(2,1)S(1)}, bf16[256,512]{1,0:T(8,128)(2,1)S(1)}, u32[]{:S(2)}, u32[]{:S(2)}) collective-permute-start(bf16[256,512]{1,0:T(8,128)(2,1)S(1)} %get-tuple-element.58.refs_0_), channel_id=1, source_target_pairs={{0,8},{4,12},{8,0},{12,4},{16,24},{20,28},{24,16},{28,20},{1,9},{5... | collective-permute-start | bytes 786440 | tf_op jit(solution)/shard_map/ppermute | solution.py:19
  4.3 1.5 %collective-permute-start.7 = (bf16[256,512]{1,0:T(8,128)(2,1)S(1)}, bf16[256,512]{1,0:T(8,128)(2,1)S(1)}, u32[]{:S(2)}, u32[]{:S(2)}) collective-permute-start(bf16[256,512]{1,0:T(8,128)(2,1)S(1)} %get-tuple-element.59.refs_1_), channel_id=1, source_target_pairs={{0,16},{4,20},{8,24},{12,28},{16,0},{20,4},{24,8},{28,12},{1,17},{... | collective-permute-start | bytes 786440 | tf_op jit(solution)/shard_map/ppermute | solution.py:19
  5.8 3.4 %shard_map.64 = (bf16[256,512]{1,0:T(8,128)(2,1)S(1)}, bf16[256,512]{1,0:T(8,128)(2,1)S(1)}, bf16[256,512]{1,0:T(8,128)(2,1)S(1)}, bf16[256,512]{1,0:T(8,128)(2,1)S(1)}) custom-call(s32[1]{0:T(128)} %bitcast.me, bf16[1024,512]{1,0:T(8,128)(2,1)S(1)} %collective-permute-done.sibling, bf16[1024,512]{1,0:T(8,128)(2,1)} %interface.1, bf16[3,512,512]{2,1,0:T(8,128)(2,1)} %keep.2, ...), custom_call_target="tpu_custom_call" | custom-call | flops 536870912 | bytes 1048576 | tf_op jit(solution)/shard_map/pallas_call | solution.py:42
  9.3 0.6 %collective-permute-start.1 = (bf16[256,512]{1,0:T(8,128)(2,1)S(1)}, bf16[256,512]{1,0:T(8,128)(2,1)S(1)}, u32[]{:S(2)}, u32[]{:S(2)}) collective-permute-start(bf16[256,512]{1,0:T(8,128)(2,1)S(1)} %get-tuple-element.36), channel_id=1, source_target_pairs={{0,8},{4,12},{8,0},{12,4},{16,24},{20,28},{24,16},{28,20},{1,9},{5... | collective-permute-start | bytes 786440 | tf_op jit(solution)/shard_map/ppermute | solution.py:19
  9.9 1.0 %collective-permute-start.2 = (bf16[256,512]{1,0:T(8,128)(2,1)S(1)}, bf16[256,512]{1,0:T(8,128)(2,1)S(1)}, u32[]{:S(2)}, u32[]{:S(2)}) collective-permute-start(bf16[256,512]{1,0:T(8,128)(2,1)S(1)} %get-tuple-element.37), channel_id=1, source_target_pairs={{0,16},{4,20},{8,24},{12,28},{16,0},{20,4},{24,8},{28,12},{1,17},{... | collective-permute-start | bytes 786440 | tf_op jit(solution)/shard_map/ppermute | solution.py:19
  10.8 2.0 %collective-permute-start.3 = (bf16[256,512]{1,0:T(8,128)(2,1)S(1)}, bf16[256,512]{1,0:T(8,128)(2,1)S(1)}, u32[]{:S(2)}, u32[]{:S(2)}) collective-permute-start(bf16[256,512]{1,0:T(8,128)(2,1)S(1)} %get-tuple-element.38), channel_id=1, source_target_pairs={{0,24},{4,28},{8,16},{12,20},{16,8},{20,12},{24,0},{28,4},{1,25},{... | collective-permute-start | bytes 786440 | tf_op jit(solution)/shard_map/ppermute | solution.py:19
  13.3 1.6 %collective-permute-start.8 = (bf16[512,512]{1,0:T(8,128)(2,1)S(1)}, bf16[512,512]{1,0:T(8,128)(2,1)S(1)}, u32[]{:S(2)}, u32[]{:S(2)}) collective-permute-start(bf16[512,512]{1,0:T(8,128)(2,1)S(1)} %shard_map.69.refs_2_), channel_id=1, source_target_pairs={{0,1},{1,0},{2,3},{3,2},{4,5},{5,4},{6,7},{7,6},{8,9},{9,8},{10,11... | collective-permute-start | bytes 1572872 | tf_op jit(solution)/shard_map/ppermute | solution.py:19
  15.0 1.6 %shard_map.65 = (bf16[2,512,512]{2,1,0:T(8,128)(2,1)S(1)}, bf16[2,512,512]{2,1,0:T(8,128)(2,1)S(1)}) custom-call(bf16[3,512,512]{2,1,0:T(8,128)(2,1)} %keep.2, bf16[3,512,512]{2,1,0:T(8,128)(2,1)} %cross.2), custom_call_target="tpu_custom_call" | custom-call | flops 1 | tf_op jit(solution)/shard_map/pallas_call | solution.py:42
  16.6 2.0 %collective-permute-done.1.x1 = bf16[256,512]{1,0:T(8,128)(2,1)S(1)} collective-permute-done((bf16[256,512]{1,0:T(8,128)(2,1)S(1)}, bf16[256,512]{1,0:T(8,128)(2,1)S(1)}, u32[]{:S(2)}, u32[]{:S(2)}) %collective-permute-start.1) | collective-permute-done | bytes 262176 | tf_op jit(solution)/shard_map/ppermute | solution.py:19
  18.5 0.6 %collective-permute-start.9 = (bf16[256,512]{1,0:T(8,128)(2,1)S(1)}, bf16[256,512]{1,0:T(8,128)(2,1)S(1)}, u32[]{:S(2)}, u32[]{:S(2)}) collective-permute-start(bf16[256,512]{1,0:T(8,128)(2,1)S(1)} %collective-permute-done.6.refs_0_), channel_id=1, source_target_pairs={{0,16},{4,20},{8,24},{12,28},{16,0},{20,4},{24,8},{28,12},{1,17},{... | collective-permute-start | bytes 786440 | tf_op jit(solution)/shard_map/ppermute | solution.py:19
  19.1 1.5 %collective-permute-start.10 = (bf16[256,512]{1,0:T(8,128)(2,1)S(1)}, bf16[256,512]{1,0:T(8,128)(2,1)S(1)}, u32[]{:S(2)}, u32[]{:S(2)}) collective-permute-start(bf16[256,512]{1,0:T(8,128)(2,1)S(1)} %collective-permute-done.7.refs_1_), channel_id=1, source_target_pairs={{0,8},{4,12},{8,0},{12,4},{16,24},{20,28},{24,16},{28,20},{1,9},{5... | collective-permute-start | bytes 786440 | tf_op jit(solution)/shard_map/ppermute | solution.py:19
  20.6 3.4 %collective-permute-done.2.x2 = bf16[256,512]{1,0:T(8,128)(2,1)S(1)} collective-permute-done((bf16[256,512]{1,0:T(8,128)(2,1)S(1)}, bf16[256,512]{1,0:T(8,128)(2,1)S(1)}, u32[]{:S(2)}, u32[]{:S(2)}) %collective-permute-start.2) | collective-permute-done | bytes 262176 | tf_op jit(solution)/shard_map/ppermute | solution.py:19
  24.2 0.8 %shard_map.66 = (bf16[256,512]{1,0:T(8,128)(2,1)S(1)}, bf16[256,512]{1,0:T(8,128)(2,1)S(1)}) custom-call(bf16[256,512]{1,0:T(8,128)(2,1)S(1)} %get-tuple-element.41.x0, bf16[256,512]{1,0:T(8,128)(2,1)S(1)} %collective-permute-done.1.x1, bf16[2,512,512]{2,1,0:T(8,128)(2,1)S(1)} %get-tuple-element.45.keep, bf16[2,512,512]{2,1,0:T(8,128)(2,1)S(1)} %get-tuple-element.46.cross), custom_call_target="tpu_custom_call" | custom-call | flops 17179869184 | bytes 33554432 | tf_op jit(solution)/shard_map/pallas_call | solution.py:42
  25.0 2.1 %shard_map.67 = (bf16[256,512]{1,0:T(8,128)(2,1)S(1)}, bf16[256,512]{1,0:T(8,128)(2,1)S(1)}, bf16[256,512]{1,0:T(8,128)(2,1)S(1)}, bf16[256,512]{1,0:T(8,128)(2,1)S(1)}) custom-call(bf16[256,512]{1,0:T(8,128)(2,1)S(1)} %collective-permute-done.2.x2, bf16[256,512]{1,0:T(8,128)(2,1)S(1)} %collective-permute-done.3.x3, ...), custom_call_target="tpu_custom_call" | custom-call | flops 17179869184 | bytes 33554432 | tf_op jit(solution)/shard_map/pallas_call | solution.py:42
  27.0 2.6 %collective-permute-done.9.refs_4_ = bf16[256,512]{1,0:T(8,128)(2,1)S(1)} collective-permute-done((bf16[256,512]{1,0:T(8,128)(2,1)S(1)}, bf16[256,512]{1,0:T(8,128)(2,1)S(1)}, u32[]{:S(2)}, u32[]{:S(2)}) %collective-permute-start.9) | collective-permute-done | bytes 262176 | tf_op jit(solution)/shard_map/ppermute | solution.py:19
  29.8 1.3 %collective-permute-start.12 = (bf16[256,512]{1,0:T(8,128)(2,1)S(1)}, bf16[256,512]{1,0:T(8,128)(2,1)S(1)}, u32[]{:S(2)}, u32[]{:S(2)}) collective-permute-start(bf16[256,512]{1,0:T(8,128)(2,1)S(1)} %get-tuple-element.64), channel_id=1, source_target_pairs={{0,8},{4,12},{8,0},{12,4},{16,24},{20,28},{24,16},{28,20},{1,9},{5... | collective-permute-start | bytes 786440 | tf_op jit(solution)/shard_map/ppermute | solution.py:19
  31.1 0.8 %collective-permute-start.4 = (bf16[256,512]{1,0:T(8,128)(2,1)S(1)}, bf16[256,512]{1,0:T(8,128)(2,1)S(1)}, u32[]{:S(2)}, u32[]{:S(2)}) collective-permute-start(bf16[256,512]{1,0:T(8,128)(2,1)S(1)} %get-tuple-element.49), channel_id=1, source_target_pairs={{0,16},{4,20},{8,24},{12,28},{16,0},{20,4},{24,8},{28,12},{1,17},{... | collective-permute-start | bytes 786440 | tf_op jit(solution)/shard_map/ppermute | solution.py:19
  31.9 1.4 %collective-permute-start.5 = (bf16[256,512]{1,0:T(8,128)(2,1)S(1)}, bf16[256,512]{1,0:T(8,128)(2,1)S(1)}, u32[]{:S(2)}, u32[]{:S(2)}) collective-permute-start(bf16[256,512]{1,0:T(8,128)(2,1)S(1)} %get-tuple-element.50), channel_id=1, source_target_pairs={{0,24},{4,28},{8,16},{12,20},{16,8},{20,12},{24,0},{28,4},{1,25},{... | collective-permute-start | bytes 786440 | tf_op jit(solution)/shard_map/ppermute | solution.py:19
  33.4 5.6 %collective-permute-done.12.rest_1_ = bf16[256,512]{1,0:T(8,128)(2,1)S(1)} collective-permute-done((bf16[256,512]{1,0:T(8,128)(2,1)S(1)}, bf16[256,512]{1,0:T(8,128)(2,1)S(1)}, u32[]{:S(2)}, u32[]{:S(2)}) %collective-permute-start.12) | collective-permute-done | bytes 262176 | tf_op jit(solution)/shard_map/ppermute | solution.py:19
  39.0 3.5 %shard_map.71.rest_4_ = bf16[1024,512]{1,0:T(8,128)(2,1)} custom-call(s32[1]{0:T(128)} %bitcast.me, s32[1]{0:T(128)} %bitcast.1.z, s32[8,128]{1,0:T(8,128)S(1)} %bitcast.3, bf16[256,512]{1,0:T(8,128)(2,1)S(1)} %get-tuple-element.57.rest_0_, bf16[256,512]{1,0:T(8,128)(2,1)S(1)} %collective-permute-done.12.rest_1_, bf16[2048,512]{1,0:T(8,128)(2,1)S(1)} %shard_map.70.rest_2_, ...), custom_call_target="tpu_custom_call" | custom-call | flops 2147483648 | bytes 4194304 | tf_op jit(solution)/shard_map/pallas_call | solution.py:42
  42.5 1.0 %collective-permute-done.4.rest_0_ = bf16[256,512]{1,0:T(8,128)(2,1)S(1)} collective-permute-done((bf16[256,512]{1,0:T(8,128)(2,1)S(1)}, bf16[256,512]{1,0:T(8,128)(2,1)S(1)}, u32[]{:S(2)}, u32[]{:S(2)}) %collective-permute-start.4) | collective-permute-done | bytes 262176 | tf_op jit(solution)/shard_map/ppermute | solution.py:19
  43.5 1.6 %collective-permute-done.5.rest_1_ = bf16[256,512]{1,0:T(8,128)(2,1)S(1)} collective-permute-done((bf16[256,512]{1,0:T(8,128)(2,1)S(1)}, bf16[256,512]{1,0:T(8,128)(2,1)S(1)}, u32[]{:S(2)}, u32[]{:S(2)}) %collective-permute-start.5) | collective-permute-done | bytes 262176 | tf_op jit(solution)/shard_map/ppermute | solution.py:19
  45.1 3.5 %shard_map.72 = bf16[1024,512]{1,0:T(8,128)(2,1)} custom-call(s32[1]{0:T(128)} %bitcast.me, s32[1]{0:T(128)} %bitcast.1.z, s32[8,128]{1,0:T(8,128)S(1)} %bitcast.4, bf16[256,512]{1,0:T(8,128)(2,1)S(1)} %collective-permute-done.4.rest_0_, bf16[256,512]{1,0:T(8,128)(2,1)S(1)} %collective-permute-done.5.rest_1_, ...), custom_call_target="tpu_custom_call", output_to_operand_aliasing={{}: (7, {})} | custom-call | flops 2147483648 | bytes 4194304 | tf_op jit(solution)/shard_map/pallas_call | solution.py:42
  (13 shorter events, 1.4 us)
Async XLA Ops:
  0.0 5.8 %collective-permute-start = (bf16[1024,512]{1,0:T(8,128)(2,1)}, bf16[1024,512]{1,0:T(8,128)(2,1)S(1)}, u32[]{:S(2)}, u32[]{:S(2)}) collective-permute-start(bf16[1024,512]{1,0:T(8,128)(2,1)} %interface.1), channel_id=1, source_target_pairs={{0,4},{4,0},{8,12},{12,8},{16,20},{20,16},{24,28},{28,24},{1,5},{5... | collective-permute-start | bytes 3145736 | tf_op jit(solution)/shard_map/ppermute | solution.py:19
  1.8 11.1 %collective-permute-start.6 = (bf16[256,512]{1,0:T(8,128)(2,1)S(1)}, bf16[256,512]{1,0:T(8,128)(2,1)S(1)}, u32[]{:S(2)}, u32[]{:S(2)}) collective-permute-start(bf16[256,512]{1,0:T(8,128)(2,1)S(1)} %get-tuple-element.58.refs_0_), channel_id=1, source_target_pairs={{0,8},{4,12},{8,0},{12,4},{16,24},{20,28},{24,16},{28,20},{1,9},{5... | collective-permute-start | bytes 786440 | tf_op jit(solution)/shard_map/ppermute | solution.py:19
  4.3 9.0 %collective-permute-start.7 = (bf16[256,512]{1,0:T(8,128)(2,1)S(1)}, bf16[256,512]{1,0:T(8,128)(2,1)S(1)}, u32[]{:S(2)}, u32[]{:S(2)}) collective-permute-start(bf16[256,512]{1,0:T(8,128)(2,1)S(1)} %get-tuple-element.59.refs_1_), channel_id=1, source_target_pairs={{0,16},{4,20},{8,24},{12,28},{16,0},{20,4},{24,8},{28,12},{1,17},{... | collective-permute-start | bytes 786440 | tf_op jit(solution)/shard_map/ppermute | solution.py:19
  9.3 9.2 %collective-permute-start.1 = (bf16[256,512]{1,0:T(8,128)(2,1)S(1)}, bf16[256,512]{1,0:T(8,128)(2,1)S(1)}, u32[]{:S(2)}, u32[]{:S(2)}) collective-permute-start(bf16[256,512]{1,0:T(8,128)(2,1)S(1)} %get-tuple-element.36), channel_id=1, source_target_pairs={{0,8},{4,12},{8,0},{12,4},{16,24},{20,28},{24,16},{28,20},{1,9},{5... | collective-permute-start | bytes 786440 | tf_op jit(solution)/shard_map/ppermute | solution.py:19
  9.9 14.1 %collective-permute-start.2 = (bf16[256,512]{1,0:T(8,128)(2,1)S(1)}, bf16[256,512]{1,0:T(8,128)(2,1)S(1)}, u32[]{:S(2)}, u32[]{:S(2)}) collective-permute-start(bf16[256,512]{1,0:T(8,128)(2,1)S(1)} %get-tuple-element.37), channel_id=1, source_target_pairs={{0,16},{4,20},{8,24},{12,28},{16,0},{20,4},{24,8},{28,12},{1,17},{... | collective-permute-start | bytes 786440 | tf_op jit(solution)/shard_map/ppermute | solution.py:19
  10.8 13.3 %collective-permute-start.3 = (bf16[256,512]{1,0:T(8,128)(2,1)S(1)}, bf16[256,512]{1,0:T(8,128)(2,1)S(1)}, u32[]{:S(2)}, u32[]{:S(2)}) collective-permute-start(bf16[256,512]{1,0:T(8,128)(2,1)S(1)} %get-tuple-element.38), channel_id=1, source_target_pairs={{0,24},{4,28},{8,16},{12,20},{16,8},{20,12},{24,0},{28,4},{1,25},{... | collective-permute-start | bytes 786440 | tf_op jit(solution)/shard_map/ppermute | solution.py:19
  13.3 13.7 %collective-permute-start.8 = (bf16[512,512]{1,0:T(8,128)(2,1)S(1)}, bf16[512,512]{1,0:T(8,128)(2,1)S(1)}, u32[]{:S(2)}, u32[]{:S(2)}) collective-permute-start(bf16[512,512]{1,0:T(8,128)(2,1)S(1)} %shard_map.69.refs_2_), channel_id=1, source_target_pairs={{0,1},{1,0},{2,3},{3,2},{4,5},{5,4},{6,7},{7,6},{8,9},{9,8},{10,11... | collective-permute-start | bytes 1572872 | tf_op jit(solution)/shard_map/ppermute | solution.py:19
  18.5 11.1 %collective-permute-start.9 = (bf16[256,512]{1,0:T(8,128)(2,1)S(1)}, bf16[256,512]{1,0:T(8,128)(2,1)S(1)}, u32[]{:S(2)}, u32[]{:S(2)}) collective-permute-start(bf16[256,512]{1,0:T(8,128)(2,1)S(1)} %collective-permute-done.6.refs_0_), channel_id=1, source_target_pairs={{0,16},{4,20},{8,24},{12,28},{16,0},{20,4},{24,8},{28,12},{1,17},{... | collective-permute-start | bytes 786440 | tf_op jit(solution)/shard_map/ppermute | solution.py:19
  19.1 10.5 %collective-permute-start.10 = (bf16[256,512]{1,0:T(8,128)(2,1)S(1)}, bf16[256,512]{1,0:T(8,128)(2,1)S(1)}, u32[]{:S(2)}, u32[]{:S(2)}) collective-permute-start(bf16[256,512]{1,0:T(8,128)(2,1)S(1)} %collective-permute-done.7.refs_1_), channel_id=1, source_target_pairs={{0,8},{4,12},{8,0},{12,4},{16,24},{20,28},{24,16},{28,20},{1,9},{5... | collective-permute-start | bytes 786440 | tf_op jit(solution)/shard_map/ppermute | solution.py:19
  29.6 9.4 %copy-start = (s32[1024,1]{0,1:T(1,128)S(1)}, s32[1024,1]{0,1:T(1,128)}, u32[]{:S(2)}) copy-start(s32[1024,1]{0,1:T(1,128)} %param.7) | copy-start | bytes 12292
  29.7 9.3 %collective-permute-start.11 = (bf16[2048,512]{1,0:T(8,128)(2,1)S(1)}, bf16[2048,512]{1,0:T(8,128)(2,1)S(1)}, u32[]{:S(2)}, u32[]{:S(2)}) collective-permute-start(bf16[2048,512]{1,0:T(8,128)(2,1)S(1)} %shard_map.70.rest_2_), channel_id=1, source_target_pairs={{0,4},{4,0},{8,12},{12,8},{16,20},{20,16},{24,28},{28,24},{1,5},{5... | collective-permute-start | bytes 6291464 | tf_op jit(solution)/shard_map/ppermute | solution.py:19
  29.8 9.2 %collective-permute-start.12 = (bf16[256,512]{1,0:T(8,128)(2,1)S(1)}, bf16[256,512]{1,0:T(8,128)(2,1)S(1)}, u32[]{:S(2)}, u32[]{:S(2)}) collective-permute-start(bf16[256,512]{1,0:T(8,128)(2,1)S(1)} %get-tuple-element.64), channel_id=1, source_target_pairs={{0,8},{4,12},{8,0},{12,4},{16,24},{20,28},{24,16},{28,20},{1,9},{5... | collective-permute-start | bytes 786440 | tf_op jit(solution)/shard_map/ppermute | solution.py:19
  31.1 12.4 %collective-permute-start.4 = (bf16[256,512]{1,0:T(8,128)(2,1)S(1)}, bf16[256,512]{1,0:T(8,128)(2,1)S(1)}, u32[]{:S(2)}, u32[]{:S(2)}) collective-permute-start(bf16[256,512]{1,0:T(8,128)(2,1)S(1)} %get-tuple-element.49), channel_id=1, source_target_pairs={{0,16},{4,20},{8,24},{12,28},{16,0},{20,4},{24,8},{28,12},{1,17},{... | collective-permute-start | bytes 786440 | tf_op jit(solution)/shard_map/ppermute | solution.py:19
  31.9 13.2 %collective-permute-start.5 = (bf16[256,512]{1,0:T(8,128)(2,1)S(1)}, bf16[256,512]{1,0:T(8,128)(2,1)S(1)}, u32[]{:S(2)}, u32[]{:S(2)}) collective-permute-start(bf16[256,512]{1,0:T(8,128)(2,1)S(1)} %get-tuple-element.50), channel_id=1, source_target_pairs={{0,24},{4,28},{8,16},{12,20},{16,8},{20,12},{24,0},{28,4},{1,25},{... | collective-permute-start | bytes 786440 | tf_op jit(solution)/shard_map/ppermute | solution.py:19

commit v4 on v3

--- a/solution.py
+++ b/solution.py
@@ -152,6 +152,12 @@
         copy.wait()
 
 
+def passed(*refs):
+    count = len(refs) // 2
+    for value, out in zip(refs[:count], refs[count:]):
+        out[...] = value[...]
+
+
 def fetched(keep, cross, keep_here, cross_here, sems):
     loads = [
         pltpu.make_async_copy(keep.at[1:], keep_here, sems.at[0]),
@@ -254,6 +260,10 @@
     pieces = [mine, other, pack_near, pack_far, d_mine, d_other]
     (pack,) = call(packed, [array(8 * depth, features)], 1, [VMEM] * 6, *together(*pieces, done[0])[:6])
     matrices = [pack, swapped(pack, 1)]
+    returned = [back[m] for m in (1,)]
+    *returned, = call(passed, [part] * len(returned), 1 << 36, [VMEM] * len(returned), *returned)
+    for m, rows_back in zip((1,), returned):
+        back[m] = rows_back
     out = None
     for blocks in ((0, 1), (2, 3)):
         extra = [] if out is None else [out]

time: 48.8 us -> 45.2 us (0.926)
  waiting for transfers between devices: 16.8 us -> 13.1 us
    ppermute x13, waiting for transfers between devices: 16.8 us -> 13.1 us  [swapped(): return lax.ppermute(value, axis, pairs)]
    pallas_call x9 -> x10, Pallas kernels: 16.3 us -> 16.3 us  [call(): pl.pallas_call(body, out_shape=[shape for shape, _ in outs], in_specs=spe...]
  transfers between devices with their start and end apart: 13 -> 13, of which waited for: 8 -> 6; matrix products, arithmetic and copies ran while one was open for 0% -> 0% of each run, Pallas kernels for 26% -> 28%
where the time goes in v4:
time: 45.2 us; the launch traced here: 45 us
  Pallas kernels  16.3 us (36%)
  starting transfers between devices  15.4 us (34%)
  waiting for transfers between devices  13.1 us (29%)
    pallas_call x10, Pallas kernels, call(): pl.pallas_call(body, out_shape=[shape for shape, _ in outs], in_specs=spe...  16.3 us
    ppermute x13, starting transfers between devices, swapped(): return lax.ppermute(value, axis, pairs)  15.4 us
    ppermute x13, waiting for transfers between devices, swapped(): return lax.ppermute(value, axis, pairs)  13.1 us
  transfers between devices with their start and end apart: 13, of which 6 were waited for; matrix products, arithmetic and copies ran while one was open for 0% of the time, Pallas kernels for 28%

profile of v4, /device:TPU:0, one launch (start us, length us, event | category | flops | bytes accessed | tf_op | source)
XLA Modules:
  0.0 45.0 jit_solution(14859051370302249919)
XLA Ops:
  0.0 0.5 %collective-permute-start = (bf16[1024,512]{1,0:T(8,128)(2,1)}, bf16[1024,512]{1,0:T(8,128)(2,1)S(1)}, u32[]{:S(2)}, u32[]{:S(2)}) collective-permute-start(bf16[1024,512]{1,0:T(8,128)(2,1)} %interface.1), channel_id=1, source_target_pairs={{0,4},{4,0},{8,12},{12,8},{16,20},{20,16},{24,28},{28,24},{1,5},{5... | collective-permute-start | bytes 3145736 | tf_op jit(solution)/shard_map/ppermute | solution.py:19
  0.5 1.3 %shard_map.68 = (bf16[256,512]{1,0:T(8,128)(2,1)S(1)}, bf16[256,512]{1,0:T(8,128)(2,1)S(1)}) custom-call(s32[1]{0:T(128)} %bitcast.1.z, bf16[1,512,512]{2,1,0:T(8,128)(2,1)} %coupling.1, s32[1,8,8]{2,1,0:T(8,128)} %pattern.1), custom_call_target="tpu_custom_call" | custom-call | flops 1 | tf_op jit(solution)/shard_map/pallas_call | solution.py:42
  1.8 2.6 %collective-permute-start.6 = (bf16[256,512]{1,0:T(8,128)(2,1)S(1)}, bf16[256,512]{1,0:T(8,128)(2,1)S(1)}, u32[]{:S(2)}, u32[]{:S(2)}) collective-permute-start(bf16[256,512]{1,0:T(8,128)(2,1)S(1)} %get-tuple-element.58.refs_0_), channel_id=1, source_target_pairs={{0,8},{4,12},{8,0},{12,4},{16,24},{20,28},{24,16},{28,20},{1,9},{5... | collective-permute-start | bytes 786440 | tf_op jit(solution)/shard_map/ppermute | solution.py:19
  4.3 1.5 %collective-permute-start.7 = (bf16[256,512]{1,0:T(8,128)(2,1)S(1)}, bf16[256,512]{1,0:T(8,128)(2,1)S(1)}, u32[]{:S(2)}, u32[]{:S(2)}) collective-permute-start(bf16[256,512]{1,0:T(8,128)(2,1)S(1)} %get-tuple-element.59.refs_1_), channel_id=1, source_target_pairs={{0,16},{4,20},{8,24},{12,28},{16,0},{20,4},{24,8},{28,12},{1,17},{... | collective-permute-start | bytes 786440 | tf_op jit(solution)/shard_map/ppermute | solution.py:19
  5.8 3.4 %shard_map.64 = (bf16[256,512]{1,0:T(8,128)(2,1)S(1)}, bf16[256,512]{1,0:T(8,128)(2,1)S(1)}, bf16[256,512]{1,0:T(8,128)(2,1)S(1)}, bf16[256,512]{1,0:T(8,128)(2,1)S(1)}) custom-call(s32[1]{0:T(128)} %bitcast.me, bf16[1024,512]{1,0:T(8,128)(2,1)S(1)} %collective-permute-done.sibling, bf16[1024,512]{1,0:T(8,128)(2,1)} %interface.1, bf16[3,512,512]{2,1,0:T(8,128)(2,1)} %keep.2, ...), custom_call_target="tpu_custom_call" | custom-call | flops 536870912 | bytes 1048576 | tf_op jit(solution)/shard_map/pallas_call | solution.py:42
  9.3 0.6 %collective-permute-start.1 = (bf16[256,512]{1,0:T(8,128)(2,1)S(1)}, bf16[256,512]{1,0:T(8,128)(2,1)S(1)}, u32[]{:S(2)}, u32[]{:S(2)}) collective-permute-start(bf16[256,512]{1,0:T(8,128)(2,1)S(1)} %get-tuple-element.36), channel_id=1, source_target_pairs={{0,8},{4,12},{8,0},{12,4},{16,24},{20,28},{24,16},{28,20},{1,9},{5... | collective-permute-start | bytes 786440 | tf_op jit(solution)/shard_map/ppermute | solution.py:19
  9.9 1.0 %collective-permute-start.2 = (bf16[256,512]{1,0:T(8,128)(2,1)S(1)}, bf16[256,512]{1,0:T(8,128)(2,1)S(1)}, u32[]{:S(2)}, u32[]{:S(2)}) collective-permute-start(bf16[256,512]{1,0:T(8,128)(2,1)S(1)} %get-tuple-element.37), channel_id=1, source_target_pairs={{0,16},{4,20},{8,24},{12,28},{16,0},{20,4},{24,8},{28,12},{1,17},{... | collective-permute-start | bytes 786440 | tf_op jit(solution)/shard_map/ppermute | solution.py:19
  10.8 2.0 %collective-permute-start.3 = (bf16[256,512]{1,0:T(8,128)(2,1)S(1)}, bf16[256,512]{1,0:T(8,128)(2,1)S(1)}, u32[]{:S(2)}, u32[]{:S(2)}) collective-permute-start(bf16[256,512]{1,0:T(8,128)(2,1)S(1)} %get-tuple-element.38), channel_id=1, source_target_pairs={{0,24},{4,28},{8,16},{12,20},{16,8},{20,12},{24,0},{28,4},{1,25},{... | collective-permute-start | bytes 786440 | tf_op jit(solution)/shard_map/ppermute | solution.py:19
  12.8 0.5 %collective-permute-done.7.refs_1_ = bf16[256,512]{1,0:T(8,128)(2,1)S(1)} collective-permute-done((bf16[256,512]{1,0:T(8,128)(2,1)S(1)}, bf16[256,512]{1,0:T(8,128)(2,1)S(1)}, u32[]{:S(2)}, u32[]{:S(2)}) %collective-permute-start.7) | collective-permute-done | bytes 262176 | tf_op jit(solution)/shard_map/ppermute | solution.py:19
  13.3 1.6 %collective-permute-start.8 = (bf16[512,512]{1,0:T(8,128)(2,1)S(1)}, bf16[512,512]{1,0:T(8,128)(2,1)S(1)}, u32[]{:S(2)}, u32[]{:S(2)}) collective-permute-start(bf16[512,512]{1,0:T(8,128)(2,1)S(1)} %shard_map.69.refs_2_), channel_id=1, source_target_pairs={{0,1},{1,0},{2,3},{3,2},{4,5},{5,4},{6,7},{7,6},{8,9},{9,8},{10,11... | collective-permute-start | bytes 1572872 | tf_op jit(solution)/shard_map/ppermute | solution.py:19
  15.0 1.6 %shard_map.65 = (bf16[2,512,512]{2,1,0:T(8,128)(2,1)S(1)}, bf16[2,512,512]{2,1,0:T(8,128)(2,1)S(1)}) custom-call(bf16[3,512,512]{2,1,0:T(8,128)(2,1)} %keep.2, bf16[3,512,512]{2,1,0:T(8,128)(2,1)} %cross.2), custom_call_target="tpu_custom_call" | custom-call | flops 1 | tf_op jit(solution)/shard_map/pallas_call | solution.py:42
  16.6 2.0 %collective-permute-done.1.x1 = bf16[256,512]{1,0:T(8,128)(2,1)S(1)} collective-permute-done((bf16[256,512]{1,0:T(8,128)(2,1)S(1)}, bf16[256,512]{1,0:T(8,128)(2,1)S(1)}, u32[]{:S(2)}, u32[]{:S(2)}) %collective-permute-start.1) | collective-permute-done | bytes 262176 | tf_op jit(solution)/shard_map/ppermute | solution.py:19
  18.5 0.6 %collective-permute-start.9 = (bf16[256,512]{1,0:T(8,128)(2,1)S(1)}, bf16[256,512]{1,0:T(8,128)(2,1)S(1)}, u32[]{:S(2)}, u32[]{:S(2)}) collective-permute-start(bf16[256,512]{1,0:T(8,128)(2,1)S(1)} %collective-permute-done.6.refs_0_), channel_id=1, source_target_pairs={{0,16},{4,20},{8,24},{12,28},{16,0},{20,4},{24,8},{28,12},{1,17},{... | collective-permute-start | bytes 786440 | tf_op jit(solution)/shard_map/ppermute | solution.py:19
  19.1 1.5 %collective-permute-start.10 = (bf16[256,512]{1,0:T(8,128)(2,1)S(1)}, bf16[256,512]{1,0:T(8,128)(2,1)S(1)}, u32[]{:S(2)}, u32[]{:S(2)}) collective-permute-start(bf16[256,512]{1,0:T(8,128)(2,1)S(1)} %collective-permute-done.7.refs_1_), channel_id=1, source_target_pairs={{0,8},{4,12},{8,0},{12,4},{16,24},{20,28},{24,16},{28,20},{1,9},{5... | collective-permute-start | bytes 786440 | tf_op jit(solution)/shard_map/ppermute | solution.py:19
  20.6 3.4 %collective-permute-done.2.x2 = bf16[256,512]{1,0:T(8,128)(2,1)S(1)} collective-permute-done((bf16[256,512]{1,0:T(8,128)(2,1)S(1)}, bf16[256,512]{1,0:T(8,128)(2,1)S(1)}, u32[]{:S(2)}, u32[]{:S(2)}) %collective-permute-start.2) | collective-permute-done | bytes 262176 | tf_op jit(solution)/shard_map/ppermute | solution.py:19
  24.2 0.8 %shard_map.66 = (bf16[256,512]{1,0:T(8,128)(2,1)S(1)}, bf16[256,512]{1,0:T(8,128)(2,1)S(1)}) custom-call(bf16[256,512]{1,0:T(8,128)(2,1)S(1)} %get-tuple-element.41.x0, bf16[256,512]{1,0:T(8,128)(2,1)S(1)} %collective-permute-done.1.x1, bf16[2,512,512]{2,1,0:T(8,128)(2,1)S(1)} %get-tuple-element.45.keep, bf16[2,512,512]{2,1,0:T(8,128)(2,1)S(1)} %get-tuple-element.46.cross), custom_call_target="tpu_custom_call" | custom-call | flops 17179869184 | bytes 33554432 | tf_op jit(solution)/shard_map/pallas_call | solution.py:42
  25.0 2.1 %shard_map.67 = (bf16[256,512]{1,0:T(8,128)(2,1)S(1)}, bf16[256,512]{1,0:T(8,128)(2,1)S(1)}, bf16[256,512]{1,0:T(8,128)(2,1)S(1)}, bf16[256,512]{1,0:T(8,128)(2,1)S(1)}) custom-call(bf16[256,512]{1,0:T(8,128)(2,1)S(1)} %collective-permute-done.2.x2, bf16[256,512]{1,0:T(8,128)(2,1)S(1)} %collective-permute-done.3.x3, ...), custom_call_target="tpu_custom_call" | custom-call | flops 17179869184 | bytes 33554432 | tf_op jit(solution)/shard_map/pallas_call | solution.py:42
  27.0 1.6 %collective-permute-start.12 = (bf16[256,512]{1,0:T(8,128)(2,1)S(1)}, bf16[256,512]{1,0:T(8,128)(2,1)S(1)}, u32[]{:S(2)}, u32[]{:S(2)}) collective-permute-start(bf16[256,512]{1,0:T(8,128)(2,1)S(1)} %get-tuple-element.64), channel_id=1, source_target_pairs={{0,8},{4,12},{8,0},{12,4},{16,24},{20,28},{24,16},{28,20},{1,9},{5... | collective-permute-start | bytes 786440 | tf_op jit(solution)/shard_map/ppermute | solution.py:19
  28.6 0.6 %collective-permute-start.4 = (bf16[256,512]{1,0:T(8,128)(2,1)S(1)}, bf16[256,512]{1,0:T(8,128)(2,1)S(1)}, u32[]{:S(2)}, u32[]{:S(2)}) collective-permute-start(bf16[256,512]{1,0:T(8,128)(2,1)S(1)} %get-tuple-element.49), channel_id=1, source_target_pairs={{0,16},{4,20},{8,24},{12,28},{16,0},{20,4},{24,8},{28,12},{1,17},{... | collective-permute-start | bytes 786440 | tf_op jit(solution)/shard_map/ppermute | solution.py:19
  29.2 1.4 %collective-permute-start.5 = (bf16[256,512]{1,0:T(8,128)(2,1)S(1)}, bf16[256,512]{1,0:T(8,128)(2,1)S(1)}, u32[]{:S(2)}, u32[]{:S(2)}) collective-permute-start(bf16[256,512]{1,0:T(8,128)(2,1)S(1)} %get-tuple-element.50), channel_id=1, source_target_pairs={{0,24},{4,28},{8,16},{12,20},{16,8},{20,12},{24,0},{28,4},{1,25},{... | collective-permute-start | bytes 786440 | tf_op jit(solution)/shard_map/ppermute | solution.py:19
  30.9 5.5 %collective-permute-done.12.refs_0_ = bf16[256,512]{1,0:T(8,128)(2,1)S(1)} collective-permute-done((bf16[256,512]{1,0:T(8,128)(2,1)S(1)}, bf16[256,512]{1,0:T(8,128)(2,1)S(1)}, u32[]{:S(2)}, u32[]{:S(2)}) %collective-permute-start.12) | collective-permute-done | bytes 262176 | tf_op jit(solution)/shard_map/ppermute | solution.py:19
  36.4 3.5 %shard_map.72.rest_4_ = bf16[1024,512]{1,0:T(8,128)(2,1)} custom-call(s32[1]{0:T(128)} %bitcast.me, s32[1]{0:T(128)} %bitcast.1.z, s32[8,128]{1,0:T(8,128)S(1)} %bitcast.3, bf16[256,512]{1,0:T(8,128)(2,1)S(1)} %get-tuple-element.57.rest_0_, bf16[256,512]{1,0:T(8,128)(2,1)S(1)} %shard_map.71.rest_1_, bf16[2048,512]{1,0:T(8,128)(2,1)S(1)} %shard_map.70.rest_2_, ...), custom_call_target="tpu_custom_call" | custom-call | flops 2147483648 | bytes 4194304 | tf_op jit(solution)/shard_map/pallas_call | solution.py:42
  39.9 1.6 %collective-permute-done.4.rest_0_ = bf16[256,512]{1,0:T(8,128)(2,1)S(1)} collective-permute-done((bf16[256,512]{1,0:T(8,128)(2,1)S(1)}, bf16[256,512]{1,0:T(8,128)(2,1)S(1)}, u32[]{:S(2)}, u32[]{:S(2)}) %collective-permute-start.4) | collective-permute-done | bytes 262176 | tf_op jit(solution)/shard_map/ppermute | solution.py:19
  41.5 3.5 %shard_map.73 = bf16[1024,512]{1,0:T(8,128)(2,1)} custom-call(s32[1]{0:T(128)} %bitcast.me, s32[1]{0:T(128)} %bitcast.1.z, s32[8,128]{1,0:T(8,128)S(1)} %bitcast.4, bf16[256,512]{1,0:T(8,128)(2,1)S(1)} %collective-permute-done.4.rest_0_, bf16[256,512]{1,0:T(8,128)(2,1)S(1)} %collective-permute-done.5.rest_1_, ...), custom_call_target="tpu_custom_call", output_to_operand_aliasing={{}: (7, {})} | custom-call | flops 2147483648 | bytes 4194304 | tf_op jit(solution)/shard_map/pallas_call | solution.py:42
  (14 shorter events, 0.5 us)
Async XLA Ops:
  0.0 5.8 %collective-permute-start = (bf16[1024,512]{1,0:T(8,128)(2,1)}, bf16[1024,512]{1,0:T(8,128)(2,1)S(1)}, u32[]{:S(2)}, u32[]{:S(2)}) collective-permute-start(bf16[1024,512]{1,0:T(8,128)(2,1)} %interface.1), channel_id=1, source_target_pairs={{0,4},{4,0},{8,12},{12,8},{16,20},{20,16},{24,28},{28,24},{1,5},{5... | collective-permute-start | bytes 3145736 | tf_op jit(solution)/shard_map/ppermute | solution.py:19
  1.8 11.1 %collective-permute-start.6 = (bf16[256,512]{1,0:T(8,128)(2,1)S(1)}, bf16[256,512]{1,0:T(8,128)(2,1)S(1)}, u32[]{:S(2)}, u32[]{:S(2)}) collective-permute-start(bf16[256,512]{1,0:T(8,128)(2,1)S(1)} %get-tuple-element.58.refs_0_), channel_id=1, source_target_pairs={{0,8},{4,12},{8,0},{12,4},{16,24},{20,28},{24,16},{28,20},{1,9},{5... | collective-permute-start | bytes 786440 | tf_op jit(solution)/shard_map/ppermute | solution.py:19
  4.3 9.0 %collective-permute-start.7 = (bf16[256,512]{1,0:T(8,128)(2,1)S(1)}, bf16[256,512]{1,0:T(8,128)(2,1)S(1)}, u32[]{:S(2)}, u32[]{:S(2)}) collective-permute-start(bf16[256,512]{1,0:T(8,128)(2,1)S(1)} %get-tuple-element.59.refs_1_), channel_id=1, source_target_pairs={{0,16},{4,20},{8,24},{12,28},{16,0},{20,4},{24,8},{28,12},{1,17},{... | collective-permute-start | bytes 786440 | tf_op jit(solution)/shard_map/ppermute | solution.py:19
  9.3 9.2 %collective-permute-start.1 = (bf16[256,512]{1,0:T(8,128)(2,1)S(1)}, bf16[256,512]{1,0:T(8,128)(2,1)S(1)}, u32[]{:S(2)}, u32[]{:S(2)}) collective-permute-start(bf16[256,512]{1,0:T(8,128)(2,1)S(1)} %get-tuple-element.36), channel_id=1, source_target_pairs={{0,8},{4,12},{8,0},{12,4},{16,24},{20,28},{24,16},{28,20},{1,9},{5... | collective-permute-start | bytes 786440 | tf_op jit(solution)/shard_map/ppermute | solution.py:19
  9.9 14.1 %collective-permute-start.2 = (bf16[256,512]{1,0:T(8,128)(2,1)S(1)}, bf16[256,512]{1,0:T(8,128)(2,1)S(1)}, u32[]{:S(2)}, u32[]{:S(2)}) collective-permute-start(bf16[256,512]{1,0:T(8,128)(2,1)S(1)} %get-tuple-element.37), channel_id=1, source_target_pairs={{0,16},{4,20},{8,24},{12,28},{16,0},{20,4},{24,8},{28,12},{1,17},{... | collective-permute-start | bytes 786440 | tf_op jit(solution)/shard_map/ppermute | solution.py:19
  10.8 13.3 %collective-permute-start.3 = (bf16[256,512]{1,0:T(8,128)(2,1)S(1)}, bf16[256,512]{1,0:T(8,128)(2,1)S(1)}, u32[]{:S(2)}, u32[]{:S(2)}) collective-permute-start(bf16[256,512]{1,0:T(8,128)(2,1)S(1)} %get-tuple-element.38), channel_id=1, source_target_pairs={{0,24},{4,28},{8,16},{12,20},{16,8},{20,12},{24,0},{28,4},{1,25},{... | collective-permute-start | bytes 786440 | tf_op jit(solution)/shard_map/ppermute | solution.py:19
  13.3 15.9 %collective-permute-start.8 = (bf16[512,512]{1,0:T(8,128)(2,1)S(1)}, bf16[512,512]{1,0:T(8,128)(2,1)S(1)}, u32[]{:S(2)}, u32[]{:S(2)}) collective-permute-start(bf16[512,512]{1,0:T(8,128)(2,1)S(1)} %shard_map.69.refs_2_), channel_id=1, source_target_pairs={{0,1},{1,0},{2,3},{3,2},{4,5},{5,4},{6,7},{7,6},{8,9},{9,8},{10,11... | collective-permute-start | bytes 1572872 | tf_op jit(solution)/shard_map/ppermute | solution.py:19
  18.5 12.1 %collective-permute-start.9 = (bf16[256,512]{1,0:T(8,128)(2,1)S(1)}, bf16[256,512]{1,0:T(8,128)(2,1)S(1)}, u32[]{:S(2)}, u32[]{:S(2)}) collective-permute-start(bf16[256,512]{1,0:T(8,128)(2,1)S(1)} %collective-permute-done.6.refs_0_), channel_id=1, source_target_pairs={{0,16},{4,20},{8,24},{12,28},{16,0},{20,4},{24,8},{28,12},{1,17},{... | collective-permute-start | bytes 786440 | tf_op jit(solution)/shard_map/ppermute | solution.py:19
  19.1 11.6 %collective-permute-start.10 = (bf16[256,512]{1,0:T(8,128)(2,1)S(1)}, bf16[256,512]{1,0:T(8,128)(2,1)S(1)}, u32[]{:S(2)}, u32[]{:S(2)}) collective-permute-start(bf16[256,512]{1,0:T(8,128)(2,1)S(1)} %collective-permute-done.7.refs_1_), channel_id=1, source_target_pairs={{0,8},{4,12},{8,0},{12,4},{16,24},{20,28},{24,16},{28,20},{1,9},{5... | collective-permute-start | bytes 786440 | tf_op jit(solution)/shard_map/ppermute | solution.py:19
  27.0 9.3 %collective-permute-start.12 = (bf16[256,512]{1,0:T(8,128)(2,1)S(1)}, bf16[256,512]{1,0:T(8,128)(2,1)S(1)}, u32[]{:S(2)}, u32[]{:S(2)}) collective-permute-start(bf16[256,512]{1,0:T(8,128)(2,1)S(1)} %get-tuple-element.64), channel_id=1, source_target_pairs={{0,8},{4,12},{8,0},{12,4},{16,24},{20,28},{24,16},{28,20},{1,9},{5... | collective-permute-start | bytes 786440 | tf_op jit(solution)/shard_map/ppermute | solution.py:19
  28.6 12.9 %collective-permute-start.4 = (bf16[256,512]{1,0:T(8,128)(2,1)S(1)}, bf16[256,512]{1,0:T(8,128)(2,1)S(1)}, u32[]{:S(2)}, u32[]{:S(2)}) collective-permute-start(bf16[256,512]{1,0:T(8,128)(2,1)S(1)} %get-tuple-element.49), channel_id=1, source_target_pairs={{0,16},{4,20},{8,24},{12,28},{16,0},{20,4},{24,8},{28,12},{1,17},{... | collective-permute-start | bytes 786440 | tf_op jit(solution)/shard_map/ppermute | solution.py:19
  29.2 12.2 %collective-permute-start.5 = (bf16[256,512]{1,0:T(8,128)(2,1)S(1)}, bf16[256,512]{1,0:T(8,128)(2,1)S(1)}, u32[]{:S(2)}, u32[]{:S(2)}) collective-permute-start(bf16[256,512]{1,0:T(8,128)(2,1)S(1)} %get-tuple-element.50), channel_id=1, source_target_pairs={{0,24},{4,28},{8,16},{12,20},{16,8},{20,12},{24,0},{28,4},{1,25},{... | collective-permute-start | bytes 786440 | tf_op jit(solution)/shard_map/ppermute | solution.py:19
  30.8 5.6 %copy-start = (s32[1024,1]{0,1:T(1,128)S(1)}, s32[1024,1]{0,1:T(1,128)}, u32[]{:S(2)}) copy-start(s32[1024,1]{0,1:T(1,128)} %param.7) | copy-start | bytes 12292
  30.8 5.6 %collective-permute-start.11 = (bf16[2048,512]{1,0:T(8,128)(2,1)S(1)}, bf16[2048,512]{1,0:T(8,128)(2,1)S(1)}, u32[]{:S(2)}, u32[]{:S(2)}) collective-permute-start(bf16[2048,512]{1,0:T(8,128)(2,1)S(1)} %shard_map.70.rest_2_), channel_id=1, source_target_pairs={{0,4},{4,0},{8,12},{12,8},{16,20},{20,16},{24,28},{28,24},{1,5},{5... | collective-permute-start | bytes 6291464 | tf_op jit(solution)/shard_map/ppermute | solution.py:19

commit v5 on v4

--- a/solution.py
+++ b/solution.py
@@ -133,16 +133,14 @@
     relative = jnp.concatenate(columns_of, axis=0)
     parts = [half_rows(z, other, depth) for other in range(2)]
     values = [jnp.concatenate([x[:, part] for x in xs], axis=0) for part in parts]
-    chosen = [[jnp.where(relative == r, value, jnp.zeros_like(value)) for value in values] for r in range(8)]
     copies = []
     for n in range(2):
         columns = slice(n * depth, (n + 1) * depth)
         total = jnp.zeros((n_block * size, depth), jnp.float32)
         for r in range(8):
-            for h in range(2):
-                at = PLACES[r // 2][h] * depth
-                piece = packs[r % 2][at : at + depth, columns]
-                total += jnp.dot(chosen[r][h], piece, preferred_element_type=jnp.float32)
+            halves = [packs[r % 2][at * depth : (at + 1) * depth, columns] for at in PLACES[r // 2]]
+            each = [jnp.dot(v, half, preferred_element_type=jnp.float32) for v, half in zip(values, halves)]
+            total = jnp.where(relative == r, each[0] + each[1], total)
         held[:, columns] = total.astype(jnp.bfloat16)
         for i, m in enumerate(blocks):
             to = out.at[block_rows(me, m, size), columns]
@@ -243,13 +241,12 @@
         *(in_hbm(w) for w in together(keep_proj, sibling_proj, sent[0])[:2]),
         scratch=[pltpu.SemaphoreType.DMA((2,))],
     )
+    y0, y1 = call(second_level, [part] * 2, 1, [VMEM] * 4, x[0], x[1], *weights)
     if few:
         x_mine, y_other, _ = together(*near, sent[0])
         (pack_near,) = call(packed, [array(2 * depth, features)], 1, [VMEM] * 2, x_mine, y_other)
         pack_far = swapped(pack_near, 1, "blk")
-        d_mine, d_other = swapped(after(x_mine, x[1]), 4), swapped(after(y_other, x[1]), 2)
-        x = together(*x)
-    y0, y1 = call(second_level, [part] * 2, (1 << 34), [VMEM] * 4, x[0], x[1], *weights)
+        d_mine, d_other = swapped(after(x_mine, y0), 4), swapped(after(y_other, y0), 2)
     done = call(third_level, [part] * 4, (1 << 34), [VMEM] * 6, x[2], x[3], y0, y1, *weights)
     back = [done[0]] + [swapped(done[m], 2 * m) for m in (1, 2, 3)]
     if not few:

time: 45.2 us -> 44.2 us (0.978)
  Pallas kernels: 16.3 us -> 15.7 us
    pallas_call x10, Pallas kernels: 16.3 us -> 15.7 us  [call(): pl.pallas_call(body, out_shape=[shape for shape, _ in outs], in_specs=spe...]
where the time goes in v5:
time: 44.2 us; the launch traced here: 44.1 us
  Pallas kernels  15.7 us (36%)
  starting transfers between devices  15.5 us (35%)
  waiting for transfers between devices  12.7 us (29%)
    pallas_call x10, Pallas kernels, call(): pl.pallas_call(body, out_shape=[shape for shape, _ in outs], in_specs=spe...  15.7 us
    ppermute x13, starting transfers between devices, swapped(): return lax.ppermute(value, axis, pairs)  15.5 us
    ppermute x13, waiting for transfers between devices, swapped(): return lax.ppermute(value, axis, pairs)  12.7 us
  transfers between devices with their start and end apart: 13, of which 6 were waited for; matrix products, arithmetic and copies ran while one was open for 0% of the time, Pallas kernels for 28%

profile of v5, /device:TPU:0, one launch (start us, length us, event | category | flops | bytes accessed | tf_op | source)
XLA Modules:
  0.0 44.1 jit_solution(14320436758389781366)
XLA Ops:
  0.0 0.5 %collective-permute-start = (bf16[1024,512]{1,0:T(8,128)(2,1)}, bf16[1024,512]{1,0:T(8,128)(2,1)S(1)}, u32[]{:S(2)}, u32[]{:S(2)}) collective-permute-start(bf16[1024,512]{1,0:T(8,128)(2,1)} %interface.1), channel_id=1, source_target_pairs={{0,4},{4,0},{8,12},{12,8},{16,20},{20,16},{24,28},{28,24},{1,5},{5... | collective-permute-start | bytes 3145736 | tf_op jit(solution)/shard_map/ppermute | solution.py:19
  0.5 1.3 %shard_map.68 = (bf16[256,512]{1,0:T(8,128)(2,1)S(1)}, bf16[256,512]{1,0:T(8,128)(2,1)S(1)}) custom-call(s32[1]{0:T(128)} %bitcast.1.z, bf16[1,512,512]{2,1,0:T(8,128)(2,1)} %coupling.1, s32[1,8,8]{2,1,0:T(8,128)} %pattern.1), custom_call_target="tpu_custom_call" | custom-call | flops 1 | tf_op jit(solution)/shard_map/pallas_call | solution.py:42
  1.8 2.6 %collective-permute-start.6 = (bf16[256,512]{1,0:T(8,128)(2,1)S(1)}, bf16[256,512]{1,0:T(8,128)(2,1)S(1)}, u32[]{:S(2)}, u32[]{:S(2)}) collective-permute-start(bf16[256,512]{1,0:T(8,128)(2,1)S(1)} %get-tuple-element.50.refs_0_), channel_id=1, source_target_pairs={{0,8},{4,12},{8,0},{12,4},{16,24},{20,28},{24,16},{28,20},{1,9},{5... | collective-permute-start | bytes 786440 | tf_op jit(solution)/shard_map/ppermute | solution.py:19
  4.3 1.5 %collective-permute-start.7 = (bf16[256,512]{1,0:T(8,128)(2,1)S(1)}, bf16[256,512]{1,0:T(8,128)(2,1)S(1)}, u32[]{:S(2)}, u32[]{:S(2)}) collective-permute-start(bf16[256,512]{1,0:T(8,128)(2,1)S(1)} %get-tuple-element.51.refs_1_), channel_id=1, source_target_pairs={{0,16},{4,20},{8,24},{12,28},{16,0},{20,4},{24,8},{28,12},{1,17},{... | collective-permute-start | bytes 786440 | tf_op jit(solution)/shard_map/ppermute | solution.py:19
  5.8 3.4 %shard_map.64 = (bf16[256,512]{1,0:T(8,128)(2,1)S(1)}, bf16[256,512]{1,0:T(8,128)(2,1)S(1)}, bf16[256,512]{1,0:T(8,128)(2,1)S(1)}, bf16[256,512]{1,0:T(8,128)(2,1)S(1)}) custom-call(s32[1]{0:T(128)} %bitcast.me, bf16[1024,512]{1,0:T(8,128)(2,1)S(1)} %collective-permute-done.sibling, bf16[1024,512]{1,0:T(8,128)(2,1)} %interface.1, bf16[3,512,512]{2,1,0:T(8,128)(2,1)} %keep.2, ...), custom_call_target="tpu_custom_call" | custom-call | flops 536870912 | bytes 1048576 | tf_op jit(solution)/shard_map/pallas_call | solution.py:42
  9.3 0.6 %collective-permute-start.3 = (bf16[256,512]{1,0:T(8,128)(2,1)S(1)}, bf16[256,512]{1,0:T(8,128)(2,1)S(1)}, u32[]{:S(2)}, u32[]{:S(2)}) collective-permute-start(bf16[256,512]{1,0:T(8,128)(2,1)S(1)} %get-tuple-element.34), channel_id=1, source_target_pairs={{0,8},{4,12},{8,0},{12,4},{16,24},{20,28},{24,16},{28,20},{1,9},{5... | collective-permute-start | bytes 786440 | tf_op jit(solution)/shard_map/ppermute | solution.py:19
  9.9 1.0 %collective-permute-start.1 = (bf16[256,512]{1,0:T(8,128)(2,1)S(1)}, bf16[256,512]{1,0:T(8,128)(2,1)S(1)}, u32[]{:S(2)}, u32[]{:S(2)}) collective-permute-start(bf16[256,512]{1,0:T(8,128)(2,1)S(1)} %get-tuple-element.31), channel_id=1, source_target_pairs={{0,16},{4,20},{8,24},{12,28},{16,0},{20,4},{24,8},{28,12},{1,17},{... | collective-permute-start | bytes 786440 | tf_op jit(solution)/shard_map/ppermute | solution.py:19
  10.8 2.0 %collective-permute-start.2 = (bf16[256,512]{1,0:T(8,128)(2,1)S(1)}, bf16[256,512]{1,0:T(8,128)(2,1)S(1)}, u32[]{:S(2)}, u32[]{:S(2)}) collective-permute-start(bf16[256,512]{1,0:T(8,128)(2,1)S(1)} %get-tuple-element.32), channel_id=1, source_target_pairs={{0,24},{4,28},{8,16},{12,20},{16,8},{20,12},{24,0},{28,4},{1,25},{... | collective-permute-start | bytes 786440 | tf_op jit(solution)/shard_map/ppermute | solution.py:19
  12.8 0.5 %collective-permute-done.7.refs_1_ = bf16[256,512]{1,0:T(8,128)(2,1)S(1)} collective-permute-done((bf16[256,512]{1,0:T(8,128)(2,1)S(1)}, bf16[256,512]{1,0:T(8,128)(2,1)S(1)}, u32[]{:S(2)}, u32[]{:S(2)}) %collective-permute-start.7) | collective-permute-done | bytes 262176 | tf_op jit(solution)/shard_map/ppermute | solution.py:19
  13.3 1.6 %collective-permute-start.8 = (bf16[512,512]{1,0:T(8,128)(2,1)S(1)}, bf16[512,512]{1,0:T(8,128)(2,1)S(1)}, u32[]{:S(2)}, u32[]{:S(2)}) collective-permute-start(bf16[512,512]{1,0:T(8,128)(2,1)S(1)} %shard_map.69.refs_2_), channel_id=1, source_target_pairs={{0,1},{1,0},{2,3},{3,2},{4,5},{5,4},{6,7},{7,6},{8,9},{9,8},{10,11... | collective-permute-start | bytes 1572872 | tf_op jit(solution)/shard_map/ppermute | solution.py:19
  15.0 1.6 %shard_map.65 = (bf16[2,512,512]{2,1,0:T(8,128)(2,1)S(1)}, bf16[2,512,512]{2,1,0:T(8,128)(2,1)S(1)}) custom-call(bf16[3,512,512]{2,1,0:T(8,128)(2,1)} %keep.2, bf16[3,512,512]{2,1,0:T(8,128)(2,1)} %cross.2), custom_call_target="tpu_custom_call" | custom-call | flops 1 | tf_op jit(solution)/shard_map/pallas_call | solution.py:42
  16.6 2.0 %collective-permute-done.3.x1 = bf16[256,512]{1,0:T(8,128)(2,1)S(1)} collective-permute-done((bf16[256,512]{1,0:T(8,128)(2,1)S(1)}, bf16[256,512]{1,0:T(8,128)(2,1)S(1)}, u32[]{:S(2)}, u32[]{:S(2)}) %collective-permute-start.3) | collective-permute-done | bytes 262176 | tf_op jit(solution)/shard_map/ppermute | solution.py:19
  18.5 0.8 %shard_map.66 = (bf16[256,512]{1,0:T(8,128)(2,1)S(1)}, bf16[256,512]{1,0:T(8,128)(2,1)S(1)}) custom-call(bf16[256,512]{1,0:T(8,128)(2,1)S(1)} %get-tuple-element.33.x0, bf16[256,512]{1,0:T(8,128)(2,1)S(1)} %collective-permute-done.3.x1, bf16[2,512,512]{2,1,0:T(8,128)(2,1)S(1)} %get-tuple-element.37.keep, bf16[2,512,512]{2,1,0:T(8,128)(2,1)S(1)} %get-tuple-element.38.cross), custom_call_target="tpu_custom_call" | custom-call | flops 1 | tf_op jit(solution)/shard_map/pallas_call | solution.py:42
  19.3 0.6 %collective-permute-start.9 = (bf16[256,512]{1,0:T(8,128)(2,1)S(1)}, bf16[256,512]{1,0:T(8,128)(2,1)S(1)}, u32[]{:S(2)}, u32[]{:S(2)}) collective-permute-start(bf16[256,512]{1,0:T(8,128)(2,1)S(1)} %collective-permute-done.6.refs_0_), channel_id=1, source_target_pairs={{0,16},{4,20},{8,24},{12,28},{16,0},{20,4},{24,8},{28,12},{1,17},{... | collective-permute-start | bytes 786440 | tf_op jit(solution)/shard_map/ppermute | solution.py:19
  19.9 1.5 %collective-permute-start.10 = (bf16[256,512]{1,0:T(8,128)(2,1)S(1)}, bf16[256,512]{1,0:T(8,128)(2,1)S(1)}, u32[]{:S(2)}, u32[]{:S(2)}) collective-permute-start(bf16[256,512]{1,0:T(8,128)(2,1)S(1)} %collective-permute-done.7.refs_1_), channel_id=1, source_target_pairs={{0,8},{4,12},{8,0},{12,4},{16,24},{20,28},{24,16},{28,20},{1,9},{5... | collective-permute-start | bytes 786440 | tf_op jit(solution)/shard_map/ppermute | solution.py:19
  21.4 2.6 %collective-permute-done.1.x2 = bf16[256,512]{1,0:T(8,128)(2,1)S(1)} collective-permute-done((bf16[256,512]{1,0:T(8,128)(2,1)S(1)}, bf16[256,512]{1,0:T(8,128)(2,1)S(1)}, u32[]{:S(2)}, u32[]{:S(2)}) %collective-permute-start.1) | collective-permute-done | bytes 262176 | tf_op jit(solution)/shard_map/ppermute | solution.py:19
  24.2 2.1 %shard_map.67 = (bf16[256,512]{1,0:T(8,128)(2,1)S(1)}, bf16[256,512]{1,0:T(8,128)(2,1)S(1)}, bf16[256,512]{1,0:T(8,128)(2,1)S(1)}, bf16[256,512]{1,0:T(8,128)(2,1)S(1)}) custom-call(bf16[256,512]{1,0:T(8,128)(2,1)S(1)} %collective-permute-done.1.x2, bf16[256,512]{1,0:T(8,128)(2,1)S(1)} %collective-permute-done.2.x3, ...), custom_call_target="tpu_custom_call" | custom-call | flops 17179869184 | bytes 33554432 | tf_op jit(solution)/shard_map/pallas_call | solution.py:42
  26.2 1.6 %collective-permute-start.12 = (bf16[256,512]{1,0:T(8,128)(2,1)S(1)}, bf16[256,512]{1,0:T(8,128)(2,1)S(1)}, u32[]{:S(2)}, u32[]{:S(2)}) collective-permute-start(bf16[256,512]{1,0:T(8,128)(2,1)S(1)} %get-tuple-element.56), channel_id=1, source_target_pairs={{0,8},{4,12},{8,0},{12,4},{16,24},{20,28},{24,16},{28,20},{1,9},{5... | collective-permute-start | bytes 786440 | tf_op jit(solution)/shard_map/ppermute | solution.py:19
  27.8 0.6 %collective-permute-start.4 = (bf16[256,512]{1,0:T(8,128)(2,1)S(1)}, bf16[256,512]{1,0:T(8,128)(2,1)S(1)}, u32[]{:S(2)}, u32[]{:S(2)}) collective-permute-start(bf16[256,512]{1,0:T(8,128)(2,1)S(1)} %get-tuple-element.41), channel_id=1, source_target_pairs={{0,16},{4,20},{8,24},{12,28},{16,0},{20,4},{24,8},{28,12},{1,17},{... | collective-permute-start | bytes 786440 | tf_op jit(solution)/shard_map/ppermute | solution.py:19
  28.4 1.4 %collective-permute-start.5 = (bf16[256,512]{1,0:T(8,128)(2,1)S(1)}, bf16[256,512]{1,0:T(8,128)(2,1)S(1)}, u32[]{:S(2)}, u32[]{:S(2)}) collective-permute-start(bf16[256,512]{1,0:T(8,128)(2,1)S(1)} %get-tuple-element.42), channel_id=1, source_target_pairs={{0,24},{4,28},{8,16},{12,20},{16,8},{20,12},{24,0},{28,4},{1,25},{... | collective-permute-start | bytes 786440 | tf_op jit(solution)/shard_map/ppermute | solution.py:19
  30.0 5.5 %collective-permute-done.12.refs_0_ = bf16[256,512]{1,0:T(8,128)(2,1)S(1)} collective-permute-done((bf16[256,512]{1,0:T(8,128)(2,1)S(1)}, bf16[256,512]{1,0:T(8,128)(2,1)S(1)}, u32[]{:S(2)}, u32[]{:S(2)}) %collective-permute-start.12) | collective-permute-done | bytes 262176 | tf_op jit(solution)/shard_map/ppermute | solution.py:19
  35.6 3.2 %shard_map.72.rest_4_ = bf16[1024,512]{1,0:T(8,128)(2,1)} custom-call(s32[1]{0:T(128)} %bitcast.me, s32[1]{0:T(128)} %bitcast.1.z, s32[8,128]{1,0:T(8,128)S(1)} %bitcast.3, bf16[256,512]{1,0:T(8,128)(2,1)S(1)} %get-tuple-element.49.rest_0_, bf16[256,512]{1,0:T(8,128)(2,1)S(1)} %shard_map.71.rest_1_, bf16[2048,512]{1,0:T(8,128)(2,1)S(1)} %shard_map.70.rest_2_, ...), custom_call_target="tpu_custom_call" | custom-call | flops 2147483648 | bytes 4194304 | tf_op jit(solution)/shard_map/pallas_call | solution.py:42
  38.8 2.1 %collective-permute-done.4.rest_0_ = bf16[256,512]{1,0:T(8,128)(2,1)S(1)} collective-permute-done((bf16[256,512]{1,0:T(8,128)(2,1)S(1)}, bf16[256,512]{1,0:T(8,128)(2,1)S(1)}, u32[]{:S(2)}, u32[]{:S(2)}) %collective-permute-start.4) | collective-permute-done | bytes 262176 | tf_op jit(solution)/shard_map/ppermute | solution.py:19
  40.8 3.2 %shard_map.73 = bf16[1024,512]{1,0:T(8,128)(2,1)} custom-call(s32[1]{0:T(128)} %bitcast.me, s32[1]{0:T(128)} %bitcast.1.z, s32[8,128]{1,0:T(8,128)S(1)} %bitcast.4, bf16[256,512]{1,0:T(8,128)(2,1)S(1)} %collective-permute-done.4.rest_0_, bf16[256,512]{1,0:T(8,128)(2,1)S(1)} %collective-permute-done.5.rest_1_, ...), custom_call_target="tpu_custom_call", output_to_operand_aliasing={{}: (7, {})} | custom-call | flops 2147483648 | bytes 4194304 | tf_op jit(solution)/shard_map/pallas_call | solution.py:42
  (14 shorter events, 0.5 us)
Async XLA Ops:
  0.0 5.8 %collective-permute-start = (bf16[1024,512]{1,0:T(8,128)(2,1)}, bf16[1024,512]{1,0:T(8,128)(2,1)S(1)}, u32[]{:S(2)}, u32[]{:S(2)}) collective-permute-start(bf16[1024,512]{1,0:T(8,128)(2,1)} %interface.1), channel_id=1, source_target_pairs={{0,4},{4,0},{8,12},{12,8},{16,20},{20,16},{24,28},{28,24},{1,5},{5... | collective-permute-start | bytes 3145736 | tf_op jit(solution)/shard_map/ppermute | solution.py:19
  1.8 11.1 %collective-permute-start.6 = (bf16[256,512]{1,0:T(8,128)(2,1)S(1)}, bf16[256,512]{1,0:T(8,128)(2,1)S(1)}, u32[]{:S(2)}, u32[]{:S(2)}) collective-permute-start(bf16[256,512]{1,0:T(8,128)(2,1)S(1)} %get-tuple-element.50.refs_0_), channel_id=1, source_target_pairs={{0,8},{4,12},{8,0},{12,4},{16,24},{20,28},{24,16},{28,20},{1,9},{5... | collective-permute-start | bytes 786440 | tf_op jit(solution)/shard_map/ppermute | solution.py:19
  4.3 9.0 %collective-permute-start.7 = (bf16[256,512]{1,0:T(8,128)(2,1)S(1)}, bf16[256,512]{1,0:T(8,128)(2,1)S(1)}, u32[]{:S(2)}, u32[]{:S(2)}) collective-permute-start(bf16[256,512]{1,0:T(8,128)(2,1)S(1)} %get-tuple-element.51.refs_1_), channel_id=1, source_target_pairs={{0,16},{4,20},{8,24},{12,28},{16,0},{20,4},{24,8},{28,12},{1,17},{... | collective-permute-start | bytes 786440 | tf_op jit(solution)/shard_map/ppermute | solution.py:19
  9.3 9.2 %collective-permute-start.3 = (bf16[256,512]{1,0:T(8,128)(2,1)S(1)}, bf16[256,512]{1,0:T(8,128)(2,1)S(1)}, u32[]{:S(2)}, u32[]{:S(2)}) collective-permute-start(bf16[256,512]{1,0:T(8,128)(2,1)S(1)} %get-tuple-element.34), channel_id=1, source_target_pairs={{0,8},{4,12},{8,0},{12,4},{16,24},{20,28},{24,16},{28,20},{1,9},{5... | collective-permute-start | bytes 786440 | tf_op jit(solution)/shard_map/ppermute | solution.py:19
  9.9 14.1 %collective-permute-start.1 = (bf16[256,512]{1,0:T(8,128)(2,1)S(1)}, bf16[256,512]{1,0:T(8,128)(2,1)S(1)}, u32[]{:S(2)}, u32[]{:S(2)}) collective-permute-start(bf16[256,512]{1,0:T(8,128)(2,1)S(1)} %get-tuple-element.31), channel_id=1, source_target_pairs={{0,16},{4,20},{8,24},{12,28},{16,0},{20,4},{24,8},{28,12},{1,17},{... | collective-permute-start | bytes 786440 | tf_op jit(solution)/shard_map/ppermute | solution.py:19
  10.8 13.3 %collective-permute-start.2 = (bf16[256,512]{1,0:T(8,128)(2,1)S(1)}, bf16[256,512]{1,0:T(8,128)(2,1)S(1)}, u32[]{:S(2)}, u32[]{:S(2)}) collective-permute-start(bf16[256,512]{1,0:T(8,128)(2,1)S(1)} %get-tuple-element.32), channel_id=1, source_target_pairs={{0,24},{4,28},{8,16},{12,20},{16,8},{20,12},{24,0},{28,4},{1,25},{... | collective-permute-start | bytes 786440 | tf_op jit(solution)/shard_map/ppermute | solution.py:19
  13.3 15.1 %collective-permute-start.8 = (bf16[512,512]{1,0:T(8,128)(2,1)S(1)}, bf16[512,512]{1,0:T(8,128)(2,1)S(1)}, u32[]{:S(2)}, u32[]{:S(2)}) collective-permute-start(bf16[512,512]{1,0:T(8,128)(2,1)S(1)} %shard_map.69.refs_2_), channel_id=1, source_target_pairs={{0,1},{1,0},{2,3},{3,2},{4,5},{5,4},{6,7},{7,6},{8,9},{9,8},{10,11... | collective-permute-start | bytes 1572872 | tf_op jit(solution)/shard_map/ppermute | solution.py:19
  19.3 10.5 %collective-permute-start.9 = (bf16[256,512]{1,0:T(8,128)(2,1)S(1)}, bf16[256,512]{1,0:T(8,128)(2,1)S(1)}, u32[]{:S(2)}, u32[]{:S(2)}) collective-permute-start(bf16[256,512]{1,0:T(8,128)(2,1)S(1)} %collective-permute-done.6.refs_0_), channel_id=1, source_target_pairs={{0,16},{4,20},{8,24},{12,28},{16,0},{20,4},{24,8},{28,12},{1,17},{... | collective-permute-start | bytes 786440 | tf_op jit(solution)/shard_map/ppermute | solution.py:19
  19.9 9.9 %collective-permute-start.10 = (bf16[256,512]{1,0:T(8,128)(2,1)S(1)}, bf16[256,512]{1,0:T(8,128)(2,1)S(1)}, u32[]{:S(2)}, u32[]{:S(2)}) collective-permute-start(bf16[256,512]{1,0:T(8,128)(2,1)S(1)} %collective-permute-done.7.refs_1_), channel_id=1, source_target_pairs={{0,8},{4,12},{8,0},{12,4},{16,24},{20,28},{24,16},{28,20},{1,9},{5... | collective-permute-start | bytes 786440 | tf_op jit(solution)/shard_map/ppermute | solution.py:19
  26.2 9.3 %collective-permute-start.12 = (bf16[256,512]{1,0:T(8,128)(2,1)S(1)}, bf16[256,512]{1,0:T(8,128)(2,1)S(1)}, u32[]{:S(2)}, u32[]{:S(2)}) collective-permute-start(bf16[256,512]{1,0:T(8,128)(2,1)S(1)} %get-tuple-element.56), channel_id=1, source_target_pairs={{0,8},{4,12},{8,0},{12,4},{16,24},{20,28},{24,16},{28,20},{1,9},{5... | collective-permute-start | bytes 786440 | tf_op jit(solution)/shard_map/ppermute | solution.py:19
  27.8 13.1 %collective-permute-start.4 = (bf16[256,512]{1,0:T(8,128)(2,1)S(1)}, bf16[256,512]{1,0:T(8,128)(2,1)S(1)}, u32[]{:S(2)}, u32[]{:S(2)}) collective-permute-start(bf16[256,512]{1,0:T(8,128)(2,1)S(1)} %get-tuple-element.41), channel_id=1, source_target_pairs={{0,16},{4,20},{8,24},{12,28},{16,0},{20,4},{24,8},{28,12},{1,17},{... | collective-permute-start | bytes 786440 | tf_op jit(solution)/shard_map/ppermute | solution.py:19
  28.4 12.4 %collective-permute-start.5 = (bf16[256,512]{1,0:T(8,128)(2,1)S(1)}, bf16[256,512]{1,0:T(8,128)(2,1)S(1)}, u32[]{:S(2)}, u32[]{:S(2)}) collective-permute-start(bf16[256,512]{1,0:T(8,128)(2,1)S(1)} %get-tuple-element.42), channel_id=1, source_target_pairs={{0,24},{4,28},{8,16},{12,20},{16,8},{20,12},{24,0},{28,4},{1,25},{... | collective-permute-start | bytes 786440 | tf_op jit(solution)/shard_map/ppermute | solution.py:19
  30.0 5.6 %copy-start = (s32[1024,1]{0,1:T(1,128)S(1)}, s32[1024,1]{0,1:T(1,128)}, u32[]{:S(2)}) copy-start(s32[1024,1]{0,1:T(1,128)} %param.7) | copy-start | bytes 12292
  30.0 5.6 %collective-permute-start.11 = (bf16[2048,512]{1,0:T(8,128)(2,1)S(1)}, bf16[2048,512]{1,0:T(8,128)(2,1)S(1)}, u32[]{:S(2)}, u32[]{:S(2)}) collective-permute-start(bf16[2048,512]{1,0:T(8,128)(2,1)S(1)} %shard_map.70.rest_2_), channel_id=1, source_target_pairs={{0,4},{4,0},{8,12},{12,8},{16,20},{20,16},{24,28},{28,24},{1,5},{5... | collective-permute-start | bytes 6291464 | tf_op jit(solution)/shard_map/ppermute | solution.py:19

commit v6 on v5

--- a/solution.py
+++ b/solution.py
@@ -213,7 +213,7 @@
         in_hbm(pattern),
         scratch=[
             pltpu.VMEM(coupling.shape, coupling.dtype),
-            pltpu.VMEM(pattern.shape, pattern.dtype),
+            pltpu.SMEM(pattern.shape, pattern.dtype),
             pltpu.SemaphoreType.DMA((2,)),
         ],
     )

time: 44.2 us -> 44.1 us (level)
  no operation moved by 1% of the time
where the time goes in v6:
time: 44.1 us; the launch traced here: 43.9 us
  Pallas kernels  15.6 us (35%)
  starting transfers between devices  15.5 us (35%)
  waiting for transfers between devices  12.7 us (29%)
    pallas_call x10, Pallas kernels, call(): pl.pallas_call(body, out_shape=[shape for shape, _ in outs], in_specs=spe...  15.6 us
    ppermute x13, starting transfers between devices, swapped(): return lax.ppermute(value, axis, pairs)  15.5 us
    ppermute x13, waiting for transfers between devices, swapped(): return lax.ppermute(value, axis, pairs)  12.7 us
  transfers between devices with their start and end apart: 13, of which 6 were waited for; matrix products, arithmetic and copies ran while one was open for 0% of the time, Pallas kernels for 28%

profile of v6, /device:TPU:0, one launch (start us, length us, event | category | flops | bytes accessed | tf_op | source)
XLA Modules:
  0.0 43.9 jit_solution(16625090592820192950)
XLA Ops:
  0.0 0.5 %collective-permute-start = (bf16[1024,512]{1,0:T(8,128)(2,1)}, bf16[1024,512]{1,0:T(8,128)(2,1)S(1)}, u32[]{:S(2)}, u32[]{:S(2)}) collective-permute-start(bf16[1024,512]{1,0:T(8,128)(2,1)} %interface.1), channel_id=1, source_target_pairs={{0,4},{4,0},{8,12},{12,8},{16,20},{20,16},{24,28},{28,24},{1,5},{5... | collective-permute-start | bytes 3145736 | tf_op jit(solution)/shard_map/ppermute | solution.py:19
  0.5 1.1 %shard_map.68 = (bf16[256,512]{1,0:T(8,128)(2,1)S(1)}, bf16[256,512]{1,0:T(8,128)(2,1)S(1)}) custom-call(s32[1]{0:T(128)} %bitcast.1.z, bf16[1,512,512]{2,1,0:T(8,128)(2,1)} %coupling.1, s32[1,8,8]{2,1,0:T(8,128)} %pattern.1), custom_call_target="tpu_custom_call" | custom-call | flops 1 | tf_op jit(solution)/shard_map/pallas_call | solution.py:42
  1.6 2.6 %collective-permute-start.6 = (bf16[256,512]{1,0:T(8,128)(2,1)S(1)}, bf16[256,512]{1,0:T(8,128)(2,1)S(1)}, u32[]{:S(2)}, u32[]{:S(2)}) collective-permute-start(bf16[256,512]{1,0:T(8,128)(2,1)S(1)} %get-tuple-element.50.refs_0_), channel_id=1, source_target_pairs={{0,8},{4,12},{8,0},{12,4},{16,24},{20,28},{24,16},{28,20},{1,9},{5... | collective-permute-start | bytes 786440 | tf_op jit(solution)/shard_map/ppermute | solution.py:19
  4.2 1.5 %collective-permute-start.7 = (bf16[256,512]{1,0:T(8,128)(2,1)S(1)}, bf16[256,512]{1,0:T(8,128)(2,1)S(1)}, u32[]{:S(2)}, u32[]{:S(2)}) collective-permute-start(bf16[256,512]{1,0:T(8,128)(2,1)S(1)} %get-tuple-element.51.refs_1_), channel_id=1, source_target_pairs={{0,16},{4,20},{8,24},{12,28},{16,0},{20,4},{24,8},{28,12},{1,17},{... | collective-permute-start | bytes 786440 | tf_op jit(solution)/shard_map/ppermute | solution.py:19
  5.7 3.4 %shard_map.64 = (bf16[256,512]{1,0:T(8,128)(2,1)S(1)}, bf16[256,512]{1,0:T(8,128)(2,1)S(1)}, bf16[256,512]{1,0:T(8,128)(2,1)S(1)}, bf16[256,512]{1,0:T(8,128)(2,1)S(1)}) custom-call(s32[1]{0:T(128)} %bitcast.me, bf16[1024,512]{1,0:T(8,128)(2,1)S(1)} %collective-permute-done.sibling, bf16[1024,512]{1,0:T(8,128)(2,1)} %interface.1, bf16[3,512,512]{2,1,0:T(8,128)(2,1)} %keep.2, ...), custom_call_target="tpu_custom_call" | custom-call | flops 536870912 | bytes 1048576 | tf_op jit(solution)/shard_map/pallas_call | solution.py:42
  9.1 0.6 %collective-permute-start.3 = (bf16[256,512]{1,0:T(8,128)(2,1)S(1)}, bf16[256,512]{1,0:T(8,128)(2,1)S(1)}, u32[]{:S(2)}, u32[]{:S(2)}) collective-permute-start(bf16[256,512]{1,0:T(8,128)(2,1)S(1)} %get-tuple-element.34), channel_id=1, source_target_pairs={{0,8},{4,12},{8,0},{12,4},{16,24},{20,28},{24,16},{28,20},{1,9},{5... | collective-permute-start | bytes 786440 | tf_op jit(solution)/shard_map/ppermute | solution.py:19
  9.7 1.1 %collective-permute-start.1 = (bf16[256,512]{1,0:T(8,128)(2,1)S(1)}, bf16[256,512]{1,0:T(8,128)(2,1)S(1)}, u32[]{:S(2)}, u32[]{:S(2)}) collective-permute-start(bf16[256,512]{1,0:T(8,128)(2,1)S(1)} %get-tuple-element.31), channel_id=1, source_target_pairs={{0,16},{4,20},{8,24},{12,28},{16,0},{20,4},{24,8},{28,12},{1,17},{... | collective-permute-start | bytes 786440 | tf_op jit(solution)/shard_map/ppermute | solution.py:19
  10.8 1.8 %collective-permute-start.2 = (bf16[256,512]{1,0:T(8,128)(2,1)S(1)}, bf16[256,512]{1,0:T(8,128)(2,1)S(1)}, u32[]{:S(2)}, u32[]{:S(2)}) collective-permute-start(bf16[256,512]{1,0:T(8,128)(2,1)S(1)} %get-tuple-element.32), channel_id=1, source_target_pairs={{0,24},{4,28},{8,16},{12,20},{16,8},{20,12},{24,0},{28,4},{1,25},{... | collective-permute-start | bytes 786440 | tf_op jit(solution)/shard_map/ppermute | solution.py:19
  12.7 0.5 %collective-permute-done.7.refs_1_ = bf16[256,512]{1,0:T(8,128)(2,1)S(1)} collective-permute-done((bf16[256,512]{1,0:T(8,128)(2,1)S(1)}, bf16[256,512]{1,0:T(8,128)(2,1)S(1)}, u32[]{:S(2)}, u32[]{:S(2)}) %collective-permute-start.7) | collective-permute-done | bytes 262176 | tf_op jit(solution)/shard_map/ppermute | solution.py:19
  13.2 1.6 %collective-permute-start.8 = (bf16[512,512]{1,0:T(8,128)(2,1)S(1)}, bf16[512,512]{1,0:T(8,128)(2,1)S(1)}, u32[]{:S(2)}, u32[]{:S(2)}) collective-permute-start(bf16[512,512]{1,0:T(8,128)(2,1)S(1)} %shard_map.69.refs_2_), channel_id=1, source_target_pairs={{0,1},{1,0},{2,3},{3,2},{4,5},{5,4},{6,7},{7,6},{8,9},{9,8},{10,11... | collective-permute-start | bytes 1572872 | tf_op jit(solution)/shard_map/ppermute | solution.py:19
  14.8 1.6 %shard_map.65 = (bf16[2,512,512]{2,1,0:T(8,128)(2,1)S(1)}, bf16[2,512,512]{2,1,0:T(8,128)(2,1)S(1)}) custom-call(bf16[3,512,512]{2,1,0:T(8,128)(2,1)} %keep.2, bf16[3,512,512]{2,1,0:T(8,128)(2,1)} %cross.2), custom_call_target="tpu_custom_call" | custom-call | flops 1 | tf_op jit(solution)/shard_map/pallas_call | solution.py:42
  16.4 2.0 %collective-permute-done.3.x1 = bf16[256,512]{1,0:T(8,128)(2,1)S(1)} collective-permute-done((bf16[256,512]{1,0:T(8,128)(2,1)S(1)}, bf16[256,512]{1,0:T(8,128)(2,1)S(1)}, u32[]{:S(2)}, u32[]{:S(2)}) %collective-permute-start.3) | collective-permute-done | bytes 262176 | tf_op jit(solution)/shard_map/ppermute | solution.py:19
  18.4 0.8 %shard_map.66 = (bf16[256,512]{1,0:T(8,128)(2,1)S(1)}, bf16[256,512]{1,0:T(8,128)(2,1)S(1)}) custom-call(bf16[256,512]{1,0:T(8,128)(2,1)S(1)} %get-tuple-element.33.x0, bf16[256,512]{1,0:T(8,128)(2,1)S(1)} %collective-permute-done.3.x1, bf16[2,512,512]{2,1,0:T(8,128)(2,1)S(1)} %get-tuple-element.37.keep, bf16[2,512,512]{2,1,0:T(8,128)(2,1)S(1)} %get-tuple-element.38.cross), custom_call_target="tpu_custom_call" | custom-call | flops 1 | tf_op jit(solution)/shard_map/pallas_call | solution.py:42
  19.2 0.6 %collective-permute-start.9 = (bf16[256,512]{1,0:T(8,128)(2,1)S(1)}, bf16[256,512]{1,0:T(8,128)(2,1)S(1)}, u32[]{:S(2)}, u32[]{:S(2)}) collective-permute-start(bf16[256,512]{1,0:T(8,128)(2,1)S(1)} %collective-permute-done.6.refs_0_), channel_id=1, source_target_pairs={{0,16},{4,20},{8,24},{12,28},{16,0},{20,4},{24,8},{28,12},{1,17},{... | collective-permute-start | bytes 786440 | tf_op jit(solution)/shard_map/ppermute | solution.py:19
  19.8 1.5 %collective-permute-start.10 = (bf16[256,512]{1,0:T(8,128)(2,1)S(1)}, bf16[256,512]{1,0:T(8,128)(2,1)S(1)}, u32[]{:S(2)}, u32[]{:S(2)}) collective-permute-start(bf16[256,512]{1,0:T(8,128)(2,1)S(1)} %collective-permute-done.7.refs_1_), channel_id=1, source_target_pairs={{0,8},{4,12},{8,0},{12,4},{16,24},{20,28},{24,16},{28,20},{1,9},{5... | collective-permute-start | bytes 786440 | tf_op jit(solution)/shard_map/ppermute | solution.py:19
  21.3 2.6 %collective-permute-done.1.x2 = bf16[256,512]{1,0:T(8,128)(2,1)S(1)} collective-permute-done((bf16[256,512]{1,0:T(8,128)(2,1)S(1)}, bf16[256,512]{1,0:T(8,128)(2,1)S(1)}, u32[]{:S(2)}, u32[]{:S(2)}) %collective-permute-start.1) | collective-permute-done | bytes 262176 | tf_op jit(solution)/shard_map/ppermute | solution.py:19
  24.0 2.1 %shard_map.67 = (bf16[256,512]{1,0:T(8,128)(2,1)S(1)}, bf16[256,512]{1,0:T(8,128)(2,1)S(1)}, bf16[256,512]{1,0:T(8,128)(2,1)S(1)}, bf16[256,512]{1,0:T(8,128)(2,1)S(1)}) custom-call(bf16[256,512]{1,0:T(8,128)(2,1)S(1)} %collective-permute-done.1.x2, bf16[256,512]{1,0:T(8,128)(2,1)S(1)} %collective-permute-done.2.x3, ...), custom_call_target="tpu_custom_call" | custom-call | flops 17179869184 | bytes 33554432 | tf_op jit(solution)/shard_map/pallas_call | solution.py:42
  26.1 1.6 %collective-permute-start.12 = (bf16[256,512]{1,0:T(8,128)(2,1)S(1)}, bf16[256,512]{1,0:T(8,128)(2,1)S(1)}, u32[]{:S(2)}, u32[]{:S(2)}) collective-permute-start(bf16[256,512]{1,0:T(8,128)(2,1)S(1)} %get-tuple-element.56), channel_id=1, source_target_pairs={{0,8},{4,12},{8,0},{12,4},{16,24},{20,28},{24,16},{28,20},{1,9},{5... | collective-permute-start | bytes 786440 | tf_op jit(solution)/shard_map/ppermute | solution.py:19
  27.6 0.6 %collective-permute-start.4 = (bf16[256,512]{1,0:T(8,128)(2,1)S(1)}, bf16[256,512]{1,0:T(8,128)(2,1)S(1)}, u32[]{:S(2)}, u32[]{:S(2)}) collective-permute-start(bf16[256,512]{1,0:T(8,128)(2,1)S(1)} %get-tuple-element.41), channel_id=1, source_target_pairs={{0,16},{4,20},{8,24},{12,28},{16,0},{20,4},{24,8},{28,12},{1,17},{... | collective-permute-start | bytes 786440 | tf_op jit(solution)/shard_map/ppermute | solution.py:19
  28.3 1.4 %collective-permute-start.5 = (bf16[256,512]{1,0:T(8,128)(2,1)S(1)}, bf16[256,512]{1,0:T(8,128)(2,1)S(1)}, u32[]{:S(2)}, u32[]{:S(2)}) collective-permute-start(bf16[256,512]{1,0:T(8,128)(2,1)S(1)} %get-tuple-element.42), channel_id=1, source_target_pairs={{0,24},{4,28},{8,16},{12,20},{16,8},{20,12},{24,0},{28,4},{1,25},{... | collective-permute-start | bytes 786440 | tf_op jit(solution)/shard_map/ppermute | solution.py:19
  29.9 5.5 %collective-permute-done.12.refs_0_ = bf16[256,512]{1,0:T(8,128)(2,1)S(1)} collective-permute-done((bf16[256,512]{1,0:T(8,128)(2,1)S(1)}, bf16[256,512]{1,0:T(8,128)(2,1)S(1)}, u32[]{:S(2)}, u32[]{:S(2)}) %collective-permute-start.12) | collective-permute-done | bytes 262176 | tf_op jit(solution)/shard_map/ppermute | solution.py:19
  35.4 3.2 %shard_map.72.rest_4_ = bf16[1024,512]{1,0:T(8,128)(2,1)} custom-call(s32[1]{0:T(128)} %bitcast.me, s32[1]{0:T(128)} %bitcast.1.z, s32[8,128]{1,0:T(8,128)S(1)} %bitcast.3, bf16[256,512]{1,0:T(8,128)(2,1)S(1)} %get-tuple-element.49.rest_0_, bf16[256,512]{1,0:T(8,128)(2,1)S(1)} %shard_map.71.rest_1_, bf16[2048,512]{1,0:T(8,128)(2,1)S(1)} %shard_map.70.rest_2_, ...), custom_call_target="tpu_custom_call" | custom-call | flops 2147483648 | bytes 4194304 | tf_op jit(solution)/shard_map/pallas_call | solution.py:42
  38.6 2.0 %collective-permute-done.4.rest_0_ = bf16[256,512]{1,0:T(8,128)(2,1)S(1)} collective-permute-done((bf16[256,512]{1,0:T(8,128)(2,1)S(1)}, bf16[256,512]{1,0:T(8,128)(2,1)S(1)}, u32[]{:S(2)}, u32[]{:S(2)}) %collective-permute-start.4) | collective-permute-done | bytes 262176 | tf_op jit(solution)/shard_map/ppermute | solution.py:19
  40.7 3.2 %shard_map.73 = bf16[1024,512]{1,0:T(8,128)(2,1)} custom-call(s32[1]{0:T(128)} %bitcast.me, s32[1]{0:T(128)} %bitcast.1.z, s32[8,128]{1,0:T(8,128)S(1)} %bitcast.4, bf16[256,512]{1,0:T(8,128)(2,1)S(1)} %collective-permute-done.4.rest_0_, bf16[256,512]{1,0:T(8,128)(2,1)S(1)} %collective-permute-done.5.rest_1_, ...), custom_call_target="tpu_custom_call", output_to_operand_aliasing={{}: (7, {})} | custom-call | flops 2147483648 | bytes 4194304 | tf_op jit(solution)/shard_map/pallas_call | solution.py:42
  (14 shorter events, 0.5 us)
Async XLA Ops:
  0.0 5.7 %collective-permute-start = (bf16[1024,512]{1,0:T(8,128)(2,1)}, bf16[1024,512]{1,0:T(8,128)(2,1)S(1)}, u32[]{:S(2)}, u32[]{:S(2)}) collective-permute-start(bf16[1024,512]{1,0:T(8,128)(2,1)} %interface.1), channel_id=1, source_target_pairs={{0,4},{4,0},{8,12},{12,8},{16,20},{20,16},{24,28},{28,24},{1,5},{5... | collective-permute-start | bytes 3145736 | tf_op jit(solution)/shard_map/ppermute | solution.py:19
  1.6 11.1 %collective-permute-start.6 = (bf16[256,512]{1,0:T(8,128)(2,1)S(1)}, bf16[256,512]{1,0:T(8,128)(2,1)S(1)}, u32[]{:S(2)}, u32[]{:S(2)}) collective-permute-start(bf16[256,512]{1,0:T(8,128)(2,1)S(1)} %get-tuple-element.50.refs_0_), channel_id=1, source_target_pairs={{0,8},{4,12},{8,0},{12,4},{16,24},{20,28},{24,16},{28,20},{1,9},{5... | collective-permute-start | bytes 786440 | tf_op jit(solution)/shard_map/ppermute | solution.py:19
  4.2 9.0 %collective-permute-start.7 = (bf16[256,512]{1,0:T(8,128)(2,1)S(1)}, bf16[256,512]{1,0:T(8,128)(2,1)S(1)}, u32[]{:S(2)}, u32[]{:S(2)}) collective-permute-start(bf16[256,512]{1,0:T(8,128)(2,1)S(1)} %get-tuple-element.51.refs_1_), channel_id=1, source_target_pairs={{0,16},{4,20},{8,24},{12,28},{16,0},{20,4},{24,8},{28,12},{1,17},{... | collective-permute-start | bytes 786440 | tf_op jit(solution)/shard_map/ppermute | solution.py:19
  9.1 9.2 %collective-permute-start.3 = (bf16[256,512]{1,0:T(8,128)(2,1)S(1)}, bf16[256,512]{1,0:T(8,128)(2,1)S(1)}, u32[]{:S(2)}, u32[]{:S(2)}) collective-permute-start(bf16[256,512]{1,0:T(8,128)(2,1)S(1)} %get-tuple-element.34), channel_id=1, source_target_pairs={{0,8},{4,12},{8,0},{12,4},{16,24},{20,28},{24,16},{28,20},{1,9},{5... | collective-permute-start | bytes 786440 | tf_op jit(solution)/shard_map/ppermute | solution.py:19
  9.7 14.1 %collective-permute-start.1 = (bf16[256,512]{1,0:T(8,128)(2,1)S(1)}, bf16[256,512]{1,0:T(8,128)(2,1)S(1)}, u32[]{:S(2)}, u32[]{:S(2)}) collective-permute-start(bf16[256,512]{1,0:T(8,128)(2,1)S(1)} %get-tuple-element.31), channel_id=1, source_target_pairs={{0,16},{4,20},{8,24},{12,28},{16,0},{20,4},{24,8},{28,12},{1,17},{... | collective-permute-start | bytes 786440 | tf_op jit(solution)/shard_map/ppermute | solution.py:19
  10.8 13.2 %collective-permute-start.2 = (bf16[256,512]{1,0:T(8,128)(2,1)S(1)}, bf16[256,512]{1,0:T(8,128)(2,1)S(1)}, u32[]{:S(2)}, u32[]{:S(2)}) collective-permute-start(bf16[256,512]{1,0:T(8,128)(2,1)S(1)} %get-tuple-element.32), channel_id=1, source_target_pairs={{0,24},{4,28},{8,16},{12,20},{16,8},{20,12},{24,0},{28,4},{1,25},{... | collective-permute-start | bytes 786440 | tf_op jit(solution)/shard_map/ppermute | solution.py:19
  13.2 15.1 %collective-permute-start.8 = (bf16[512,512]{1,0:T(8,128)(2,1)S(1)}, bf16[512,512]{1,0:T(8,128)(2,1)S(1)}, u32[]{:S(2)}, u32[]{:S(2)}) collective-permute-start(bf16[512,512]{1,0:T(8,128)(2,1)S(1)} %shard_map.69.refs_2_), channel_id=1, source_target_pairs={{0,1},{1,0},{2,3},{3,2},{4,5},{5,4},{6,7},{7,6},{8,9},{9,8},{10,11... | collective-permute-start | bytes 1572872 | tf_op jit(solution)/shard_map/ppermute | solution.py:19
  19.2 10.5 %collective-permute-start.9 = (bf16[256,512]{1,0:T(8,128)(2,1)S(1)}, bf16[256,512]{1,0:T(8,128)(2,1)S(1)}, u32[]{:S(2)}, u32[]{:S(2)}) collective-permute-start(bf16[256,512]{1,0:T(8,128)(2,1)S(1)} %collective-permute-done.6.refs_0_), channel_id=1, source_target_pairs={{0,16},{4,20},{8,24},{12,28},{16,0},{20,4},{24,8},{28,12},{1,17},{... | collective-permute-start | bytes 786440 | tf_op jit(solution)/shard_map/ppermute | solution.py:19
  19.8 9.9 %collective-permute-start.10 = (bf16[256,512]{1,0:T(8,128)(2,1)S(1)}, bf16[256,512]{1,0:T(8,128)(2,1)S(1)}, u32[]{:S(2)}, u32[]{:S(2)}) collective-permute-start(bf16[256,512]{1,0:T(8,128)(2,1)S(1)} %collective-permute-done.7.refs_1_), channel_id=1, source_target_pairs={{0,8},{4,12},{8,0},{12,4},{16,24},{20,28},{24,16},{28,20},{1,9},{5... | collective-permute-start | bytes 786440 | tf_op jit(solution)/shard_map/ppermute | solution.py:19
  26.1 9.3 %collective-permute-start.12 = (bf16[256,512]{1,0:T(8,128)(2,1)S(1)}, bf16[256,512]{1,0:T(8,128)(2,1)S(1)}, u32[]{:S(2)}, u32[]{:S(2)}) collective-permute-start(bf16[256,512]{1,0:T(8,128)(2,1)S(1)} %get-tuple-element.56), channel_id=1, source_target_pairs={{0,8},{4,12},{8,0},{12,4},{16,24},{20,28},{24,16},{28,20},{1,9},{5... | collective-permute-start | bytes 786440 | tf_op jit(solution)/shard_map/ppermute | solution.py:19
  27.6 13.1 %collective-permute-start.4 = (bf16[256,512]{1,0:T(8,128)(2,1)S(1)}, bf16[256,512]{1,0:T(8,128)(2,1)S(1)}, u32[]{:S(2)}, u32[]{:S(2)}) collective-permute-start(bf16[256,512]{1,0:T(8,128)(2,1)S(1)} %get-tuple-element.41), channel_id=1, source_target_pairs={{0,16},{4,20},{8,24},{12,28},{16,0},{20,4},{24,8},{28,12},{1,17},{... | collective-permute-start | bytes 786440 | tf_op jit(solution)/shard_map/ppermute | solution.py:19
  28.3 12.4 %collective-permute-start.5 = (bf16[256,512]{1,0:T(8,128)(2,1)S(1)}, bf16[256,512]{1,0:T(8,128)(2,1)S(1)}, u32[]{:S(2)}, u32[]{:S(2)}) collective-permute-start(bf16[256,512]{1,0:T(8,128)(2,1)S(1)} %get-tuple-element.42), channel_id=1, source_target_pairs={{0,24},{4,28},{8,16},{12,20},{16,8},{20,12},{24,0},{28,4},{1,25},{... | collective-permute-start | bytes 786440 | tf_op jit(solution)/shard_map/ppermute | solution.py:19
  29.8 5.6 %copy-start = (s32[1024,1]{0,1:T(1,128)S(1)}, s32[1024,1]{0,1:T(1,128)}, u32[]{:S(2)}) copy-start(s32[1024,1]{0,1:T(1,128)} %param.7) | copy-start | bytes 12292
  29.8 5.6 %collective-permute-start.11 = (bf16[2048,512]{1,0:T(8,128)(2,1)S(1)}, bf16[2048,512]{1,0:T(8,128)(2,1)S(1)}, u32[]{:S(2)}, u32[]{:S(2)}) collective-permute-start(bf16[2048,512]{1,0:T(8,128)(2,1)S(1)} %shard_map.70.rest_2_), channel_id=1, source_target_pairs={{0,4},{4,0},{8,12},{12,8},{16,20},{20,16},{24,28},{28,24},{1,5},{5... | collective-permute-start | bytes 6291464 | tf_op jit(solution)/shard_map/ppermute | solution.py:19

commit v7 on v6

--- a/solution.py
+++ b/solution.py
@@ -33,7 +33,10 @@
 
 def mixed(own, sibling, keep, cross):
     combined = jnp.dot(own, keep, preferred_element_type=jnp.float32)
-    combined = combined + jnp.dot(sibling, cross, preferred_element_type=jnp.float32)
+    return normal(combined + jnp.dot(sibling, cross, preferred_element_type=jnp.float32))
+
+
+def normal(combined):
     scale_rows = lax.rsqrt(jnp.mean(combined * combined, axis=1, keepdims=True) + EPSILON)
     return (combined * scale_rows).astype(jnp.bfloat16)
 
@@ -58,22 +61,25 @@
 def first_level(me, sibling, interface, keep, cross, *rest):
     outs, (own, keep_here, cross_here, sems) = rest[:4], rest[4:]
     size = outs[0].shape[0]
+    order = (1, 2, 3, 0)
     loads = [
+        pltpu.make_async_copy(cross.at[0], cross_here, sems.at[5]),
         pltpu.make_async_copy(keep.at[0], keep_here, sems.at[4]),
-        pltpu.make_async_copy(cross.at[0], cross_here, sems.at[5]),
     ]
-    order = (1, 2, 3, 0)
     for m in order:
         rows = block_rows(me, m, size)
         loads.append(pltpu.make_async_copy(interface.at[rows], own.at[rows], sems.at[m]))
     for load in loads:
         load.start()
     loads[0].wait()
+    terms = []
+    for m in order:
+        terms.append(jnp.dot(sibling[block_rows(me, m, size), :], cross_here[...], preferred_element_type=jnp.float32))
     loads[1].wait()
-    for m, load in zip(order, loads[2:]):
+    for m, load, term in zip(order, loads[2:], terms):
         load.wait()
         rows = block_rows(me, m, size)
-        outs[m][...] = mixed(own[rows, :], sibling[rows, :], keep_here[...], cross_here[...])
+        outs[m][...] = normal(jnp.dot(own[rows, :], keep_here[...], preferred_element_type=jnp.float32) + term)
 
 
 def second_level(x0, x1, keep, cross, out0, out1):

time: 44.1 us -> 44.1 us (level)
  no operation moved by 1% of the time
where the time goes in v7:
time: 44.1 us; the launch traced here: 43.9 us
  starting transfers between devices  15.7 us (36%)
  Pallas kernels  15.4 us (35%)
  waiting for transfers between devices  12.7 us (29%)
    ppermute x13, starting transfers between devices, swapped(): return lax.ppermute(value, axis, pairs)  15.7 us
    pallas_call x10, Pallas kernels, call(): pl.pallas_call(body, out_shape=[shape for shape, _ in outs], in_specs=spe...  15.4 us
    ppermute x13, waiting for transfers between devices, swapped(): return lax.ppermute(value, axis, pairs)  12.7 us
  transfers between devices with their start and end apart: 13, of which 6 were waited for; matrix products, arithmetic and copies ran while one was open for 0% of the time, Pallas kernels for 28%

profile of v7, /device:TPU:0, one launch (start us, length us, event | category | flops | bytes accessed | tf_op | source)
XLA Modules:
  0.0 43.9 jit_solution(12822142117903953694)
XLA Ops:
  0.0 0.5 %collective-permute-start = (bf16[1024,512]{1,0:T(8,128)(2,1)}, bf16[1024,512]{1,0:T(8,128)(2,1)S(1)}, u32[]{:S(2)}, u32[]{:S(2)}) collective-permute-start(bf16[1024,512]{1,0:T(8,128)(2,1)} %interface.1), channel_id=1, source_target_pairs={{0,4},{4,0},{8,12},{12,8},{16,20},{20,16},{24,28},{28,24},{1,5},{5... | collective-permute-start | bytes 3145736 | tf_op jit(solution)/shard_map/ppermute | solution.py:19
  0.5 1.1 %shard_map.68 = (bf16[256,512]{1,0:T(8,128)(2,1)S(1)}, bf16[256,512]{1,0:T(8,128)(2,1)S(1)}) custom-call(s32[1]{0:T(128)} %bitcast.1.z, bf16[1,512,512]{2,1,0:T(8,128)(2,1)} %coupling.1, s32[1,8,8]{2,1,0:T(8,128)} %pattern.1), custom_call_target="tpu_custom_call" | custom-call | flops 1 | tf_op jit(solution)/shard_map/pallas_call | solution.py:45
  1.6 2.6 %collective-permute-start.6 = (bf16[256,512]{1,0:T(8,128)(2,1)S(1)}, bf16[256,512]{1,0:T(8,128)(2,1)S(1)}, u32[]{:S(2)}, u32[]{:S(2)}) collective-permute-start(bf16[256,512]{1,0:T(8,128)(2,1)S(1)} %get-tuple-element.50.refs_0_), channel_id=1, source_target_pairs={{0,8},{4,12},{8,0},{12,4},{16,24},{20,28},{24,16},{28,20},{1,9},{5... | collective-permute-start | bytes 786440 | tf_op jit(solution)/shard_map/ppermute | solution.py:19
  4.2 1.5 %collective-permute-start.7 = (bf16[256,512]{1,0:T(8,128)(2,1)S(1)}, bf16[256,512]{1,0:T(8,128)(2,1)S(1)}, u32[]{:S(2)}, u32[]{:S(2)}) collective-permute-start(bf16[256,512]{1,0:T(8,128)(2,1)S(1)} %get-tuple-element.51.refs_1_), channel_id=1, source_target_pairs={{0,16},{4,20},{8,24},{12,28},{16,0},{20,4},{24,8},{28,12},{1,17},{... | collective-permute-start | bytes 786440 | tf_op jit(solution)/shard_map/ppermute | solution.py:19
  5.7 3.3 %shard_map.64 = (bf16[256,512]{1,0:T(8,128)(2,1)S(1)}, bf16[256,512]{1,0:T(8,128)(2,1)S(1)}, bf16[256,512]{1,0:T(8,128)(2,1)S(1)}, bf16[256,512]{1,0:T(8,128)(2,1)S(1)}) custom-call(s32[1]{0:T(128)} %bitcast.me, bf16[1024,512]{1,0:T(8,128)(2,1)S(1)} %collective-permute-done.sibling, bf16[1024,512]{1,0:T(8,128)(2,1)} %interface.1, bf16[3,512,512]{2,1,0:T(8,128)(2,1)} %keep.2, ...), custom_call_target="tpu_custom_call" | custom-call | flops 536870912 | bytes 1048576 | tf_op jit(solution)/shard_map/pallas_call | solution.py:45
  8.9 0.6 %collective-permute-start.3 = (bf16[256,512]{1,0:T(8,128)(2,1)S(1)}, bf16[256,512]{1,0:T(8,128)(2,1)S(1)}, u32[]{:S(2)}, u32[]{:S(2)}) collective-permute-start(bf16[256,512]{1,0:T(8,128)(2,1)S(1)} %get-tuple-element.34), channel_id=1, source_target_pairs={{0,8},{4,12},{8,0},{12,4},{16,24},{20,28},{24,16},{28,20},{1,9},{5... | collective-permute-start | bytes 786440 | tf_op jit(solution)/shard_map/ppermute | solution.py:19
  9.5 1.1 %collective-permute-start.1 = (bf16[256,512]{1,0:T(8,128)(2,1)S(1)}, bf16[256,512]{1,0:T(8,128)(2,1)S(1)}, u32[]{:S(2)}, u32[]{:S(2)}) collective-permute-start(bf16[256,512]{1,0:T(8,128)(2,1)S(1)} %get-tuple-element.31), channel_id=1, source_target_pairs={{0,16},{4,20},{8,24},{12,28},{16,0},{20,4},{24,8},{28,12},{1,17},{... | collective-permute-start | bytes 786440 | tf_op jit(solution)/shard_map/ppermute | solution.py:19
  10.7 1.8 %collective-permute-start.2 = (bf16[256,512]{1,0:T(8,128)(2,1)S(1)}, bf16[256,512]{1,0:T(8,128)(2,1)S(1)}, u32[]{:S(2)}, u32[]{:S(2)}) collective-permute-start(bf16[256,512]{1,0:T(8,128)(2,1)S(1)} %get-tuple-element.32), channel_id=1, source_target_pairs={{0,24},{4,28},{8,16},{12,20},{16,8},{20,12},{24,0},{28,4},{1,25},{... | collective-permute-start | bytes 786440 | tf_op jit(solution)/shard_map/ppermute | solution.py:19
  12.5 0.8 %collective-permute-done.7.refs_1_ = bf16[256,512]{1,0:T(8,128)(2,1)S(1)} collective-permute-done((bf16[256,512]{1,0:T(8,128)(2,1)S(1)}, bf16[256,512]{1,0:T(8,128)(2,1)S(1)}, u32[]{:S(2)}, u32[]{:S(2)}) %collective-permute-start.7) | collective-permute-done | bytes 262176 | tf_op jit(solution)/shard_map/ppermute | solution.py:19
  13.3 1.6 %collective-permute-start.8 = (bf16[512,512]{1,0:T(8,128)(2,1)S(1)}, bf16[512,512]{1,0:T(8,128)(2,1)S(1)}, u32[]{:S(2)}, u32[]{:S(2)}) collective-permute-start(bf16[512,512]{1,0:T(8,128)(2,1)S(1)} %shard_map.69.refs_2_), channel_id=1, source_target_pairs={{0,1},{1,0},{2,3},{3,2},{4,5},{5,4},{6,7},{7,6},{8,9},{9,8},{10,11... | collective-permute-start | bytes 1572872 | tf_op jit(solution)/shard_map/ppermute | solution.py:19
  15.0 1.6 %shard_map.65 = (bf16[2,512,512]{2,1,0:T(8,128)(2,1)S(1)}, bf16[2,512,512]{2,1,0:T(8,128)(2,1)S(1)}) custom-call(bf16[3,512,512]{2,1,0:T(8,128)(2,1)} %keep.2, bf16[3,512,512]{2,1,0:T(8,128)(2,1)} %cross.2), custom_call_target="tpu_custom_call" | custom-call | flops 1 | tf_op jit(solution)/shard_map/pallas_call | solution.py:45
  16.5 1.6 %collective-permute-done.3.x1 = bf16[256,512]{1,0:T(8,128)(2,1)S(1)} collective-permute-done((bf16[256,512]{1,0:T(8,128)(2,1)S(1)}, bf16[256,512]{1,0:T(8,128)(2,1)S(1)}, u32[]{:S(2)}, u32[]{:S(2)}) %collective-permute-start.3) | collective-permute-done | bytes 262176 | tf_op jit(solution)/shard_map/ppermute | solution.py:19
  18.2 0.8 %shard_map.66 = (bf16[256,512]{1,0:T(8,128)(2,1)S(1)}, bf16[256,512]{1,0:T(8,128)(2,1)S(1)}) custom-call(bf16[256,512]{1,0:T(8,128)(2,1)S(1)} %get-tuple-element.33.x0, bf16[256,512]{1,0:T(8,128)(2,1)S(1)} %collective-permute-done.3.x1, bf16[2,512,512]{2,1,0:T(8,128)(2,1)S(1)} %get-tuple-element.37.keep, bf16[2,512,512]{2,1,0:T(8,128)(2,1)S(1)} %get-tuple-element.38.cross), custom_call_target="tpu_custom_call" | custom-call | flops 1 | tf_op jit(solution)/shard_map/pallas_call | solution.py:45
  19.0 0.8 %collective-permute-start.9 = (bf16[256,512]{1,0:T(8,128)(2,1)S(1)}, bf16[256,512]{1,0:T(8,128)(2,1)S(1)}, u32[]{:S(2)}, u32[]{:S(2)}) collective-permute-start(bf16[256,512]{1,0:T(8,128)(2,1)S(1)} %collective-permute-done.6.refs_0_), channel_id=1, source_target_pairs={{0,16},{4,20},{8,24},{12,28},{16,0},{20,4},{24,8},{28,12},{1,17},{... | collective-permute-start | bytes 786440 | tf_op jit(solution)/shard_map/ppermute | solution.py:19
  19.8 1.5 %collective-permute-start.10 = (bf16[256,512]{1,0:T(8,128)(2,1)S(1)}, bf16[256,512]{1,0:T(8,128)(2,1)S(1)}, u32[]{:S(2)}, u32[]{:S(2)}) collective-permute-start(bf16[256,512]{1,0:T(8,128)(2,1)S(1)} %collective-permute-done.7.refs_1_), channel_id=1, source_target_pairs={{0,8},{4,12},{8,0},{12,4},{16,24},{20,28},{24,16},{28,20},{1,9},{5... | collective-permute-start | bytes 786440 | tf_op jit(solution)/shard_map/ppermute | solution.py:19
  21.3 2.6 %collective-permute-done.1.x2 = bf16[256,512]{1,0:T(8,128)(2,1)S(1)} collective-permute-done((bf16[256,512]{1,0:T(8,128)(2,1)S(1)}, bf16[256,512]{1,0:T(8,128)(2,1)S(1)}, u32[]{:S(2)}, u32[]{:S(2)}) %collective-permute-start.1) | collective-permute-done | bytes 262176 | tf_op jit(solution)/shard_map/ppermute | solution.py:19
  24.0 2.1 %shard_map.67 = (bf16[256,512]{1,0:T(8,128)(2,1)S(1)}, bf16[256,512]{1,0:T(8,128)(2,1)S(1)}, bf16[256,512]{1,0:T(8,128)(2,1)S(1)}, bf16[256,512]{1,0:T(8,128)(2,1)S(1)}) custom-call(bf16[256,512]{1,0:T(8,128)(2,1)S(1)} %collective-permute-done.1.x2, bf16[256,512]{1,0:T(8,128)(2,1)S(1)} %collective-permute-done.2.x3, ...), custom_call_target="tpu_custom_call" | custom-call | flops 17179869184 | bytes 33554432 | tf_op jit(solution)/shard_map/pallas_call | solution.py:45
  26.1 1.6 %collective-permute-start.12 = (bf16[256,512]{1,0:T(8,128)(2,1)S(1)}, bf16[256,512]{1,0:T(8,128)(2,1)S(1)}, u32[]{:S(2)}, u32[]{:S(2)}) collective-permute-start(bf16[256,512]{1,0:T(8,128)(2,1)S(1)} %get-tuple-element.56), channel_id=1, source_target_pairs={{0,8},{4,12},{8,0},{12,4},{16,24},{20,28},{24,16},{28,20},{1,9},{5... | collective-permute-start | bytes 786440 | tf_op jit(solution)/shard_map/ppermute | solution.py:19
  27.6 0.6 %collective-permute-start.4 = (bf16[256,512]{1,0:T(8,128)(2,1)S(1)}, bf16[256,512]{1,0:T(8,128)(2,1)S(1)}, u32[]{:S(2)}, u32[]{:S(2)}) collective-permute-start(bf16[256,512]{1,0:T(8,128)(2,1)S(1)} %get-tuple-element.41), channel_id=1, source_target_pairs={{0,16},{4,20},{8,24},{12,28},{16,0},{20,4},{24,8},{28,12},{1,17},{... | collective-permute-start | bytes 786440 | tf_op jit(solution)/shard_map/ppermute | solution.py:19
  28.3 1.4 %collective-permute-start.5 = (bf16[256,512]{1,0:T(8,128)(2,1)S(1)}, bf16[256,512]{1,0:T(8,128)(2,1)S(1)}, u32[]{:S(2)}, u32[]{:S(2)}) collective-permute-start(bf16[256,512]{1,0:T(8,128)(2,1)S(1)} %get-tuple-element.42), channel_id=1, source_target_pairs={{0,24},{4,28},{8,16},{12,20},{16,8},{20,12},{24,0},{28,4},{1,25},{... | collective-permute-start | bytes 786440 | tf_op jit(solution)/shard_map/ppermute | solution.py:19
  29.9 5.5 %collective-permute-done.12.refs_0_ = bf16[256,512]{1,0:T(8,128)(2,1)S(1)} collective-permute-done((bf16[256,512]{1,0:T(8,128)(2,1)S(1)}, bf16[256,512]{1,0:T(8,128)(2,1)S(1)}, u32[]{:S(2)}, u32[]{:S(2)}) %collective-permute-start.12) | collective-permute-done | bytes 262176 | tf_op jit(solution)/shard_map/ppermute | solution.py:19
  35.4 3.2 %shard_map.72.rest_4_ = bf16[1024,512]{1,0:T(8,128)(2,1)} custom-call(s32[1]{0:T(128)} %bitcast.me, s32[1]{0:T(128)} %bitcast.1.z, s32[8,128]{1,0:T(8,128)S(1)} %bitcast.3, bf16[256,512]{1,0:T(8,128)(2,1)S(1)} %get-tuple-element.49.rest_0_, bf16[256,512]{1,0:T(8,128)(2,1)S(1)} %shard_map.71.rest_1_, bf16[2048,512]{1,0:T(8,128)(2,1)S(1)} %shard_map.70.rest_2_, ...), custom_call_target="tpu_custom_call" | custom-call | flops 2147483648 | bytes 4194304 | tf_op jit(solution)/shard_map/pallas_call | solution.py:45
  38.6 2.0 %collective-permute-done.4.rest_0_ = bf16[256,512]{1,0:T(8,128)(2,1)S(1)} collective-permute-done((bf16[256,512]{1,0:T(8,128)(2,1)S(1)}, bf16[256,512]{1,0:T(8,128)(2,1)S(1)}, u32[]{:S(2)}, u32[]{:S(2)}) %collective-permute-start.4) | collective-permute-done | bytes 262176 | tf_op jit(solution)/shard_map/ppermute | solution.py:19
  40.7 3.2 %shard_map.73 = bf16[1024,512]{1,0:T(8,128)(2,1)} custom-call(s32[1]{0:T(128)} %bitcast.me, s32[1]{0:T(128)} %bitcast.1.z, s32[8,128]{1,0:T(8,128)S(1)} %bitcast.4, bf16[256,512]{1,0:T(8,128)(2,1)S(1)} %collective-permute-done.4.rest_0_, bf16[256,512]{1,0:T(8,128)(2,1)S(1)} %collective-permute-done.5.rest_1_, ...), custom_call_target="tpu_custom_call", output_to_operand_aliasing={{}: (7, {})} | custom-call | flops 2147483648 | bytes 4194304 | tf_op jit(solution)/shard_map/pallas_call | solution.py:45
  (14 shorter events, 0.5 us)
Async XLA Ops:
  0.0 5.7 %collective-permute-start = (bf16[1024,512]{1,0:T(8,128)(2,1)}, bf16[1024,512]{1,0:T(8,128)(2,1)S(1)}, u32[]{:S(2)}, u32[]{:S(2)}) collective-permute-start(bf16[1024,512]{1,0:T(8,128)(2,1)} %interface.1), channel_id=1, source_target_pairs={{0,4},{4,0},{8,12},{12,8},{16,20},{20,16},{24,28},{28,24},{1,5},{5... | collective-permute-start | bytes 3145736 | tf_op jit(solution)/shard_map/ppermute | solution.py:19
  1.6 10.9 %collective-permute-start.6 = (bf16[256,512]{1,0:T(8,128)(2,1)S(1)}, bf16[256,512]{1,0:T(8,128)(2,1)S(1)}, u32[]{:S(2)}, u32[]{:S(2)}) collective-permute-start(bf16[256,512]{1,0:T(8,128)(2,1)S(1)} %get-tuple-element.50.refs_0_), channel_id=1, source_target_pairs={{0,8},{4,12},{8,0},{12,4},{16,24},{20,28},{24,16},{28,20},{1,9},{5... | collective-permute-start | bytes 786440 | tf_op jit(solution)/shard_map/ppermute | solution.py:19
  4.2 9.1 %collective-permute-start.7 = (bf16[256,512]{1,0:T(8,128)(2,1)S(1)}, bf16[256,512]{1,0:T(8,128)(2,1)S(1)}, u32[]{:S(2)}, u32[]{:S(2)}) collective-permute-start(bf16[256,512]{1,0:T(8,128)(2,1)S(1)} %get-tuple-element.51.refs_1_), channel_id=1, source_target_pairs={{0,16},{4,20},{8,24},{12,28},{16,0},{20,4},{24,8},{28,12},{1,17},{... | collective-permute-start | bytes 786440 | tf_op jit(solution)/shard_map/ppermute | solution.py:19
  8.9 9.2 %collective-permute-start.3 = (bf16[256,512]{1,0:T(8,128)(2,1)S(1)}, bf16[256,512]{1,0:T(8,128)(2,1)S(1)}, u32[]{:S(2)}, u32[]{:S(2)}) collective-permute-start(bf16[256,512]{1,0:T(8,128)(2,1)S(1)} %get-tuple-element.34), channel_id=1, source_target_pairs={{0,8},{4,12},{8,0},{12,4},{16,24},{20,28},{24,16},{28,20},{1,9},{5... | collective-permute-start | bytes 786440 | tf_op jit(solution)/shard_map/ppermute | solution.py:19
  9.5 14.3 %collective-permute-start.1 = (bf16[256,512]{1,0:T(8,128)(2,1)S(1)}, bf16[256,512]{1,0:T(8,128)(2,1)S(1)}, u32[]{:S(2)}, u32[]{:S(2)}) collective-permute-start(bf16[256,512]{1,0:T(8,128)(2,1)S(1)} %get-tuple-element.31), channel_id=1, source_target_pairs={{0,16},{4,20},{8,24},{12,28},{16,0},{20,4},{24,8},{28,12},{1,17},{... | collective-permute-start | bytes 786440 | tf_op jit(solution)/shard_map/ppermute | solution.py:19
  10.7 13.4 %collective-permute-start.2 = (bf16[256,512]{1,0:T(8,128)(2,1)S(1)}, bf16[256,512]{1,0:T(8,128)(2,1)S(1)}, u32[]{:S(2)}, u32[]{:S(2)}) collective-permute-start(bf16[256,512]{1,0:T(8,128)(2,1)S(1)} %get-tuple-element.32), channel_id=1, source_target_pairs={{0,24},{4,28},{8,16},{12,20},{16,8},{20,12},{24,0},{28,4},{1,25},{... | collective-permute-start | bytes 786440 | tf_op jit(solution)/shard_map/ppermute | solution.py:19
  13.3 14.9 %collective-permute-start.8 = (bf16[512,512]{1,0:T(8,128)(2,1)S(1)}, bf16[512,512]{1,0:T(8,128)(2,1)S(1)}, u32[]{:S(2)}, u32[]{:S(2)}) collective-permute-start(bf16[512,512]{1,0:T(8,128)(2,1)S(1)} %shard_map.69.refs_2_), channel_id=1, source_target_pairs={{0,1},{1,0},{2,3},{3,2},{4,5},{5,4},{6,7},{7,6},{8,9},{9,8},{10,11... | collective-permute-start | bytes 1572872 | tf_op jit(solution)/shard_map/ppermute | solution.py:19
  19.0 10.7 %collective-permute-start.9 = (bf16[256,512]{1,0:T(8,128)(2,1)S(1)}, bf16[256,512]{1,0:T(8,128)(2,1)S(1)}, u32[]{:S(2)}, u32[]{:S(2)}) collective-permute-start(bf16[256,512]{1,0:T(8,128)(2,1)S(1)} %collective-permute-done.6.refs_0_), channel_id=1, source_target_pairs={{0,16},{4,20},{8,24},{12,28},{16,0},{20,4},{24,8},{28,12},{1,17},{... | collective-permute-start | bytes 786440 | tf_op jit(solution)/shard_map/ppermute | solution.py:19
  19.8 9.9 %collective-permute-start.10 = (bf16[256,512]{1,0:T(8,128)(2,1)S(1)}, bf16[256,512]{1,0:T(8,128)(2,1)S(1)}, u32[]{:S(2)}, u32[]{:S(2)}) collective-permute-start(bf16[256,512]{1,0:T(8,128)(2,1)S(1)} %collective-permute-done.7.refs_1_), channel_id=1, source_target_pairs={{0,8},{4,12},{8,0},{12,4},{16,24},{20,28},{24,16},{28,20},{1,9},{5... | collective-permute-start | bytes 786440 | tf_op jit(solution)/shard_map/ppermute | solution.py:19
  26.1 9.3 %collective-permute-start.12 = (bf16[256,512]{1,0:T(8,128)(2,1)S(1)}, bf16[256,512]{1,0:T(8,128)(2,1)S(1)}, u32[]{:S(2)}, u32[]{:S(2)}) collective-permute-start(bf16[256,512]{1,0:T(8,128)(2,1)S(1)} %get-tuple-element.56), channel_id=1, source_target_pairs={{0,8},{4,12},{8,0},{12,4},{16,24},{20,28},{24,16},{28,20},{1,9},{5... | collective-permute-start | bytes 786440 | tf_op jit(solution)/shard_map/ppermute | solution.py:19
  27.6 13.1 %collective-permute-start.4 = (bf16[256,512]{1,0:T(8,128)(2,1)S(1)}, bf16[256,512]{1,0:T(8,128)(2,1)S(1)}, u32[]{:S(2)}, u32[]{:S(2)}) collective-permute-start(bf16[256,512]{1,0:T(8,128)(2,1)S(1)} %get-tuple-element.41), channel_id=1, source_target_pairs={{0,16},{4,20},{8,24},{12,28},{16,0},{20,4},{24,8},{28,12},{1,17},{... | collective-permute-start | bytes 786440 | tf_op jit(solution)/shard_map/ppermute | solution.py:19
  28.3 12.4 %collective-permute-start.5 = (bf16[256,512]{1,0:T(8,128)(2,1)S(1)}, bf16[256,512]{1,0:T(8,128)(2,1)S(1)}, u32[]{:S(2)}, u32[]{:S(2)}) collective-permute-start(bf16[256,512]{1,0:T(8,128)(2,1)S(1)} %get-tuple-element.42), channel_id=1, source_target_pairs={{0,24},{4,28},{8,16},{12,20},{16,8},{20,12},{24,0},{28,4},{1,25},{... | collective-permute-start | bytes 786440 | tf_op jit(solution)/shard_map/ppermute | solution.py:19
  29.8 5.6 %copy-start = (s32[1024,1]{0,1:T(1,128)S(1)}, s32[1024,1]{0,1:T(1,128)}, u32[]{:S(2)}) copy-start(s32[1024,1]{0,1:T(1,128)} %param.7) | copy-start | bytes 12292
  29.8 5.6 %collective-permute-start.11 = (bf16[2048,512]{1,0:T(8,128)(2,1)S(1)}, bf16[2048,512]{1,0:T(8,128)(2,1)S(1)}, u32[]{:S(2)}, u32[]{:S(2)}) collective-permute-start(bf16[2048,512]{1,0:T(8,128)(2,1)S(1)} %shard_map.70.rest_2_), channel_id=1, source_target_pairs={{0,4},{4,0},{8,12},{12,8},{16,20},{20,16},{24,28},{28,24},{1,5},{5... | collective-permute-start | bytes 6291464 | tf_op jit(solution)/shard_map/ppermute | solution.py:19

commit v8 on v7

--- a/solution.py
+++ b/solution.py
@@ -124,19 +124,25 @@
         at += part.shape[0]
 
 
+def named(me, owners, out):
+    lanes = owners.shape[1]
+    groups = owners.shape[0] // 4
+    diagonal = lax.broadcasted_iota(jnp.int32, (lanes, lanes), 0) == lax.broadcasted_iota(jnp.int32, (lanes, lanes), 1)
+    for m in range(4):
+        block = owners[pl.ds((((me[0] >> 1) & 3) ^ m) * groups, groups), :] ^ me[0]
+        for i in range(groups):
+            column = jnp.sum(jnp.where(diagonal, block[i : i + 1, :], 0), axis=1, keepdims=True)
+            at = (m * groups + i) * lanes
+            out[at : at + lanes, :] = jnp.broadcast_to(column, (lanes, lanes))
+
+
 def couple(blocks, me, z, owners, *rest):
     n_block = len(blocks)
     xs, packs, (out, held, sems) = rest[:n_block], rest[n_block : n_block + 2], rest[-3:]
     size, features = xs[0].shape
     depth = features // 2
-    lanes = owners.shape[1]
-    groups = size // lanes
-    diagonal = lax.broadcasted_iota(jnp.int32, (lanes, lanes), 0) == lax.broadcasted_iota(jnp.int32, (lanes, lanes), 1)
-    columns_of = []
-    for m in blocks:
-        named = owners[pl.ds((((me[0] >> 1) & 3) ^ m) * groups, groups), :] ^ me[0]
-        columns_of += [jnp.sum(jnp.where(diagonal, named[i : i + 1, :], 0), axis=1, keepdims=True) for i in range(groups)]
-    relative = jnp.concatenate(columns_of, axis=0)
+    wide = jnp.concatenate([owners[m * size : (m + 1) * size, :] for m in blocks], axis=0)
+    relative = jnp.concatenate([wide] * (depth // wide.shape[1]), axis=1)
     parts = [half_rows(z, other, depth) for other in range(2)]
     values = [jnp.concatenate([x[:, part] for x in xs], axis=0) for part in parts]
     copies = []
@@ -267,6 +273,9 @@
     *returned, = call(passed, [part] * len(returned), 1 << 36, [VMEM] * len(returned), *returned)
     for m, rows_back in zip((1,), returned):
         back[m] = rows_back
+    (relative,) = call(
+        named, [(jax.ShapeDtypeStruct((rows, 128), jnp.int32), VMEM)], 1, [SMEM, VMEM], me, after(owners.reshape(-1, 128), done[0])
+    )
     out = None
     for blocks in ((0, 1), (2, 3)):
         extra = [] if out is None else [out]
@@ -278,7 +287,7 @@
             [SMEM] * 2 + [VMEM] * (1 + n_block + len(matrices)) + [HBM] * len(extra),
             me,
             z,
-            owners.reshape(-1, 128),
+            relative,
             *(back[m] for m in blocks),
             *matrices,
             *extra,

time: 44.1 us -> 44 us (level)
    pallas_call x10 -> x11, Pallas kernels: 15.4 us -> 15.6 us  [call(): pl.pallas_call(body, out_shape=[shape for shape, _ in outs], in_specs=spe...]
where the time goes in v8:
time: 44 us; the launch traced here: 43.8 us
  starting transfers between devices  15.7 us (36%)
  Pallas kernels  15.6 us (35%)
  waiting for transfers between devices  12.4 us (28%)
    ppermute x13, starting transfers between devices, swapped(): return lax.ppermute(value, axis, pairs)  15.7 us
    pallas_call x11, Pallas kernels, call(): pl.pallas_call(body, out_shape=[shape for shape, _ in outs], in_specs=spe...  15.6 us
    ppermute x13, waiting for transfers between devices, swapped(): return lax.ppermute(value, axis, pairs)  12.4 us
  transfers between devices with their start and end apart: 13, of which 6 were waited for; matrix products, arithmetic and copies ran while one was open for 0% of the time, Pallas kernels for 28%

profile of v8, /device:TPU:0, one launch (start us, length us, event | category | flops | bytes accessed | tf_op | source)
XLA Modules:
  0.0 43.8 jit_solution(2435014254779172558)
XLA Ops:
  0.0 0.5 %collective-permute-start = (bf16[1024,512]{1,0:T(8,128)(2,1)}, bf16[1024,512]{1,0:T(8,128)(2,1)S(1)}, u32[]{:S(2)}, u32[]{:S(2)}) collective-permute-start(bf16[1024,512]{1,0:T(8,128)(2,1)} %interface.1), channel_id=1, source_target_pairs={{0,4},{4,0},{8,12},{12,8},{16,20},{20,16},{24,28},{28,24},{1,5},{5... | collective-permute-start | bytes 3145736 | tf_op jit(solution)/shard_map/ppermute | solution.py:19
  0.5 1.1 %shard_map.69 = (bf16[256,512]{1,0:T(8,128)(2,1)S(1)}, bf16[256,512]{1,0:T(8,128)(2,1)S(1)}) custom-call(s32[1]{0:T(128)} %bitcast.1.z, bf16[1,512,512]{2,1,0:T(8,128)(2,1)} %coupling.1, s32[1,8,8]{2,1,0:T(8,128)} %pattern.1), custom_call_target="tpu_custom_call" | custom-call | flops 1 | tf_op jit(solution)/shard_map/pallas_call | solution.py:45
  1.6 2.6 %collective-permute-start.6 = (bf16[256,512]{1,0:T(8,128)(2,1)S(1)}, bf16[256,512]{1,0:T(8,128)(2,1)S(1)}, u32[]{:S(2)}, u32[]{:S(2)}) collective-permute-start(bf16[256,512]{1,0:T(8,128)(2,1)S(1)} %get-tuple-element.52.refs_0_), channel_id=1, source_target_pairs={{0,8},{4,12},{8,0},{12,4},{16,24},{20,28},{24,16},{28,20},{1,9},{5... | collective-permute-start | bytes 786440 | tf_op jit(solution)/shard_map/ppermute | solution.py:19
  4.2 1.5 %collective-permute-start.7 = (bf16[256,512]{1,0:T(8,128)(2,1)S(1)}, bf16[256,512]{1,0:T(8,128)(2,1)S(1)}, u32[]{:S(2)}, u32[]{:S(2)}) collective-permute-start(bf16[256,512]{1,0:T(8,128)(2,1)S(1)} %get-tuple-element.53.refs_1_), channel_id=1, source_target_pairs={{0,16},{4,20},{8,24},{12,28},{16,0},{20,4},{24,8},{28,12},{1,17},{... | collective-permute-start | bytes 786440 | tf_op jit(solution)/shard_map/ppermute | solution.py:19
  5.7 3.3 %shard_map.64 = (bf16[256,512]{1,0:T(8,128)(2,1)S(1)}, bf16[256,512]{1,0:T(8,128)(2,1)S(1)}, bf16[256,512]{1,0:T(8,128)(2,1)S(1)}, bf16[256,512]{1,0:T(8,128)(2,1)S(1)}) custom-call(s32[1]{0:T(128)} %bitcast.me, bf16[1024,512]{1,0:T(8,128)(2,1)S(1)} %collective-permute-done.sibling, bf16[1024,512]{1,0:T(8,128)(2,1)} %interface.1, bf16[3,512,512]{2,1,0:T(8,128)(2,1)} %keep.2, ...), custom_call_target="tpu_custom_call" | custom-call | flops 536870912 | bytes 1048576 | tf_op jit(solution)/shard_map/pallas_call | solution.py:45
  8.9 0.6 %collective-permute-start.3 = (bf16[256,512]{1,0:T(8,128)(2,1)S(1)}, bf16[256,512]{1,0:T(8,128)(2,1)S(1)}, u32[]{:S(2)}, u32[]{:S(2)}) collective-permute-start(bf16[256,512]{1,0:T(8,128)(2,1)S(1)} %get-tuple-element.35), channel_id=1, source_target_pairs={{0,8},{4,12},{8,0},{12,4},{16,24},{20,28},{24,16},{28,20},{1,9},{5... | collective-permute-start | bytes 786440 | tf_op jit(solution)/shard_map/ppermute | solution.py:19
  9.5 1.1 %collective-permute-start.1 = (bf16[256,512]{1,0:T(8,128)(2,1)S(1)}, bf16[256,512]{1,0:T(8,128)(2,1)S(1)}, u32[]{:S(2)}, u32[]{:S(2)}) collective-permute-start(bf16[256,512]{1,0:T(8,128)(2,1)S(1)} %get-tuple-element.32), channel_id=1, source_target_pairs={{0,16},{4,20},{8,24},{12,28},{16,0},{20,4},{24,8},{28,12},{1,17},{... | collective-permute-start | bytes 786440 | tf_op jit(solution)/shard_map/ppermute | solution.py:19
  10.7 1.8 %collective-permute-start.2 = (bf16[256,512]{1,0:T(8,128)(2,1)S(1)}, bf16[256,512]{1,0:T(8,128)(2,1)S(1)}, u32[]{:S(2)}, u32[]{:S(2)}) collective-permute-start(bf16[256,512]{1,0:T(8,128)(2,1)S(1)} %get-tuple-element.33), channel_id=1, source_target_pairs={{0,24},{4,28},{8,16},{12,20},{16,8},{20,12},{24,0},{28,4},{1,25},{... | collective-permute-start | bytes 786440 | tf_op jit(solution)/shard_map/ppermute | solution.py:19
  12.5 0.8 %collective-permute-done.7.refs_1_ = bf16[256,512]{1,0:T(8,128)(2,1)S(1)} collective-permute-done((bf16[256,512]{1,0:T(8,128)(2,1)S(1)}, bf16[256,512]{1,0:T(8,128)(2,1)S(1)}, u32[]{:S(2)}, u32[]{:S(2)}) %collective-permute-start.7) | collective-permute-done | bytes 262176 | tf_op jit(solution)/shard_map/ppermute | solution.py:19
  13.3 1.6 %collective-permute-start.8 = (bf16[512,512]{1,0:T(8,128)(2,1)S(1)}, bf16[512,512]{1,0:T(8,128)(2,1)S(1)}, u32[]{:S(2)}, u32[]{:S(2)}) collective-permute-start(bf16[512,512]{1,0:T(8,128)(2,1)S(1)} %shard_map.70.refs_2_), channel_id=1, source_target_pairs={{0,1},{1,0},{2,3},{3,2},{4,5},{5,4},{6,7},{7,6},{8,9},{9,8},{10,11... | collective-permute-start | bytes 1572872 | tf_op jit(solution)/shard_map/ppermute | solution.py:19
  15.0 1.6 %shard_map.65 = (bf16[2,512,512]{2,1,0:T(8,128)(2,1)S(1)}, bf16[2,512,512]{2,1,0:T(8,128)(2,1)S(1)}) custom-call(bf16[3,512,512]{2,1,0:T(8,128)(2,1)} %keep.2, bf16[3,512,512]{2,1,0:T(8,128)(2,1)} %cross.2), custom_call_target="tpu_custom_call" | custom-call | flops 1 | tf_op jit(solution)/shard_map/pallas_call | solution.py:45
  16.5 1.6 %collective-permute-done.3.x1 = bf16[256,512]{1,0:T(8,128)(2,1)S(1)} collective-permute-done((bf16[256,512]{1,0:T(8,128)(2,1)S(1)}, bf16[256,512]{1,0:T(8,128)(2,1)S(1)}, u32[]{:S(2)}, u32[]{:S(2)}) %collective-permute-start.3) | collective-permute-done | bytes 262176 | tf_op jit(solution)/shard_map/ppermute | solution.py:19
  18.2 0.8 %shard_map.66 = (bf16[256,512]{1,0:T(8,128)(2,1)S(1)}, bf16[256,512]{1,0:T(8,128)(2,1)S(1)}) custom-call(bf16[256,512]{1,0:T(8,128)(2,1)S(1)} %get-tuple-element.34.x0, bf16[256,512]{1,0:T(8,128)(2,1)S(1)} %collective-permute-done.3.x1, bf16[2,512,512]{2,1,0:T(8,128)(2,1)S(1)} %get-tuple-element.38.keep, bf16[2,512,512]{2,1,0:T(8,128)(2,1)S(1)} %get-tuple-element.39.cross), custom_call_target="tpu_custom_call" | custom-call | flops 1 | tf_op jit(solution)/shard_map/pallas_call | solution.py:45
  19.0 0.8 %collective-permute-start.9 = (bf16[256,512]{1,0:T(8,128)(2,1)S(1)}, bf16[256,512]{1,0:T(8,128)(2,1)S(1)}, u32[]{:S(2)}, u32[]{:S(2)}) collective-permute-start(bf16[256,512]{1,0:T(8,128)(2,1)S(1)} %collective-permute-done.6.refs_0_), channel_id=1, source_target_pairs={{0,16},{4,20},{8,24},{12,28},{16,0},{20,4},{24,8},{28,12},{1,17},{... | collective-permute-start | bytes 786440 | tf_op jit(solution)/shard_map/ppermute | solution.py:19
  19.8 1.5 %collective-permute-start.10 = (bf16[256,512]{1,0:T(8,128)(2,1)S(1)}, bf16[256,512]{1,0:T(8,128)(2,1)S(1)}, u32[]{:S(2)}, u32[]{:S(2)}) collective-permute-start(bf16[256,512]{1,0:T(8,128)(2,1)S(1)} %collective-permute-done.7.refs_1_), channel_id=1, source_target_pairs={{0,8},{4,12},{8,0},{12,4},{16,24},{20,28},{24,16},{28,20},{1,9},{5... | collective-permute-start | bytes 786440 | tf_op jit(solution)/shard_map/ppermute | solution.py:19
  21.3 2.6 %collective-permute-done.1.x2 = bf16[256,512]{1,0:T(8,128)(2,1)S(1)} collective-permute-done((bf16[256,512]{1,0:T(8,128)(2,1)S(1)}, bf16[256,512]{1,0:T(8,128)(2,1)S(1)}, u32[]{:S(2)}, u32[]{:S(2)}) %collective-permute-start.1) | collective-permute-done | bytes 262176 | tf_op jit(solution)/shard_map/ppermute | solution.py:19
  24.0 2.1 %shard_map.67 = (bf16[256,512]{1,0:T(8,128)(2,1)S(1)}, bf16[256,512]{1,0:T(8,128)(2,1)S(1)}, bf16[256,512]{1,0:T(8,128)(2,1)S(1)}, bf16[256,512]{1,0:T(8,128)(2,1)S(1)}) custom-call(bf16[256,512]{1,0:T(8,128)(2,1)S(1)} %collective-permute-done.1.x2, bf16[256,512]{1,0:T(8,128)(2,1)S(1)} %collective-permute-done.2.x3, ...), custom_call_target="tpu_custom_call" | custom-call | flops 17179869184 | bytes 33554432 | tf_op jit(solution)/shard_map/pallas_call | solution.py:45
  26.1 1.6 %collective-permute-start.12 = (bf16[256,512]{1,0:T(8,128)(2,1)S(1)}, bf16[256,512]{1,0:T(8,128)(2,1)S(1)}, u32[]{:S(2)}, u32[]{:S(2)}) collective-permute-start(bf16[256,512]{1,0:T(8,128)(2,1)S(1)} %get-tuple-element.58), channel_id=1, source_target_pairs={{0,8},{4,12},{8,0},{12,4},{16,24},{20,28},{24,16},{28,20},{1,9},{5... | collective-permute-start | bytes 786440 | tf_op jit(solution)/shard_map/ppermute | solution.py:19
  27.6 0.6 %collective-permute-start.4 = (bf16[256,512]{1,0:T(8,128)(2,1)S(1)}, bf16[256,512]{1,0:T(8,128)(2,1)S(1)}, u32[]{:S(2)}, u32[]{:S(2)}) collective-permute-start(bf16[256,512]{1,0:T(8,128)(2,1)S(1)} %get-tuple-element.44), channel_id=1, source_target_pairs={{0,16},{4,20},{8,24},{12,28},{16,0},{20,4},{24,8},{28,12},{1,17},{... | collective-permute-start | bytes 786440 | tf_op jit(solution)/shard_map/ppermute | solution.py:19
  28.6 1.5 %collective-permute-start.5 = (bf16[256,512]{1,0:T(8,128)(2,1)S(1)}, bf16[256,512]{1,0:T(8,128)(2,1)S(1)}, u32[]{:S(2)}, u32[]{:S(2)}) collective-permute-start(bf16[256,512]{1,0:T(8,128)(2,1)S(1)} %get-tuple-element.45), channel_id=1, source_target_pairs={{0,24},{4,28},{8,16},{12,20},{16,8},{20,12},{24,0},{28,4},{1,25},{... | collective-permute-start | bytes 786440 | tf_op jit(solution)/shard_map/ppermute | solution.py:19
  30.3 5.1 %collective-permute-done.12.refs_0_ = bf16[256,512]{1,0:T(8,128)(2,1)S(1)} collective-permute-done((bf16[256,512]{1,0:T(8,128)(2,1)S(1)}, bf16[256,512]{1,0:T(8,128)(2,1)S(1)}, u32[]{:S(2)}, u32[]{:S(2)}) %collective-permute-start.12) | collective-permute-done | bytes 262176 | tf_op jit(solution)/shard_map/ppermute | solution.py:19
  35.4 3.1 %shard_map.73.rest_4_ = bf16[1024,512]{1,0:T(8,128)(2,1)} custom-call(s32[1]{0:T(128)} %bitcast.me, s32[1]{0:T(128)} %bitcast.1.z, s32[1024,128]{1,0:T(8,128)S(1)} %shard_map.68.owners, bf16[256,512]{1,0:T(8,128)(2,1)S(1)} %get-tuple-element.42.rest_0_, bf16[256,512]{1,0:T(8,128)(2,1)S(1)} %shard_map.72.rest_1_, bf16[2048,512]{1,0:T(8,128)(2,1)S(1)} %shard_map.71.rest_2_, ...), custom_call_target="tpu_custom_call" | custom-call | flops 2147483648 | bytes 4194304 | tf_op jit(solution)/shard_map/pallas_call | solution.py:45
  38.5 2.1 %collective-permute-done.4.rest_0_ = bf16[256,512]{1,0:T(8,128)(2,1)S(1)} collective-permute-done((bf16[256,512]{1,0:T(8,128)(2,1)S(1)}, bf16[256,512]{1,0:T(8,128)(2,1)S(1)}, u32[]{:S(2)}, u32[]{:S(2)}) %collective-permute-start.4) | collective-permute-done | bytes 262176 | tf_op jit(solution)/shard_map/ppermute | solution.py:19
  40.7 3.1 %shard_map.74 = bf16[1024,512]{1,0:T(8,128)(2,1)} custom-call(s32[1]{0:T(128)} %bitcast.me, s32[1]{0:T(128)} %bitcast.1.z, s32[1024,128]{1,0:T(8,128)S(1)} %shard_map.68.owners, bf16[256,512]{1,0:T(8,128)(2,1)S(1)} %collective-permute-done.4.rest_0_, bf16[256,512]{1,0:T(8,128)(2,1)S(1)} %collective-permute-done.5.rest_1_, ...), custom_call_target="tpu_custom_call", output_to_operand_aliasing={{}: (7, {})} | custom-call | flops 2147483648 | bytes 4194304 | tf_op jit(solution)/shard_map/pallas_call | solution.py:45
  (15 shorter events, 0.8 us)
Async XLA Ops:
  0.0 5.7 %collective-permute-start = (bf16[1024,512]{1,0:T(8,128)(2,1)}, bf16[1024,512]{1,0:T(8,128)(2,1)S(1)}, u32[]{:S(2)}, u32[]{:S(2)}) collective-permute-start(bf16[1024,512]{1,0:T(8,128)(2,1)} %interface.1), channel_id=1, source_target_pairs={{0,4},{4,0},{8,12},{12,8},{16,20},{20,16},{24,28},{28,24},{1,5},{5... | collective-permute-start | bytes 3145736 | tf_op jit(solution)/shard_map/ppermute | solution.py:19
  1.6 10.9 %collective-permute-start.6 = (bf16[256,512]{1,0:T(8,128)(2,1)S(1)}, bf16[256,512]{1,0:T(8,128)(2,1)S(1)}, u32[]{:S(2)}, u32[]{:S(2)}) collective-permute-start(bf16[256,512]{1,0:T(8,128)(2,1)S(1)} %get-tuple-element.52.refs_0_), channel_id=1, source_target_pairs={{0,8},{4,12},{8,0},{12,4},{16,24},{20,28},{24,16},{28,20},{1,9},{5... | collective-permute-start | bytes 786440 | tf_op jit(solution)/shard_map/ppermute | solution.py:19
  4.2 9.1 %collective-permute-start.7 = (bf16[256,512]{1,0:T(8,128)(2,1)S(1)}, bf16[256,512]{1,0:T(8,128)(2,1)S(1)}, u32[]{:S(2)}, u32[]{:S(2)}) collective-permute-start(bf16[256,512]{1,0:T(8,128)(2,1)S(1)} %get-tuple-element.53.refs_1_), channel_id=1, source_target_pairs={{0,16},{4,20},{8,24},{12,28},{16,0},{20,4},{24,8},{28,12},{1,17},{... | collective-permute-start | bytes 786440 | tf_op jit(solution)/shard_map/ppermute | solution.py:19
  8.9 9.2 %collective-permute-start.3 = (bf16[256,512]{1,0:T(8,128)(2,1)S(1)}, bf16[256,512]{1,0:T(8,128)(2,1)S(1)}, u32[]{:S(2)}, u32[]{:S(2)}) collective-permute-start(bf16[256,512]{1,0:T(8,128)(2,1)S(1)} %get-tuple-element.35), channel_id=1, source_target_pairs={{0,8},{4,12},{8,0},{12,4},{16,24},{20,28},{24,16},{28,20},{1,9},{5... | collective-permute-start | bytes 786440 | tf_op jit(solution)/shard_map/ppermute | solution.py:19
  9.5 14.3 %collective-permute-start.1 = (bf16[256,512]{1,0:T(8,128)(2,1)S(1)}, bf16[256,512]{1,0:T(8,128)(2,1)S(1)}, u32[]{:S(2)}, u32[]{:S(2)}) collective-permute-start(bf16[256,512]{1,0:T(8,128)(2,1)S(1)} %get-tuple-element.32), channel_id=1, source_target_pairs={{0,16},{4,20},{8,24},{12,28},{16,0},{20,4},{24,8},{28,12},{1,17},{... | collective-permute-start | bytes 786440 | tf_op jit(solution)/shard_map/ppermute | solution.py:19
  10.7 13.4 %collective-permute-start.2 = (bf16[256,512]{1,0:T(8,128)(2,1)S(1)}, bf16[256,512]{1,0:T(8,128)(2,1)S(1)}, u32[]{:S(2)}, u32[]{:S(2)}) collective-permute-start(bf16[256,512]{1,0:T(8,128)(2,1)S(1)} %get-tuple-element.33), channel_id=1, source_target_pairs={{0,24},{4,28},{8,16},{12,20},{16,8},{20,12},{24,0},{28,4},{1,25},{... | collective-permute-start | bytes 786440 | tf_op jit(solution)/shard_map/ppermute | solution.py:19
  13.3 15.3 %collective-permute-start.8 = (bf16[512,512]{1,0:T(8,128)(2,1)S(1)}, bf16[512,512]{1,0:T(8,128)(2,1)S(1)}, u32[]{:S(2)}, u32[]{:S(2)}) collective-permute-start(bf16[512,512]{1,0:T(8,128)(2,1)S(1)} %shard_map.70.refs_2_), channel_id=1, source_target_pairs={{0,1},{1,0},{2,3},{3,2},{4,5},{5,4},{6,7},{7,6},{8,9},{9,8},{10,11... | collective-permute-start | bytes 1572872 | tf_op jit(solution)/shard_map/ppermute | solution.py:19
  19.0 11.1 %collective-permute-start.9 = (bf16[256,512]{1,0:T(8,128)(2,1)S(1)}, bf16[256,512]{1,0:T(8,128)(2,1)S(1)}, u32[]{:S(2)}, u32[]{:S(2)}) collective-permute-start(bf16[256,512]{1,0:T(8,128)(2,1)S(1)} %collective-permute-done.6.refs_0_), channel_id=1, source_target_pairs={{0,16},{4,20},{8,24},{12,28},{16,0},{20,4},{24,8},{28,12},{1,17},{... | collective-permute-start | bytes 786440 | tf_op jit(solution)/shard_map/ppermute | solution.py:19
  19.8 10.3 %collective-permute-start.10 = (bf16[256,512]{1,0:T(8,128)(2,1)S(1)}, bf16[256,512]{1,0:T(8,128)(2,1)S(1)}, u32[]{:S(2)}, u32[]{:S(2)}) collective-permute-start(bf16[256,512]{1,0:T(8,128)(2,1)S(1)} %collective-permute-done.7.refs_1_), channel_id=1, source_target_pairs={{0,8},{4,12},{8,0},{12,4},{16,24},{20,28},{24,16},{28,20},{1,9},{5... | collective-permute-start | bytes 786440 | tf_op jit(solution)/shard_map/ppermute | solution.py:19
  24.0 4.3 %copy-start = (s32[1024,1]{0,1:T(1,128)S(1)}, s32[1024,1]{0,1:T(1,128)}, u32[]{:S(2)}) copy-start(s32[1024,1]{0,1:T(1,128)} %param.7) | copy-start | bytes 12292
  26.1 9.3 %collective-permute-start.12 = (bf16[256,512]{1,0:T(8,128)(2,1)S(1)}, bf16[256,512]{1,0:T(8,128)(2,1)S(1)}, u32[]{:S(2)}, u32[]{:S(2)}) collective-permute-start(bf16[256,512]{1,0:T(8,128)(2,1)S(1)} %get-tuple-element.58), channel_id=1, source_target_pairs={{0,8},{4,12},{8,0},{12,4},{16,24},{20,28},{24,16},{28,20},{1,9},{5... | collective-permute-start | bytes 786440 | tf_op jit(solution)/shard_map/ppermute | solution.py:19
  27.6 13.1 %collective-permute-start.4 = (bf16[256,512]{1,0:T(8,128)(2,1)S(1)}, bf16[256,512]{1,0:T(8,128)(2,1)S(1)}, u32[]{:S(2)}, u32[]{:S(2)}) collective-permute-start(bf16[256,512]{1,0:T(8,128)(2,1)S(1)} %get-tuple-element.44), channel_id=1, source_target_pairs={{0,16},{4,20},{8,24},{12,28},{16,0},{20,4},{24,8},{28,12},{1,17},{... | collective-permute-start | bytes 786440 | tf_op jit(solution)/shard_map/ppermute | solution.py:19
  28.6 12.1 %collective-permute-start.5 = (bf16[256,512]{1,0:T(8,128)(2,1)S(1)}, bf16[256,512]{1,0:T(8,128)(2,1)S(1)}, u32[]{:S(2)}, u32[]{:S(2)}) collective-permute-start(bf16[256,512]{1,0:T(8,128)(2,1)S(1)} %get-tuple-element.45), channel_id=1, source_target_pairs={{0,24},{4,28},{8,16},{12,20},{16,8},{20,12},{24,0},{28,4},{1,25},{... | collective-permute-start | bytes 786440 | tf_op jit(solution)/shard_map/ppermute | solution.py:19
  30.2 5.2 %collective-permute-start.11 = (bf16[2048,512]{1,0:T(8,128)(2,1)S(1)}, bf16[2048,512]{1,0:T(8,128)(2,1)S(1)}, u32[]{:S(2)}, u32[]{:S(2)}) collective-permute-start(bf16[2048,512]{1,0:T(8,128)(2,1)S(1)} %shard_map.71.rest_2_), channel_id=1, source_target_pairs={{0,4},{4,0},{8,12},{12,8},{16,20},{20,16},{24,28},{28,24},{1,5},{5... | collective-permute-start | bytes 6291464 | tf_op jit(solution)/shard_map/ppermute | solution.py:19

commit v9 on v8

--- a/solution.py
+++ b/solution.py
@@ -82,18 +82,20 @@
         outs[m][...] = normal(jnp.dot(own[rows, :], keep_here[...], preferred_element_type=jnp.float32) + term)
 
 
-def second_level(x0, x1, keep, cross, out0, out1):
-    out0[...] = mixed(x0[...], x1[...], keep[0], cross[0])
-    out1[...] = mixed(x1[...], x0[...], keep[0], cross[0])
-
-
-def third_level(x2, x3, y0, y1, keep, cross, *outs):
+def second_level(x0, x1, keep, cross, *outs):
+    y = mixed(x0[...], x1[...], keep[0], cross[0]), mixed(x1[...], x0[...], keep[0], cross[0])
+    for m in range(2):
+        outs[m][...] = jnp.dot(y[m], keep[1], preferred_element_type=jnp.float32)
+        outs[m + 2][...] = jnp.dot(y[m], cross[1], preferred_element_type=jnp.float32)
+
+
+def third_level(x2, x3, term0, term1, term2, term3, keep, cross, *outs):
     y2 = mixed(x2[...], x3[...], keep[0], cross[0])
     y3 = mixed(x3[...], x2[...], keep[0], cross[0])
-    outs[1][...] = mixed(y1[...], y3, keep[1], cross[1])
-    outs[2][...] = mixed(y2, y0[...], keep[1], cross[1])
-    outs[3][...] = mixed(y3, y1[...], keep[1], cross[1])
-    outs[0][...] = mixed(y0[...], y2, keep[1], cross[1])
+    outs[1][...] = normal(term1[...] + jnp.dot(y3, cross[1], preferred_element_type=jnp.float32))
+    outs[2][...] = normal(jnp.dot(y2, keep[1], preferred_element_type=jnp.float32) + term2[...])
+    outs[3][...] = normal(jnp.dot(y3, keep[1], preferred_element_type=jnp.float32) + term3[...])
+    outs[0][...] = normal(term0[...] + jnp.dot(y2, cross[1], preferred_element_type=jnp.float32))
 
 
 def masked_coupling(z, coupling, pattern, part, rest, held, shown, sems):
@@ -253,13 +255,14 @@
         *(in_hbm(w) for w in together(keep_proj, sibling_proj, sent[0])[:2]),
         scratch=[pltpu.SemaphoreType.DMA((2,))],
     )
-    y0, y1 = call(second_level, [part] * 2, 1, [VMEM] * 4, x[0], x[1], *weights)
+    term = jax.ShapeDtypeStruct((quarter, features), jnp.float32), VMEM
+    terms = call(second_level, [term] * 4, 1, [VMEM] * 4, x[0], x[1], *weights)
     if few:
         x_mine, y_other, _ = together(*near, sent[0])
         (pack_near,) = call(packed, [array(2 * depth, features)], 1, [VMEM] * 2, x_mine, y_other)
         pack_far = swapped(pack_near, 1, "blk")
-        d_mine, d_other = swapped(after(x_mine, y0), 4), swapped(after(y_other, y0), 2)
-    done = call(third_level, [part] * 4, (1 << 34), [VMEM] * 6, x[2], x[3], y0, y1, *weights)
+        d_mine, d_other = swapped(after(x_mine, x[1]), 4), swapped(after(y_other, x[1]), 2)
+    done = call(third_level, [part] * 4, (1 << 34), [VMEM] * 8, x[2], x[3], *terms, *weights)
     back = [done[0]] + [swapped(done[m], 2 * m) for m in (1, 2, 3)]
     if not few:
         current = jnp.zeros((rows, features), jnp.bfloat16)
@@ -270,7 +273,7 @@
     (pack,) = call(packed, [array(8 * depth, features)], 1, [VMEM] * 6, *together(*pieces, done[0])[:6])
     matrices = [pack, swapped(pack, 1)]
     returned = [back[m] for m in (1,)]
-    *returned, = call(passed, [part] * len(returned), 1 << 36, [VMEM] * len(returned), *returned)
+    *returned, = call(passed, [part] * len(returned), 1 << 35, [VMEM] * len(returned), *returned)
     for m, rows_back in zip((1,), returned):
         back[m] = rows_back
     (relative,) = call(

time: 44 us -> 44 us (level)
  no operation moved by 1% of the time
where the time goes in v9:
time: 44 us; the launch traced here: 43.8 us
  starting transfers between devices  15.7 us (36%)
  Pallas kernels  15.5 us (35%)
  waiting for transfers between devices  12.5 us (28%)
    ppermute x13, starting transfers between devices, swapped(): return lax.ppermute(value, axis, pairs)  15.7 us
    pallas_call x11, Pallas kernels, call(): pl.pallas_call(body, out_shape=[shape for shape, _ in outs], in_specs=spe...  15.5 us
    ppermute x13, waiting for transfers between devices, swapped(): return lax.ppermute(value, axis, pairs)  12.5 us
  transfers between devices with their start and end apart: 13, of which 6 were waited for; matrix products, arithmetic and copies ran while one was open for 0% of the time, Pallas kernels for 28%

profile of v9, /device:TPU:0, one launch (start us, length us, event | category | flops | bytes accessed | tf_op | source)
XLA Modules:
  0.0 43.8 jit_solution(7108763267366630705)
XLA Ops:
  0.0 0.5 %collective-permute-start = (bf16[1024,512]{1,0:T(8,128)(2,1)}, bf16[1024,512]{1,0:T(8,128)(2,1)S(1)}, u32[]{:S(2)}, u32[]{:S(2)}) collective-permute-start(bf16[1024,512]{1,0:T(8,128)(2,1)} %interface.1), channel_id=1, source_target_pairs={{0,4},{4,0},{8,12},{12,8},{16,20},{20,16},{24,28},{28,24},{1,5},{5... | collective-permute-start | bytes 3145736 | tf_op jit(solution)/shard_map/ppermute | solution.py:19
  0.5 1.1 %shard_map.69 = (bf16[256,512]{1,0:T(8,128)(2,1)S(1)}, bf16[256,512]{1,0:T(8,128)(2,1)S(1)}) custom-call(s32[1]{0:T(128)} %bitcast.1.z, bf16[1,512,512]{2,1,0:T(8,128)(2,1)} %coupling.1, s32[1,8,8]{2,1,0:T(8,128)} %pattern.1), custom_call_target="tpu_custom_call" | custom-call | flops 1 | tf_op jit(solution)/shard_map/pallas_call | solution.py:45
  1.6 2.6 %collective-permute-start.6 = (bf16[256,512]{1,0:T(8,128)(2,1)S(1)}, bf16[256,512]{1,0:T(8,128)(2,1)S(1)}, u32[]{:S(2)}, u32[]{:S(2)}) collective-permute-start(bf16[256,512]{1,0:T(8,128)(2,1)S(1)} %get-tuple-element.56.refs_0_), channel_id=1, source_target_pairs={{0,8},{4,12},{8,0},{12,4},{16,24},{20,28},{24,16},{28,20},{1,9},{5... | collective-permute-start | bytes 786440 | tf_op jit(solution)/shard_map/ppermute | solution.py:19
  4.2 1.5 %collective-permute-start.7 = (bf16[256,512]{1,0:T(8,128)(2,1)S(1)}, bf16[256,512]{1,0:T(8,128)(2,1)S(1)}, u32[]{:S(2)}, u32[]{:S(2)}) collective-permute-start(bf16[256,512]{1,0:T(8,128)(2,1)S(1)} %get-tuple-element.57.refs_1_), channel_id=1, source_target_pairs={{0,16},{4,20},{8,24},{12,28},{16,0},{20,4},{24,8},{28,12},{1,17},{... | collective-permute-start | bytes 786440 | tf_op jit(solution)/shard_map/ppermute | solution.py:19
  5.7 3.3 %shard_map.64 = (bf16[256,512]{1,0:T(8,128)(2,1)S(1)}, bf16[256,512]{1,0:T(8,128)(2,1)S(1)}, bf16[256,512]{1,0:T(8,128)(2,1)S(1)}, bf16[256,512]{1,0:T(8,128)(2,1)S(1)}) custom-call(s32[1]{0:T(128)} %bitcast.me, bf16[1024,512]{1,0:T(8,128)(2,1)S(1)} %collective-permute-done.sibling, bf16[1024,512]{1,0:T(8,128)(2,1)} %interface.1, bf16[3,512,512]{2,1,0:T(8,128)(2,1)} %keep.2, ...), custom_call_target="tpu_custom_call" | custom-call | flops 536870912 | bytes 1048576 | tf_op jit(solution)/shard_map/pallas_call | solution.py:45
  8.9 0.6 %collective-permute-start.3 = (bf16[256,512]{1,0:T(8,128)(2,1)S(1)}, bf16[256,512]{1,0:T(8,128)(2,1)S(1)}, u32[]{:S(2)}, u32[]{:S(2)}) collective-permute-start(bf16[256,512]{1,0:T(8,128)(2,1)S(1)} %get-tuple-element.37), channel_id=1, source_target_pairs={{0,8},{4,12},{8,0},{12,4},{16,24},{20,28},{24,16},{28,20},{1,9},{5... | collective-permute-start | bytes 786440 | tf_op jit(solution)/shard_map/ppermute | solution.py:19
  9.5 1.1 %collective-permute-start.1 = (bf16[256,512]{1,0:T(8,128)(2,1)S(1)}, bf16[256,512]{1,0:T(8,128)(2,1)S(1)}, u32[]{:S(2)}, u32[]{:S(2)}) collective-permute-start(bf16[256,512]{1,0:T(8,128)(2,1)S(1)} %get-tuple-element.34), channel_id=1, source_target_pairs={{0,16},{4,20},{8,24},{12,28},{16,0},{20,4},{24,8},{28,12},{1,17},{... | collective-permute-start | bytes 786440 | tf_op jit(solution)/shard_map/ppermute | solution.py:19
  10.7 1.8 %collective-permute-start.2 = (bf16[256,512]{1,0:T(8,128)(2,1)S(1)}, bf16[256,512]{1,0:T(8,128)(2,1)S(1)}, u32[]{:S(2)}, u32[]{:S(2)}) collective-permute-start(bf16[256,512]{1,0:T(8,128)(2,1)S(1)} %get-tuple-element.35), channel_id=1, source_target_pairs={{0,24},{4,28},{8,16},{12,20},{16,8},{20,12},{24,0},{28,4},{1,25},{... | collective-permute-start | bytes 786440 | tf_op jit(solution)/shard_map/ppermute | solution.py:19
  12.5 0.8 %collective-permute-done.7.refs_1_ = bf16[256,512]{1,0:T(8,128)(2,1)S(1)} collective-permute-done((bf16[256,512]{1,0:T(8,128)(2,1)S(1)}, bf16[256,512]{1,0:T(8,128)(2,1)S(1)}, u32[]{:S(2)}, u32[]{:S(2)}) %collective-permute-start.7) | collective-permute-done | bytes 262176 | tf_op jit(solution)/shard_map/ppermute | solution.py:19
  13.3 1.6 %collective-permute-start.8 = (bf16[512,512]{1,0:T(8,128)(2,1)S(1)}, bf16[512,512]{1,0:T(8,128)(2,1)S(1)}, u32[]{:S(2)}, u32[]{:S(2)}) collective-permute-start(bf16[512,512]{1,0:T(8,128)(2,1)S(1)} %shard_map.70.refs_2_), channel_id=1, source_target_pairs={{0,1},{1,0},{2,3},{3,2},{4,5},{5,4},{6,7},{7,6},{8,9},{9,8},{10,11... | collective-permute-start | bytes 1572872 | tf_op jit(solution)/shard_map/ppermute | solution.py:19
  15.0 1.6 %shard_map.65 = (bf16[2,512,512]{2,1,0:T(8,128)(2,1)S(1)}, bf16[2,512,512]{2,1,0:T(8,128)(2,1)S(1)}) custom-call(bf16[3,512,512]{2,1,0:T(8,128)(2,1)} %keep.2, bf16[3,512,512]{2,1,0:T(8,128)(2,1)} %cross.2), custom_call_target="tpu_custom_call" | custom-call | flops 1 | tf_op jit(solution)/shard_map/pallas_call | solution.py:45
  16.5 1.6 %collective-permute-done.3.x1 = bf16[256,512]{1,0:T(8,128)(2,1)S(1)} collective-permute-done((bf16[256,512]{1,0:T(8,128)(2,1)S(1)}, bf16[256,512]{1,0:T(8,128)(2,1)S(1)}, u32[]{:S(2)}, u32[]{:S(2)}) %collective-permute-start.3) | collective-permute-done | bytes 262176 | tf_op jit(solution)/shard_map/ppermute | solution.py:19
  18.2 0.7 %collective-permute-start.10 = (bf16[256,512]{1,0:T(8,128)(2,1)S(1)}, bf16[256,512]{1,0:T(8,128)(2,1)S(1)}, u32[]{:S(2)}, u32[]{:S(2)}) collective-permute-start(bf16[256,512]{1,0:T(8,128)(2,1)S(1)} %collective-permute-done.7.refs_1_), channel_id=1, source_target_pairs={{0,8},{4,12},{8,0},{12,4},{16,24},{20,28},{24,16},{28,20},{1,9},{5... | collective-permute-start | bytes 786440 | tf_op jit(solution)/shard_map/ppermute | solution.py:19
  18.9 1.5 %collective-permute-start.9 = (bf16[256,512]{1,0:T(8,128)(2,1)S(1)}, bf16[256,512]{1,0:T(8,128)(2,1)S(1)}, u32[]{:S(2)}, u32[]{:S(2)}) collective-permute-start(bf16[256,512]{1,0:T(8,128)(2,1)S(1)} %collective-permute-done.6.refs_0_), channel_id=1, source_target_pairs={{0,16},{4,20},{8,24},{12,28},{16,0},{20,4},{24,8},{28,12},{1,17},{... | collective-permute-start | bytes 786440 | tf_op jit(solution)/shard_map/ppermute | solution.py:19
  20.4 1.2 %shard_map.66 = (f32[256,512]{1,0:T(8,128)S(1)}, f32[256,512]{1,0:T(8,128)S(1)}, f32[256,512]{1,0:T(8,128)S(1)}, f32[256,512]{1,0:T(8,128)S(1)}) custom-call(bf16[256,512]{1,0:T(8,128)(2,1)S(1)} %get-tuple-element.36.x0, bf16[256,512]{1,0:T(8,128)(2,1)S(1)} %collective-permute-done.3.x1, bf16[2,512,512]{2,1,0:T(8,128)(2,1)S(1)} %get-tuple-element.40.keep, ...), custom_call_target="tpu_custom_call" | custom-call | flops 1 | tf_op jit(solution)/shard_map/pallas_call | solution.py:45
  21.7 2.2 %collective-permute-done.1.x2 = bf16[256,512]{1,0:T(8,128)(2,1)S(1)} collective-permute-done((bf16[256,512]{1,0:T(8,128)(2,1)S(1)}, bf16[256,512]{1,0:T(8,128)(2,1)S(1)}, u32[]{:S(2)}, u32[]{:S(2)}) %collective-permute-start.1) | collective-permute-done | bytes 262176 | tf_op jit(solution)/shard_map/ppermute | solution.py:19
  24.0 1.5 %shard_map.67 = (bf16[256,512]{1,0:T(8,128)(2,1)S(1)}, bf16[256,512]{1,0:T(8,128)(2,1)S(1)}, bf16[256,512]{1,0:T(8,128)(2,1)S(1)}, bf16[256,512]{1,0:T(8,128)(2,1)S(1)}) custom-call(bf16[256,512]{1,0:T(8,128)(2,1)S(1)} %collective-permute-done.1.x2, bf16[256,512]{1,0:T(8,128)(2,1)S(1)} %collective-permute-done.2.x3, f32[256,512]{1,0:T(8,128)S(1)} %get-tuple-element.42.term0, ...), custom_call_target="tpu_custom_call" | custom-call | flops 17179869184 | bytes 33554432 | tf_op jit(solution)/shard_map/pallas_call | solution.py:45
  25.5 1.6 %collective-permute-start.12 = (bf16[256,512]{1,0:T(8,128)(2,1)S(1)}, bf16[256,512]{1,0:T(8,128)(2,1)S(1)}, u32[]{:S(2)}, u32[]{:S(2)}) collective-permute-start(bf16[256,512]{1,0:T(8,128)(2,1)S(1)} %get-tuple-element.62), channel_id=1, source_target_pairs={{0,8},{4,12},{8,0},{12,4},{16,24},{20,28},{24,16},{28,20},{1,9},{5... | collective-permute-start | bytes 786440 | tf_op jit(solution)/shard_map/ppermute | solution.py:19
  27.5 0.7 %collective-permute-start.4 = (bf16[256,512]{1,0:T(8,128)(2,1)S(1)}, bf16[256,512]{1,0:T(8,128)(2,1)S(1)}, u32[]{:S(2)}, u32[]{:S(2)}) collective-permute-start(bf16[256,512]{1,0:T(8,128)(2,1)S(1)} %get-tuple-element.48), channel_id=1, source_target_pairs={{0,16},{4,20},{8,24},{12,28},{16,0},{20,4},{24,8},{28,12},{1,17},{... | collective-permute-start | bytes 786440 | tf_op jit(solution)/shard_map/ppermute | solution.py:19
  28.1 1.5 %collective-permute-start.5 = (bf16[256,512]{1,0:T(8,128)(2,1)S(1)}, bf16[256,512]{1,0:T(8,128)(2,1)S(1)}, u32[]{:S(2)}, u32[]{:S(2)}) collective-permute-start(bf16[256,512]{1,0:T(8,128)(2,1)S(1)} %get-tuple-element.49), channel_id=1, source_target_pairs={{0,24},{4,28},{8,16},{12,20},{16,8},{20,12},{24,0},{28,4},{1,25},{... | collective-permute-start | bytes 786440 | tf_op jit(solution)/shard_map/ppermute | solution.py:19
  29.9 5.0 %collective-permute-done.12.refs_0_ = bf16[256,512]{1,0:T(8,128)(2,1)S(1)} collective-permute-done((bf16[256,512]{1,0:T(8,128)(2,1)S(1)}, bf16[256,512]{1,0:T(8,128)(2,1)S(1)}, u32[]{:S(2)}, u32[]{:S(2)}) %collective-permute-start.12) | collective-permute-done | bytes 262176 | tf_op jit(solution)/shard_map/ppermute | solution.py:19
  34.9 3.1 %shard_map.73.rest_4_ = bf16[1024,512]{1,0:T(8,128)(2,1)} custom-call(s32[1]{0:T(128)} %bitcast.me, s32[1]{0:T(128)} %bitcast.1.z, s32[1024,128]{1,0:T(8,128)S(1)} %shard_map.68.owners, bf16[256,512]{1,0:T(8,128)(2,1)S(1)} %get-tuple-element.46.rest_0_, bf16[256,512]{1,0:T(8,128)(2,1)S(1)} %shard_map.72.rest_1_, bf16[2048,512]{1,0:T(8,128)(2,1)S(1)} %shard_map.71.rest_2_, ...), custom_call_target="tpu_custom_call" | custom-call | flops 2147483648 | bytes 4194304 | tf_op jit(solution)/shard_map/pallas_call | solution.py:45
  38.1 2.6 %collective-permute-done.4.rest_0_ = bf16[256,512]{1,0:T(8,128)(2,1)S(1)} collective-permute-done((bf16[256,512]{1,0:T(8,128)(2,1)S(1)}, bf16[256,512]{1,0:T(8,128)(2,1)S(1)}, u32[]{:S(2)}, u32[]{:S(2)}) %collective-permute-start.4) | collective-permute-done | bytes 262176 | tf_op jit(solution)/shard_map/ppermute | solution.py:19
  40.7 3.1 %shard_map.74 = bf16[1024,512]{1,0:T(8,128)(2,1)} custom-call(s32[1]{0:T(128)} %bitcast.me, s32[1]{0:T(128)} %bitcast.1.z, s32[1024,128]{1,0:T(8,128)S(1)} %shard_map.68.owners, bf16[256,512]{1,0:T(8,128)(2,1)S(1)} %collective-permute-done.4.rest_0_, bf16[256,512]{1,0:T(8,128)(2,1)S(1)} %collective-permute-done.5.rest_1_, ...), custom_call_target="tpu_custom_call", output_to_operand_aliasing={{}: (7, {})} | custom-call | flops 2147483648 | bytes 4194304 | tf_op jit(solution)/shard_map/pallas_call | solution.py:45
  (15 shorter events, 0.8 us)
Async XLA Ops:
  0.0 5.7 %collective-permute-start = (bf16[1024,512]{1,0:T(8,128)(2,1)}, bf16[1024,512]{1,0:T(8,128)(2,1)S(1)}, u32[]{:S(2)}, u32[]{:S(2)}) collective-permute-start(bf16[1024,512]{1,0:T(8,128)(2,1)} %interface.1), channel_id=1, source_target_pairs={{0,4},{4,0},{8,12},{12,8},{16,20},{20,16},{24,28},{28,24},{1,5},{5... | collective-permute-start | bytes 3145736 | tf_op jit(solution)/shard_map/ppermute | solution.py:19
  1.6 10.9 %collective-permute-start.6 = (bf16[256,512]{1,0:T(8,128)(2,1)S(1)}, bf16[256,512]{1,0:T(8,128)(2,1)S(1)}, u32[]{:S(2)}, u32[]{:S(2)}) collective-permute-start(bf16[256,512]{1,0:T(8,128)(2,1)S(1)} %get-tuple-element.56.refs_0_), channel_id=1, source_target_pairs={{0,8},{4,12},{8,0},{12,4},{16,24},{20,28},{24,16},{28,20},{1,9},{5... | collective-permute-start | bytes 786440 | tf_op jit(solution)/shard_map/ppermute | solution.py:19
  4.2 9.1 %collective-permute-start.7 = (bf16[256,512]{1,0:T(8,128)(2,1)S(1)}, bf16[256,512]{1,0:T(8,128)(2,1)S(1)}, u32[]{:S(2)}, u32[]{:S(2)}) collective-permute-start(bf16[256,512]{1,0:T(8,128)(2,1)S(1)} %get-tuple-element.57.refs_1_), channel_id=1, source_target_pairs={{0,16},{4,20},{8,24},{12,28},{16,0},{20,4},{24,8},{28,12},{1,17},{... | collective-permute-start | bytes 786440 | tf_op jit(solution)/shard_map/ppermute | solution.py:19
  8.9 9.2 %collective-permute-start.3 = (bf16[256,512]{1,0:T(8,128)(2,1)S(1)}, bf16[256,512]{1,0:T(8,128)(2,1)S(1)}, u32[]{:S(2)}, u32[]{:S(2)}) collective-permute-start(bf16[256,512]{1,0:T(8,128)(2,1)S(1)} %get-tuple-element.37), channel_id=1, source_target_pairs={{0,8},{4,12},{8,0},{12,4},{16,24},{20,28},{24,16},{28,20},{1,9},{5... | collective-permute-start | bytes 786440 | tf_op jit(solution)/shard_map/ppermute | solution.py:19
  9.5 14.3 %collective-permute-start.1 = (bf16[256,512]{1,0:T(8,128)(2,1)S(1)}, bf16[256,512]{1,0:T(8,128)(2,1)S(1)}, u32[]{:S(2)}, u32[]{:S(2)}) collective-permute-start(bf16[256,512]{1,0:T(8,128)(2,1)S(1)} %get-tuple-element.34), channel_id=1, source_target_pairs={{0,16},{4,20},{8,24},{12,28},{16,0},{20,4},{24,8},{28,12},{1,17},{... | collective-permute-start | bytes 786440 | tf_op jit(solution)/shard_map/ppermute | solution.py:19
  10.7 13.4 %collective-permute-start.2 = (bf16[256,512]{1,0:T(8,128)(2,1)S(1)}, bf16[256,512]{1,0:T(8,128)(2,1)S(1)}, u32[]{:S(2)}, u32[]{:S(2)}) collective-permute-start(bf16[256,512]{1,0:T(8,128)(2,1)S(1)} %get-tuple-element.35), channel_id=1, source_target_pairs={{0,24},{4,28},{8,16},{12,20},{16,8},{20,12},{24,0},{28,4},{1,25},{... | collective-permute-start | bytes 786440 | tf_op jit(solution)/shard_map/ppermute | solution.py:19
  13.3 14.8 %collective-permute-start.8 = (bf16[512,512]{1,0:T(8,128)(2,1)S(1)}, bf16[512,512]{1,0:T(8,128)(2,1)S(1)}, u32[]{:S(2)}, u32[]{:S(2)}) collective-permute-start(bf16[512,512]{1,0:T(8,128)(2,1)S(1)} %shard_map.70.refs_2_), channel_id=1, source_target_pairs={{0,1},{1,0},{2,3},{3,2},{4,5},{5,4},{6,7},{7,6},{8,9},{9,8},{10,11... | collective-permute-start | bytes 1572872 | tf_op jit(solution)/shard_map/ppermute | solution.py:19
  18.2 11.4 %collective-permute-start.10 = (bf16[256,512]{1,0:T(8,128)(2,1)S(1)}, bf16[256,512]{1,0:T(8,128)(2,1)S(1)}, u32[]{:S(2)}, u32[]{:S(2)}) collective-permute-start(bf16[256,512]{1,0:T(8,128)(2,1)S(1)} %collective-permute-done.7.refs_1_), channel_id=1, source_target_pairs={{0,8},{4,12},{8,0},{12,4},{16,24},{20,28},{24,16},{28,20},{1,9},{5... | collective-permute-start | bytes 786440 | tf_op jit(solution)/shard_map/ppermute | solution.py:19
  18.9 10.8 %collective-permute-start.9 = (bf16[256,512]{1,0:T(8,128)(2,1)S(1)}, bf16[256,512]{1,0:T(8,128)(2,1)S(1)}, u32[]{:S(2)}, u32[]{:S(2)}) collective-permute-start(bf16[256,512]{1,0:T(8,128)(2,1)S(1)} %collective-permute-done.6.refs_0_), channel_id=1, source_target_pairs={{0,16},{4,20},{8,24},{12,28},{16,0},{20,4},{24,8},{28,12},{1,17},{... | collective-permute-start | bytes 786440 | tf_op jit(solution)/shard_map/ppermute | solution.py:19
  24.0 3.1 %copy-start = (s32[1024,1]{0,1:T(1,128)S(1)}, s32[1024,1]{0,1:T(1,128)}, u32[]{:S(2)}) copy-start(s32[1024,1]{0,1:T(1,128)} %param.7) | copy-start | bytes 12292
  25.5 9.4 %collective-permute-start.12 = (bf16[256,512]{1,0:T(8,128)(2,1)S(1)}, bf16[256,512]{1,0:T(8,128)(2,1)S(1)}, u32[]{:S(2)}, u32[]{:S(2)}) collective-permute-start(bf16[256,512]{1,0:T(8,128)(2,1)S(1)} %get-tuple-element.62), channel_id=1, source_target_pairs={{0,8},{4,12},{8,0},{12,4},{16,24},{20,28},{24,16},{28,20},{1,9},{5... | collective-permute-start | bytes 786440 | tf_op jit(solution)/shard_map/ppermute | solution.py:19
  27.5 13.2 %collective-permute-start.4 = (bf16[256,512]{1,0:T(8,128)(2,1)S(1)}, bf16[256,512]{1,0:T(8,128)(2,1)S(1)}, u32[]{:S(2)}, u32[]{:S(2)}) collective-permute-start(bf16[256,512]{1,0:T(8,128)(2,1)S(1)} %get-tuple-element.48), channel_id=1, source_target_pairs={{0,16},{4,20},{8,24},{12,28},{16,0},{20,4},{24,8},{28,12},{1,17},{... | collective-permute-start | bytes 786440 | tf_op jit(solution)/shard_map/ppermute | solution.py:19
  28.1 12.6 %collective-permute-start.5 = (bf16[256,512]{1,0:T(8,128)(2,1)S(1)}, bf16[256,512]{1,0:T(8,128)(2,1)S(1)}, u32[]{:S(2)}, u32[]{:S(2)}) collective-permute-start(bf16[256,512]{1,0:T(8,128)(2,1)S(1)} %get-tuple-element.49), channel_id=1, source_target_pairs={{0,24},{4,28},{8,16},{12,20},{16,8},{20,12},{24,0},{28,4},{1,25},{... | collective-permute-start | bytes 786440 | tf_op jit(solution)/shard_map/ppermute | solution.py:19
  29.8 5.2 %collective-permute-start.11 = (bf16[2048,512]{1,0:T(8,128)(2,1)S(1)}, bf16[2048,512]{1,0:T(8,128)(2,1)S(1)}, u32[]{:S(2)}, u32[]{:S(2)}) collective-permute-start(bf16[2048,512]{1,0:T(8,128)(2,1)S(1)} %shard_map.71.rest_2_), channel_id=1, source_target_pairs={{0,4},{4,0},{8,12},{12,8},{16,20},{20,16},{24,28},{28,24},{1,5},{5... | collective-permute-start | bytes 6291464 | tf_op jit(solution)/shard_map/ppermute | solution.py:19

commit v10 on v9

--- a/solution.py
+++ b/solution.py
@@ -261,7 +261,7 @@
         x_mine, y_other, _ = together(*near, sent[0])
         (pack_near,) = call(packed, [array(2 * depth, features)], 1, [VMEM] * 2, x_mine, y_other)
         pack_far = swapped(pack_near, 1, "blk")
-        d_mine, d_other = swapped(after(x_mine, x[1]), 4), swapped(after(y_other, x[1]), 2)
+        d_mine, d_other = swapped(after(x_mine, x[1]), 4), swapped(after(y_other, terms[0]), 2)
     done = call(third_level, [part] * 4, (1 << 34), [VMEM] * 8, x[2], x[3], *terms, *weights)
     back = [done[0]] + [swapped(done[m], 2 * m) for m in (1, 2, 3)]
     if not few:

time: 44 us -> 44 us (level)
  no operation moved by 1% of the time
where the time goes in v10:
time: 44 us; the launch traced here: 43.8 us
  starting transfers between devices  15.8 us (36%)
  Pallas kernels  15.5 us (35%)
  waiting for transfers between devices  12.4 us (28%)
    ppermute x13, starting transfers between devices, swapped(): return lax.ppermute(value, axis, pairs)  15.8 us
    pallas_call x11, Pallas kernels, call(): pl.pallas_call(body, out_shape=[shape for shape, _ in outs], in_specs=spe...  15.5 us
    ppermute x13, waiting for transfers between devices, swapped(): return lax.ppermute(value, axis, pairs)  12.4 us
  transfers between devices with their start and end apart: 13, of which 6 were waited for; matrix products, arithmetic and copies ran while one was open for 0% of the time, Pallas kernels for 28%

profile of v10, /device:TPU:0, one launch (start us, length us, event | category | flops | bytes accessed | tf_op | source)
XLA Modules:
  0.0 43.8 jit_solution(5848701263212060566)
XLA Ops:
  0.0 0.5 %collective-permute-start = (bf16[1024,512]{1,0:T(8,128)(2,1)}, bf16[1024,512]{1,0:T(8,128)(2,1)S(1)}, u32[]{:S(2)}, u32[]{:S(2)}) collective-permute-start(bf16[1024,512]{1,0:T(8,128)(2,1)} %interface.1), channel_id=1, source_target_pairs={{0,4},{4,0},{8,12},{12,8},{16,20},{20,16},{24,28},{28,24},{1,5},{5... | collective-permute-start | bytes 3145736 | tf_op jit(solution)/shard_map/ppermute | solution.py:19
  0.5 1.1 %shard_map.69 = (bf16[256,512]{1,0:T(8,128)(2,1)S(1)}, bf16[256,512]{1,0:T(8,128)(2,1)S(1)}) custom-call(s32[1]{0:T(128)} %bitcast.1.z, bf16[1,512,512]{2,1,0:T(8,128)(2,1)} %coupling.1, s32[1,8,8]{2,1,0:T(8,128)} %pattern.1), custom_call_target="tpu_custom_call" | custom-call | flops 1 | tf_op jit(solution)/shard_map/pallas_call | solution.py:45
  1.6 2.6 %collective-permute-start.6 = (bf16[256,512]{1,0:T(8,128)(2,1)S(1)}, bf16[256,512]{1,0:T(8,128)(2,1)S(1)}, u32[]{:S(2)}, u32[]{:S(2)}) collective-permute-start(bf16[256,512]{1,0:T(8,128)(2,1)S(1)} %get-tuple-element.56.refs_0_), channel_id=1, source_target_pairs={{0,8},{4,12},{8,0},{12,4},{16,24},{20,28},{24,16},{28,20},{1,9},{5... | collective-permute-start | bytes 786440 | tf_op jit(solution)/shard_map/ppermute | solution.py:19
  4.2 1.5 %collective-permute-start.7 = (bf16[256,512]{1,0:T(8,128)(2,1)S(1)}, bf16[256,512]{1,0:T(8,128)(2,1)S(1)}, u32[]{:S(2)}, u32[]{:S(2)}) collective-permute-start(bf16[256,512]{1,0:T(8,128)(2,1)S(1)} %get-tuple-element.57.refs_1_), channel_id=1, source_target_pairs={{0,16},{4,20},{8,24},{12,28},{16,0},{20,4},{24,8},{28,12},{1,17},{... | collective-permute-start | bytes 786440 | tf_op jit(solution)/shard_map/ppermute | solution.py:19
  5.7 3.3 %shard_map.64 = (bf16[256,512]{1,0:T(8,128)(2,1)S(1)}, bf16[256,512]{1,0:T(8,128)(2,1)S(1)}, bf16[256,512]{1,0:T(8,128)(2,1)S(1)}, bf16[256,512]{1,0:T(8,128)(2,1)S(1)}) custom-call(s32[1]{0:T(128)} %bitcast.me, bf16[1024,512]{1,0:T(8,128)(2,1)S(1)} %collective-permute-done.sibling, bf16[1024,512]{1,0:T(8,128)(2,1)} %interface.1, bf16[3,512,512]{2,1,0:T(8,128)(2,1)} %keep.2, ...), custom_call_target="tpu_custom_call" | custom-call | flops 536870912 | bytes 1048576 | tf_op jit(solution)/shard_map/pallas_call | solution.py:45
  8.9 0.6 %collective-permute-start.3 = (bf16[256,512]{1,0:T(8,128)(2,1)S(1)}, bf16[256,512]{1,0:T(8,128)(2,1)S(1)}, u32[]{:S(2)}, u32[]{:S(2)}) collective-permute-start(bf16[256,512]{1,0:T(8,128)(2,1)S(1)} %get-tuple-element.37), channel_id=1, source_target_pairs={{0,8},{4,12},{8,0},{12,4},{16,24},{20,28},{24,16},{28,20},{1,9},{5... | collective-permute-start | bytes 786440 | tf_op jit(solution)/shard_map/ppermute | solution.py:19
  9.5 1.1 %collective-permute-start.1 = (bf16[256,512]{1,0:T(8,128)(2,1)S(1)}, bf16[256,512]{1,0:T(8,128)(2,1)S(1)}, u32[]{:S(2)}, u32[]{:S(2)}) collective-permute-start(bf16[256,512]{1,0:T(8,128)(2,1)S(1)} %get-tuple-element.34), channel_id=1, source_target_pairs={{0,16},{4,20},{8,24},{12,28},{16,0},{20,4},{24,8},{28,12},{1,17},{... | collective-permute-start | bytes 786440 | tf_op jit(solution)/shard_map/ppermute | solution.py:19
  10.7 1.8 %collective-permute-start.2 = (bf16[256,512]{1,0:T(8,128)(2,1)S(1)}, bf16[256,512]{1,0:T(8,128)(2,1)S(1)}, u32[]{:S(2)}, u32[]{:S(2)}) collective-permute-start(bf16[256,512]{1,0:T(8,128)(2,1)S(1)} %get-tuple-element.35), channel_id=1, source_target_pairs={{0,24},{4,28},{8,16},{12,20},{16,8},{20,12},{24,0},{28,4},{1,25},{... | collective-permute-start | bytes 786440 | tf_op jit(solution)/shard_map/ppermute | solution.py:19
  12.5 0.8 %collective-permute-done.7.refs_1_ = bf16[256,512]{1,0:T(8,128)(2,1)S(1)} collective-permute-done((bf16[256,512]{1,0:T(8,128)(2,1)S(1)}, bf16[256,512]{1,0:T(8,128)(2,1)S(1)}, u32[]{:S(2)}, u32[]{:S(2)}) %collective-permute-start.7) | collective-permute-done | bytes 262176 | tf_op jit(solution)/shard_map/ppermute | solution.py:19
  13.3 1.6 %collective-permute-start.8 = (bf16[512,512]{1,0:T(8,128)(2,1)S(1)}, bf16[512,512]{1,0:T(8,128)(2,1)S(1)}, u32[]{:S(2)}, u32[]{:S(2)}) collective-permute-start(bf16[512,512]{1,0:T(8,128)(2,1)S(1)} %shard_map.70.refs_2_), channel_id=1, source_target_pairs={{0,1},{1,0},{2,3},{3,2},{4,5},{5,4},{6,7},{7,6},{8,9},{9,8},{10,11... | collective-permute-start | bytes 1572872 | tf_op jit(solution)/shard_map/ppermute | solution.py:19
  15.0 1.6 %shard_map.65 = (bf16[2,512,512]{2,1,0:T(8,128)(2,1)S(1)}, bf16[2,512,512]{2,1,0:T(8,128)(2,1)S(1)}) custom-call(bf16[3,512,512]{2,1,0:T(8,128)(2,1)} %keep.2, bf16[3,512,512]{2,1,0:T(8,128)(2,1)} %cross.2), custom_call_target="tpu_custom_call" | custom-call | flops 1 | tf_op jit(solution)/shard_map/pallas_call | solution.py:45
  16.5 1.6 %collective-permute-done.3.x1 = bf16[256,512]{1,0:T(8,128)(2,1)S(1)} collective-permute-done((bf16[256,512]{1,0:T(8,128)(2,1)S(1)}, bf16[256,512]{1,0:T(8,128)(2,1)S(1)}, u32[]{:S(2)}, u32[]{:S(2)}) %collective-permute-start.3) | collective-permute-done | bytes 262176 | tf_op jit(solution)/shard_map/ppermute | solution.py:19
  18.2 1.2 %shard_map.66 = (f32[256,512]{1,0:T(8,128)S(1)}, f32[256,512]{1,0:T(8,128)S(1)}, f32[256,512]{1,0:T(8,128)S(1)}, f32[256,512]{1,0:T(8,128)S(1)}) custom-call(bf16[256,512]{1,0:T(8,128)(2,1)S(1)} %get-tuple-element.36.x0, bf16[256,512]{1,0:T(8,128)(2,1)S(1)} %collective-permute-done.3.x1, bf16[2,512,512]{2,1,0:T(8,128)(2,1)S(1)} %get-tuple-element.40.keep, ...), custom_call_target="tpu_custom_call" | custom-call | flops 1 | tf_op jit(solution)/shard_map/pallas_call | solution.py:45
  19.4 0.8 %collective-permute-start.10 = (bf16[256,512]{1,0:T(8,128)(2,1)S(1)}, bf16[256,512]{1,0:T(8,128)(2,1)S(1)}, u32[]{:S(2)}, u32[]{:S(2)}) collective-permute-start(bf16[256,512]{1,0:T(8,128)(2,1)S(1)} %collective-permute-done.7.refs_1_), channel_id=1, source_target_pairs={{0,8},{4,12},{8,0},{12,4},{16,24},{20,28},{24,16},{28,20},{1,9},{5... | collective-permute-start | bytes 786440 | tf_op jit(solution)/shard_map/ppermute | solution.py:19
  20.2 1.5 %collective-permute-start.9 = (bf16[256,512]{1,0:T(8,128)(2,1)S(1)}, bf16[256,512]{1,0:T(8,128)(2,1)S(1)}, u32[]{:S(2)}, u32[]{:S(2)}) collective-permute-start(bf16[256,512]{1,0:T(8,128)(2,1)S(1)} %collective-permute-done.6.refs_0_), channel_id=1, source_target_pairs={{0,16},{4,20},{8,24},{12,28},{16,0},{20,4},{24,8},{28,12},{1,17},{... | collective-permute-start | bytes 786440 | tf_op jit(solution)/shard_map/ppermute | solution.py:19
  21.7 2.1 %collective-permute-done.1.x2 = bf16[256,512]{1,0:T(8,128)(2,1)S(1)} collective-permute-done((bf16[256,512]{1,0:T(8,128)(2,1)S(1)}, bf16[256,512]{1,0:T(8,128)(2,1)S(1)}, u32[]{:S(2)}, u32[]{:S(2)}) %collective-permute-start.1) | collective-permute-done | bytes 262176 | tf_op jit(solution)/shard_map/ppermute | solution.py:19
  24.0 1.5 %shard_map.67 = (bf16[256,512]{1,0:T(8,128)(2,1)S(1)}, bf16[256,512]{1,0:T(8,128)(2,1)S(1)}, bf16[256,512]{1,0:T(8,128)(2,1)S(1)}, bf16[256,512]{1,0:T(8,128)(2,1)S(1)}) custom-call(bf16[256,512]{1,0:T(8,128)(2,1)S(1)} %collective-permute-done.1.x2, bf16[256,512]{1,0:T(8,128)(2,1)S(1)} %collective-permute-done.2.x3, f32[256,512]{1,0:T(8,128)S(1)} %get-tuple-element.42.term0, ...), custom_call_target="tpu_custom_call" | custom-call | flops 17179869184 | bytes 33554432 | tf_op jit(solution)/shard_map/pallas_call | solution.py:45
  25.5 1.6 %collective-permute-start.12 = (bf16[256,512]{1,0:T(8,128)(2,1)S(1)}, bf16[256,512]{1,0:T(8,128)(2,1)S(1)}, u32[]{:S(2)}, u32[]{:S(2)}) collective-permute-start(bf16[256,512]{1,0:T(8,128)(2,1)S(1)} %get-tuple-element.62), channel_id=1, source_target_pairs={{0,8},{4,12},{8,0},{12,4},{16,24},{20,28},{24,16},{28,20},{1,9},{5... | collective-permute-start | bytes 786440 | tf_op jit(solution)/shard_map/ppermute | solution.py:19
  27.5 0.7 %collective-permute-start.4 = (bf16[256,512]{1,0:T(8,128)(2,1)S(1)}, bf16[256,512]{1,0:T(8,128)(2,1)S(1)}, u32[]{:S(2)}, u32[]{:S(2)}) collective-permute-start(bf16[256,512]{1,0:T(8,128)(2,1)S(1)} %get-tuple-element.48), channel_id=1, source_target_pairs={{0,16},{4,20},{8,24},{12,28},{16,0},{20,4},{24,8},{28,12},{1,17},{... | collective-permute-start | bytes 786440 | tf_op jit(solution)/shard_map/ppermute | solution.py:19
  28.1 1.5 %collective-permute-start.5 = (bf16[256,512]{1,0:T(8,128)(2,1)S(1)}, bf16[256,512]{1,0:T(8,128)(2,1)S(1)}, u32[]{:S(2)}, u32[]{:S(2)}) collective-permute-start(bf16[256,512]{1,0:T(8,128)(2,1)S(1)} %get-tuple-element.49), channel_id=1, source_target_pairs={{0,24},{4,28},{8,16},{12,20},{16,8},{20,12},{24,0},{28,4},{1,25},{... | collective-permute-start | bytes 786440 | tf_op jit(solution)/shard_map/ppermute | solution.py:19
  29.9 5.0 %collective-permute-done.12.refs_0_ = bf16[256,512]{1,0:T(8,128)(2,1)S(1)} collective-permute-done((bf16[256,512]{1,0:T(8,128)(2,1)S(1)}, bf16[256,512]{1,0:T(8,128)(2,1)S(1)}, u32[]{:S(2)}, u32[]{:S(2)}) %collective-permute-start.12) | collective-permute-done | bytes 262176 | tf_op jit(solution)/shard_map/ppermute | solution.py:19
  34.9 3.1 %shard_map.73.rest_4_ = bf16[1024,512]{1,0:T(8,128)(2,1)} custom-call(s32[1]{0:T(128)} %bitcast.me, s32[1]{0:T(128)} %bitcast.1.z, s32[1024,128]{1,0:T(8,128)S(1)} %shard_map.68.owners, bf16[256,512]{1,0:T(8,128)(2,1)S(1)} %get-tuple-element.46.rest_0_, bf16[256,512]{1,0:T(8,128)(2,1)S(1)} %shard_map.72.rest_1_, bf16[2048,512]{1,0:T(8,128)(2,1)S(1)} %shard_map.71.rest_2_, ...), custom_call_target="tpu_custom_call" | custom-call | flops 2147483648 | bytes 4194304 | tf_op jit(solution)/shard_map/pallas_call | solution.py:45
  38.1 2.6 %collective-permute-done.4.rest_0_ = bf16[256,512]{1,0:T(8,128)(2,1)S(1)} collective-permute-done((bf16[256,512]{1,0:T(8,128)(2,1)S(1)}, bf16[256,512]{1,0:T(8,128)(2,1)S(1)}, u32[]{:S(2)}, u32[]{:S(2)}) %collective-permute-start.4) | collective-permute-done | bytes 262176 | tf_op jit(solution)/shard_map/ppermute | solution.py:19
  40.7 3.1 %shard_map.74 = bf16[1024,512]{1,0:T(8,128)(2,1)} custom-call(s32[1]{0:T(128)} %bitcast.me, s32[1]{0:T(128)} %bitcast.1.z, s32[1024,128]{1,0:T(8,128)S(1)} %shard_map.68.owners, bf16[256,512]{1,0:T(8,128)(2,1)S(1)} %collective-permute-done.4.rest_0_, bf16[256,512]{1,0:T(8,128)(2,1)S(1)} %collective-permute-done.5.rest_1_, ...), custom_call_target="tpu_custom_call", output_to_operand_aliasing={{}: (7, {})} | custom-call | flops 2147483648 | bytes 4194304 | tf_op jit(solution)/shard_map/pallas_call | solution.py:45
  (15 shorter events, 0.8 us)
Async XLA Ops:
  0.0 5.7 %collective-permute-start = (bf16[1024,512]{1,0:T(8,128)(2,1)}, bf16[1024,512]{1,0:T(8,128)(2,1)S(1)}, u32[]{:S(2)}, u32[]{:S(2)}) collective-permute-start(bf16[1024,512]{1,0:T(8,128)(2,1)} %interface.1), channel_id=1, source_target_pairs={{0,4},{4,0},{8,12},{12,8},{16,20},{20,16},{24,28},{28,24},{1,5},{5... | collective-permute-start | bytes 3145736 | tf_op jit(solution)/shard_map/ppermute | solution.py:19
  1.6 10.9 %collective-permute-start.6 = (bf16[256,512]{1,0:T(8,128)(2,1)S(1)}, bf16[256,512]{1,0:T(8,128)(2,1)S(1)}, u32[]{:S(2)}, u32[]{:S(2)}) collective-permute-start(bf16[256,512]{1,0:T(8,128)(2,1)S(1)} %get-tuple-element.56.refs_0_), channel_id=1, source_target_pairs={{0,8},{4,12},{8,0},{12,4},{16,24},{20,28},{24,16},{28,20},{1,9},{5... | collective-permute-start | bytes 786440 | tf_op jit(solution)/shard_map/ppermute | solution.py:19
  4.2 9.1 %collective-permute-start.7 = (bf16[256,512]{1,0:T(8,128)(2,1)S(1)}, bf16[256,512]{1,0:T(8,128)(2,1)S(1)}, u32[]{:S(2)}, u32[]{:S(2)}) collective-permute-start(bf16[256,512]{1,0:T(8,128)(2,1)S(1)} %get-tuple-element.57.refs_1_), channel_id=1, source_target_pairs={{0,16},{4,20},{8,24},{12,28},{16,0},{20,4},{24,8},{28,12},{1,17},{... | collective-permute-start | bytes 786440 | tf_op jit(solution)/shard_map/ppermute | solution.py:19
  8.9 9.2 %collective-permute-start.3 = (bf16[256,512]{1,0:T(8,128)(2,1)S(1)}, bf16[256,512]{1,0:T(8,128)(2,1)S(1)}, u32[]{:S(2)}, u32[]{:S(2)}) collective-permute-start(bf16[256,512]{1,0:T(8,128)(2,1)S(1)} %get-tuple-element.37), channel_id=1, source_target_pairs={{0,8},{4,12},{8,0},{12,4},{16,24},{20,28},{24,16},{28,20},{1,9},{5... | collective-permute-start | bytes 786440 | tf_op jit(solution)/shard_map/ppermute | solution.py:19
  9.5 14.3 %collective-permute-start.1 = (bf16[256,512]{1,0:T(8,128)(2,1)S(1)}, bf16[256,512]{1,0:T(8,128)(2,1)S(1)}, u32[]{:S(2)}, u32[]{:S(2)}) collective-permute-start(bf16[256,512]{1,0:T(8,128)(2,1)S(1)} %get-tuple-element.34), channel_id=1, source_target_pairs={{0,16},{4,20},{8,24},{12,28},{16,0},{20,4},{24,8},{28,12},{1,17},{... | collective-permute-start | bytes 786440 | tf_op jit(solution)/shard_map/ppermute | solution.py:19
  10.7 13.4 %collective-permute-start.2 = (bf16[256,512]{1,0:T(8,128)(2,1)S(1)}, bf16[256,512]{1,0:T(8,128)(2,1)S(1)}, u32[]{:S(2)}, u32[]{:S(2)}) collective-permute-start(bf16[256,512]{1,0:T(8,128)(2,1)S(1)} %get-tuple-element.35), channel_id=1, source_target_pairs={{0,24},{4,28},{8,16},{12,20},{16,8},{20,12},{24,0},{28,4},{1,25},{... | collective-permute-start | bytes 786440 | tf_op jit(solution)/shard_map/ppermute | solution.py:19
  13.3 14.8 %collective-permute-start.8 = (bf16[512,512]{1,0:T(8,128)(2,1)S(1)}, bf16[512,512]{1,0:T(8,128)(2,1)S(1)}, u32[]{:S(2)}, u32[]{:S(2)}) collective-permute-start(bf16[512,512]{1,0:T(8,128)(2,1)S(1)} %shard_map.70.refs_2_), channel_id=1, source_target_pairs={{0,1},{1,0},{2,3},{3,2},{4,5},{5,4},{6,7},{7,6},{8,9},{9,8},{10,11... | collective-permute-start | bytes 1572872 | tf_op jit(solution)/shard_map/ppermute | solution.py:19
  19.4 10.2 %collective-permute-start.10 = (bf16[256,512]{1,0:T(8,128)(2,1)S(1)}, bf16[256,512]{1,0:T(8,128)(2,1)S(1)}, u32[]{:S(2)}, u32[]{:S(2)}) collective-permute-start(bf16[256,512]{1,0:T(8,128)(2,1)S(1)} %collective-permute-done.7.refs_1_), channel_id=1, source_target_pairs={{0,8},{4,12},{8,0},{12,4},{16,24},{20,28},{24,16},{28,20},{1,9},{5... | collective-permute-start | bytes 786440 | tf_op jit(solution)/shard_map/ppermute | solution.py:19
  20.2 9.4 %collective-permute-start.9 = (bf16[256,512]{1,0:T(8,128)(2,1)S(1)}, bf16[256,512]{1,0:T(8,128)(2,1)S(1)}, u32[]{:S(2)}, u32[]{:S(2)}) collective-permute-start(bf16[256,512]{1,0:T(8,128)(2,1)S(1)} %collective-permute-done.6.refs_0_), channel_id=1, source_target_pairs={{0,16},{4,20},{8,24},{12,28},{16,0},{20,4},{24,8},{28,12},{1,17},{... | collective-permute-start | bytes 786440 | tf_op jit(solution)/shard_map/ppermute | solution.py:19
  24.0 3.1 %copy-start = (s32[1024,1]{0,1:T(1,128)S(1)}, s32[1024,1]{0,1:T(1,128)}, u32[]{:S(2)}) copy-start(s32[1024,1]{0,1:T(1,128)} %param.7) | copy-start | bytes 12292
  25.5 9.4 %collective-permute-start.12 = (bf16[256,512]{1,0:T(8,128)(2,1)S(1)}, bf16[256,512]{1,0:T(8,128)(2,1)S(1)}, u32[]{:S(2)}, u32[]{:S(2)}) collective-permute-start(bf16[256,512]{1,0:T(8,128)(2,1)S(1)} %get-tuple-element.62), channel_id=1, source_target_pairs={{0,8},{4,12},{8,0},{12,4},{16,24},{20,28},{24,16},{28,20},{1,9},{5... | collective-permute-start | bytes 786440 | tf_op jit(solution)/shard_map/ppermute | solution.py:19
  27.5 13.2 %collective-permute-start.4 = (bf16[256,512]{1,0:T(8,128)(2,1)S(1)}, bf16[256,512]{1,0:T(8,128)(2,1)S(1)}, u32[]{:S(2)}, u32[]{:S(2)}) collective-permute-start(bf16[256,512]{1,0:T(8,128)(2,1)S(1)} %get-tuple-element.48), channel_id=1, source_target_pairs={{0,16},{4,20},{8,24},{12,28},{16,0},{20,4},{24,8},{28,12},{1,17},{... | collective-permute-start | bytes 786440 | tf_op jit(solution)/shard_map/ppermute | solution.py:19
  28.1 12.6 %collective-permute-start.5 = (bf16[256,512]{1,0:T(8,128)(2,1)S(1)}, bf16[256,512]{1,0:T(8,128)(2,1)S(1)}, u32[]{:S(2)}, u32[]{:S(2)}) collective-permute-start(bf16[256,512]{1,0:T(8,128)(2,1)S(1)} %get-tuple-element.49), channel_id=1, source_target_pairs={{0,24},{4,28},{8,16},{12,20},{16,8},{20,12},{24,0},{28,4},{1,25},{... | collective-permute-start | bytes 786440 | tf_op jit(solution)/shard_map/ppermute | solution.py:19
  29.8 5.2 %collective-permute-start.11 = (bf16[2048,512]{1,0:T(8,128)(2,1)S(1)}, bf16[2048,512]{1,0:T(8,128)(2,1)S(1)}, u32[]{:S(2)}, u32[]{:S(2)}) collective-permute-start(bf16[2048,512]{1,0:T(8,128)(2,1)S(1)} %shard_map.71.rest_2_), channel_id=1, source_target_pairs={{0,4},{4,0},{8,12},{12,8},{16,20},{20,16},{24,28},{28,24},{1,5},{5... | collective-permute-start | bytes 6291464 | tf_op jit(solution)/shard_map/ppermute | solution.py:19
